TPU v7x, 32 devices: a whole 2x2x4 slice. The times are simulated.
32 devices in a mesh: ctx: 8 (over y, x, core), tp: 4 (over z).
Axes of the slice: x: 2, y: 2, z: 4, core: 2. Of those that a mesh axis runs over, the one named last changes fastest.
Arguments:
- main_q: bfloat16 [3584, 24576], P('ctx', 'tp'), may hold values from -6 to 6
- main_k: bfloat16 [1024, 24576], P('ctx', 'tp'), may hold values from -6 to 6
- log_norms: float32 [3584, 128], P('ctx', 'tp'), may hold values from 0 to 4
- index_q: bfloat16 [3584, 64, 128], P(('ctx', 'tp')), may hold values from -8 to 8
- index_w: float32 [3584, 64], P(('ctx', 'tp')), may hold values from -2 to 2
- index_k: bfloat16 [1024, 128], P('ctx'), may hold values from -8 to 8
- row_weight: float32 [3584], P(('ctx', 'tp')), may hold values from 10 to 200
- offsets: int32 [8], P('ctx'), may hold values from 0 to 576
- key_map: int32 [8], replicated, may hold values from 0 to 7, as said below
Outputs:
- grad_index_q: float32 [3584, 64, 128], P(('ctx', 'tp'))
- grad_index_w: float32 [3584, 64], P(('ctx', 'tp'))
- grad_index_k: float32 [1024, 128], P(('ctx', 'tp'))
Inputs may be any that keep to these rules, and one draw needn't show every extreme that they name: `key_map`: each key block number appears exactly once.
All inputs are finite; a program needn't handle non-finite values.
Results may differ from a plain program's by a relative error of at most 0.0028.
Values may be sent and summed in bfloat16 or wider, within the bound.
No kernel may reach another device: no remote copies, remote signals or barrier semaphores. Data moves between devices by JAX's collectives and lax.ppermute only.
A program may use at most 128 MiB of HBM per device.

v0:
```python
import math

import jax
import jax.numpy as jnp
from jax import lax
from jax.sharding import PartitionSpec as P


def key_places(key_map, key_total, key_rows):
    storage = jnp.arange(key_total, dtype=jnp.int32)
    owners = storage // key_rows
    block_ids = jnp.arange(key_map.shape[0], dtype=jnp.int32)
    picked = jnp.sum(jnp.where(owners[:, None] == block_ids[None, :], key_map[None, :], 0), axis=1)
    return picked * key_rows + storage % key_rows


def column_mass(queries, norm_rows, row_pos, keys, key_pos):
    amount = queries.shape[0]
    heads = norm_rows.shape[1]
    key_total = keys.shape[0]
    block_keys = math.gcd(key_total, 256)
    queries_wide = queries.reshape(amount, heads, -1)
    score_scale = 1.0 / math.sqrt(queries_wide.shape[2])

    def add_block(number, running):
        first_key = number * block_keys
        key_block = lax.dynamic_slice_in_dim(keys, first_key, block_keys, 0).reshape(
            block_keys, heads, -1
        )
        key_place = lax.dynamic_slice_in_dim(key_pos, first_key, block_keys, 0)
        scores = (
            jnp.einsum("qhd,khd->qhk", queries_wide, key_block, preferred_element_type=jnp.float32)
            * score_scale
        )
        visible = key_place[None, :] <= row_pos[:, None]
        prob_terms = jnp.where(visible[:, None, :], jnp.exp(scores - norm_rows[:, :, None]), 0.0)
        return lax.dynamic_update_slice_in_dim(running, jnp.sum(prob_terms, axis=1), first_key, 1)

    return lax.fori_loop(
        0, key_total // block_keys, add_block, jnp.zeros((amount, key_total), jnp.float32)
    )


def per_device(main_q, main_k, log_norms, index_q, index_w, index_k, row_weight, offsets, key_map):
    key_rows = main_k.shape[0]
    block_rows = main_q.shape[0]
    own_rows = index_q.shape[0]
    key_total = key_rows * lax.axis_size("ctx")
    key_pos = key_places(key_map, key_total, key_rows)
    first_pos = offsets[0]
    block_pos = first_pos + jnp.arange(block_rows, dtype=jnp.int32)
    partial_mass = column_mass(
        main_q, log_norms, block_pos, lax.all_gather(main_k, "ctx", axis=0, tiled=True), key_pos
    )
    index_keys = lax.all_gather(index_k, "ctx", axis=0, tiled=True)
    row_mass = lax.psum_scatter(partial_mass, "tp", scatter_dimension=0, tiled=True)
    target = row_mass / jnp.sum(row_mass, axis=1, keepdims=True)
    own_pos = first_pos + lax.axis_index("tp") * own_rows + jnp.arange(own_rows, dtype=jnp.int32)
    visible = key_pos[None, :] <= own_pos[:, None]
    inv_root = 1.0 / math.sqrt(index_q.shape[2])
    block_keys = math.gcd(key_total, 256)
    block_count = key_total // block_keys

    def raw_scores(number):
        key_block = lax.dynamic_slice_in_dim(index_keys, number * block_keys, block_keys, 0)
        inner = (
            jnp.einsum("tjd,kd->tjk", index_q, key_block, preferred_element_type=jnp.float32)
            * inv_root
        )
        return (key_block, inner)

    def first_pass(number, logits):
        key_block, inner = raw_scores(number)
        part_logits = jnp.sum(index_w[:, :, None] * jax.nn.softplus(inner), axis=1)
        return lax.dynamic_update_slice_in_dim(logits, part_logits, number * block_keys, 1)

    logits = lax.fori_loop(
        0, block_count, first_pass, jnp.zeros((own_rows, key_total), jnp.float32)
    )
    masked = jnp.where(visible, logits, -jnp.inf)
    row_max = jnp.max(masked, axis=1, keepdims=True)
    exp_terms = jnp.exp(masked - row_max)
    index_probs = exp_terms / jnp.sum(exp_terms, axis=1, keepdims=True)
    logit_grad = row_weight[:, None] * (index_probs - target)

    def second_pass(number, running):
        grad_w, grad_q, key_terms = running
        key_block, inner = raw_scores(number)
        first_key = number * block_keys
        grad_part = lax.dynamic_slice_in_dim(logit_grad, first_key, block_keys, 1)
        grad_w = grad_w + jnp.sum(grad_part[:, None, :] * jax.nn.softplus(inner), axis=2)
        score_grad = (
            grad_part[:, None, :] * index_w[:, :, None] * jax.nn.sigmoid(inner) * inv_root
        ).astype(jnp.bfloat16)
        grad_q = grad_q + jnp.einsum(
            "tjk,kd->tjd", score_grad, key_block, preferred_element_type=jnp.float32
        )
        key_part = jnp.einsum(
            "tjk,tjd->kd", score_grad, index_q, preferred_element_type=jnp.float32
        )
        key_terms = lax.dynamic_update_slice_in_dim(key_terms, key_part, first_key, 0)
        return (grad_w, grad_q, key_terms)

    start_state = (
        jnp.zeros(index_w.shape, jnp.float32),
        jnp.zeros(index_q.shape, jnp.float32),
        jnp.zeros((key_total, index_q.shape[2]), jnp.float32),
    )
    grad_w, grad_q, key_terms = lax.fori_loop(0, block_count, second_pass, start_state)
    ctx_sums = lax.psum_scatter(key_terms, "ctx", scatter_dimension=0, tiled=True)
    grad_k = lax.psum_scatter(ctx_sums, "tp", scatter_dimension=0, tiled=True)
    return (grad_q, grad_w, grad_k)


def solution(mesh):
    placed = (
        P("ctx", "tp"),
        P("ctx", "tp"),
        P("ctx", "tp"),
        P(("ctx", "tp"), None, None),
        P(("ctx", "tp"), None),
        P("ctx", None),
        P(("ctx", "tp")),
        P("ctx"),
        P(),
    )
    return jax.shard_map(
        per_device,
        mesh=mesh,
        in_specs=placed,
        out_specs=(P(("ctx", "tp"), None, None), P(("ctx", "tp"), None), P(("ctx", "tp"), None)),
        check_vma=False,
    )
```

profile of v0, /device:TPU:0, one launch (start us, length us, event | category | flops | bytes accessed | tf_op | source)
XLA Modules:
  0.0 309.1 jit_solution(10994413200080701011)
XLA Ops:
  10.5 8.3 %copy.26 = bf16[448,6144]{0,1:T(8,128)(2,1)} copy(bf16[448,6144]{1,0:T(8,128)(2,1)} %param.15) | data formatting | bytes 11010048 | tf_op args[0]
  18.9 68.8 %all-gather.2.cloned.1.call-done = bf16[1024,6144]{0,1:T(8,128)(2,1)} async-done(((bf16[128,6144]{0,1:T(8,128)(2,1)}), bf16[1024,6144]{0,1:T(8,128)(2,1)}) %all-gather.2.cloned.1.call-update) | async-done | bytes 12582928 | tf_op jit(solution)/shard_map/all_gather | solution.py:53
  88.0 40.6 %while.46 = (s32[]{:T(128)}, f32[448,1024]{1,0:T(8,128)S(1)}, s32[1024]{0:T(1024)S(1)}, bf16[1024,6144]{0,1:T(8,128)(2,1)}, bf16[448,32,192]{0,2,1:T(8,128)(2,1)...) while((s32[]{:T(128)}, f32[448,1024]{1,0:T(8,128)S(1)}, ...), condition=%wide.region_8.9_spmd.clone, body=%wide.region_6.8_spmd.clone.sunk | while | flops 1423966720 | bytes 38632132 | solution.py:39
  91.7 6.3 %fusion.72 = f32[448,256]{1,0:T(8,128)S(1)} fusion(bf16[256,32,192]{0,2,1:T(8,128)(2,1)S(1)} %bitcast.105, bf16[448,32,192]{0,2,1:T(8,128)(2,1)S(1)} %copy-done.2, f32[448,32]{0,1:T(8,128)S(1)} %get-tuple-element.649, pred[448,256]{1,0:T(8,128)(4,1)S(1)} %broadcast_compare_fusion.2), kind=kOutput, calls=%fused_computation.17.clone.1 | convolution fusion | flops 1423851520 | bytes 9281536 | tf_op jit(solution)/shard_map/while/body/eval_jaxpr/qhd,khd->qhk/dot_general | solution.py:32
  101.9 6.3 %fusion.72 = f32[448,256]{1,0:T(8,128)S(1)} fusion(bf16[256,32,192]{0,2,1:T(8,128)(2,1)S(1)} %bitcast.105, bf16[448,32,192]{0,2,1:T(8,128)(2,1)S(1)} %copy-done.2, f32[448,32]{0,1:T(8,128)S(1)} %get-tuple-element.649, pred[448,256]{1,0:T(8,128)(4,1)S(1)} %broadcast_compare_fusion.2), kind=kOutput, calls=%fused_computation.17.clone.1 | convolution fusion | flops 1423851520 | bytes 9281536 | tf_op jit(solution)/shard_map/while/body/eval_jaxpr/qhd,khd->qhk/dot_general | solution.py:32
  112.1 6.3 %fusion.72 = f32[448,256]{1,0:T(8,128)S(1)} fusion(bf16[256,32,192]{0,2,1:T(8,128)(2,1)S(1)} %bitcast.105, bf16[448,32,192]{0,2,1:T(8,128)(2,1)S(1)} %copy-done.2, f32[448,32]{0,1:T(8,128)S(1)} %get-tuple-element.649, pred[448,256]{1,0:T(8,128)(4,1)S(1)} %broadcast_compare_fusion.2), kind=kOutput, calls=%fused_computation.17.clone.1 | convolution fusion | flops 1423851520 | bytes 9281536 | tf_op jit(solution)/shard_map/while/body/eval_jaxpr/qhd,khd->qhk/dot_general | solution.py:32
  122.2 6.3 %fusion.72 = f32[448,256]{1,0:T(8,128)S(1)} fusion(bf16[256,32,192]{0,2,1:T(8,128)(2,1)S(1)} %bitcast.105, bf16[448,32,192]{0,2,1:T(8,128)(2,1)S(1)} %copy-done.2, f32[448,32]{0,1:T(8,128)S(1)} %get-tuple-element.649, pred[448,256]{1,0:T(8,128)(4,1)S(1)} %broadcast_compare_fusion.2), kind=kOutput, calls=%fused_computation.17.clone.1 | convolution fusion | flops 1423851520 | bytes 9281536 | tf_op jit(solution)/shard_map/while/body/eval_jaxpr/qhd,khd->qhk/dot_general | solution.py:32
  132.6 9.5 %all_gather.6 = bf16[1024,128]{1,0:T(8,128)(2,1)S(1)} all-gather(bf16[128,128]{1,0:T(8,128)(2,1)S(1)} %copy-done.6), channel_id=1, replica_groups=mesh['ctx'=8,'tp'=4] {'ctx'}, dimensions={0}, use_global_device_ids=true | all-gather | bytes 294912 | tf_op jit(solution)/shard_map/all_gather | solution.py:55
  142.2 26.4 %while.45 = (s32[]{:T(128)}, f32[112,1024]{1,0:T(8,128)S(1)}, f32[112,64]{0,1:T(8,128)S(1)}, bf16[1024,128]{1,0:T(8,128)(2,1)S(1)}, bf16[112,64,128]{2,0,1:T(8,1...) while((s32[]{:T(128)}, f32[112,1024]{1,0:T(8,128)S(1)}, f32[112,64]{0,1:T(8,128)S(1)}, ...), condition=%wide.region_3.4_spmd, body=%wide.region_1.3_spmd.sunk | while | flops 486248448 | bytes 2277523 | solution.py:77
  142.2 6.5 %fusion.69 = f32[112,256]{1,0:T(8,128)S(1)} fusion(f32[112,64]{0,1:T(8,128)S(1)} %get-tuple-element.675, bf16[112,64,128]{2,0,1:T(8,128)(2,1)S(1)} %get-tuple-element.677, bf16[1024,128]{1,0:T(8,128)(2,1)S(1)} %get-tuple-element.676, s32[]{:T(128)S(6)} %select_n.118), kind=kOutput, calls=%fused_computation.3.clone.1 | convolution fusion | flops 486248448 | bytes 2048004 | tf_op jit(solution)/shard_map/while/body/eval_jaxpr/tjd,kd->tjk/dot_general | solution.py:67
  148.8 6.5 %fusion.69 = f32[112,256]{1,0:T(8,128)S(1)} fusion(f32[112,64]{0,1:T(8,128)S(1)} %get-tuple-element.675, bf16[112,64,128]{2,0,1:T(8,128)(2,1)S(1)} %get-tuple-element.677, bf16[1024,128]{1,0:T(8,128)(2,1)S(1)} %get-tuple-element.676, s32[]{:T(128)S(6)} %select_n.118), kind=kOutput, calls=%fused_computation.3.clone.1 | convolution fusion | flops 486248448 | bytes 2048004 | tf_op jit(solution)/shard_map/while/body/eval_jaxpr/tjd,kd->tjk/dot_general | solution.py:67
  155.4 6.5 %fusion.69 = f32[112,256]{1,0:T(8,128)S(1)} fusion(f32[112,64]{0,1:T(8,128)S(1)} %get-tuple-element.675, bf16[112,64,128]{2,0,1:T(8,128)(2,1)S(1)} %get-tuple-element.677, bf16[1024,128]{1,0:T(8,128)(2,1)S(1)} %get-tuple-element.676, s32[]{:T(128)S(6)} %select_n.118), kind=kOutput, calls=%fused_computation.3.clone.1 | convolution fusion | flops 486248448 | bytes 2048004 | tf_op jit(solution)/shard_map/while/body/eval_jaxpr/tjd,kd->tjk/dot_general | solution.py:67
  162.0 6.5 %fusion.69 = f32[112,256]{1,0:T(8,128)S(1)} fusion(f32[112,64]{0,1:T(8,128)S(1)} %get-tuple-element.675, bf16[112,64,128]{2,0,1:T(8,128)(2,1)S(1)} %get-tuple-element.677, bf16[1024,128]{1,0:T(8,128)(2,1)S(1)} %get-tuple-element.676, s32[]{:T(128)S(6)} %select_n.118), kind=kOutput, calls=%fused_computation.3.clone.1 | convolution fusion | flops 486248448 | bytes 2048004 | tf_op jit(solution)/shard_map/while/body/eval_jaxpr/tjd,kd->tjk/dot_general | solution.py:67
  171.9 74.2 %while.47 = (s32[]{:T(128)}, f32[112,64]{0,1:T(8,128)}, f32[112,64,128]{2,1,0:T(8,128)}, f32[1024,128]{1,0:T(8,128)S(1)}, f32[112,1024]{1,0:T(8,128)S(1)}, /*ind...) while((s32[]{:T(128)}, f32[112,64]{0,1:T(8,128)}, ...), condition=%wide.region_13.14_spmd.clone, body=%wide.region_11.13_spmd.clone.sunk | while | flops 1440488448 | bytes 37679376 | solution.py:109
  171.9 10.2 %fusion.78 = (bf16[112,64,256]{2,0,1:T(8,128)(2,1)}, f32[112,64]{0,1:T(8,128)S(1)}) fusion(f32[112,64]{0,1:T(8,128)} %get-tuple-element.713, f32[112,256]{1,0:T(8,128)S(1)} %constant_dynamic-slice_fusion.5, bf16[112,64,128]{2,0,1:T(8,128)(2,1)S(1)} %get-tuple-element.712, bf16[1024,128]{1,0:T(8,128)(2,1)S(1)} %get-tuple-element.711, s32[]{:T(128)S(6)} %select_n.121), kind=kOutput, calls=%fused_computation.37.clone.1 | convolution fusion | flops 499115008 | bytes 5742596 | tf_op jit(solution)/shard_map/while/body/eval_jaxpr/tjd,kd->tjk/dot_general | solution.py:67
  182.2 5.7 %select_add_fusion.5 = f32[112,64,128]{2,1,0:T(8,128)} fusion(f32[112,64,128]{2,1,0:T(8,128)} %get-tuple-element.696, bf16[112,64,256]{2,0,1:T(8,128)(2,1)} %get-tuple-element.621, pred[]{:T(512)S(6)} %compare.9, bf16[1024,128]{1,0:T(8,128)(2,1)S(1)} %get-tuple-element.711, s32[]{:T(128)S(6)} %select_n.121), kind=kOutput, calls=%fused_computation.40.clone.1 | convolution fusion | flops 471597056 | bytes 11075589 | tf_op jit(solution)/shard_map/while/body/eval_jaxpr/tjk,kd->tjd/dot_general | solution.py:95
  189.7 10.2 %fusion.78 = (bf16[112,64,256]{2,0,1:T(8,128)(2,1)}, f32[112,64]{0,1:T(8,128)S(1)}) fusion(f32[112,64]{0,1:T(8,128)} %get-tuple-element.713, f32[112,256]{1,0:T(8,128)S(1)} %constant_dynamic-slice_fusion.5, bf16[112,64,128]{2,0,1:T(8,128)(2,1)S(1)} %get-tuple-element.712, bf16[1024,128]{1,0:T(8,128)(2,1)S(1)} %get-tuple-element.711, s32[]{:T(128)S(6)} %select_n.121), kind=kOutput, calls=%fused_computation.37.clone.1 | convolution fusion | flops 499115008 | bytes 5742596 | tf_op jit(solution)/shard_map/while/body/eval_jaxpr/tjd,kd->tjk/dot_general | solution.py:67
  199.9 6.7 %select_add_fusion.5 = f32[112,64,128]{2,1,0:T(8,128)} fusion(f32[112,64,128]{2,1,0:T(8,128)} %get-tuple-element.696, bf16[112,64,256]{2,0,1:T(8,128)(2,1)} %get-tuple-element.621, pred[]{:T(512)S(6)} %compare.9, bf16[1024,128]{1,0:T(8,128)(2,1)S(1)} %get-tuple-element.711, s32[]{:T(128)S(6)} %select_n.121), kind=kOutput, calls=%fused_computation.40.clone.1 | convolution fusion | flops 471597056 | bytes 11075589 | tf_op jit(solution)/shard_map/while/body/eval_jaxpr/tjk,kd->tjd/dot_general | solution.py:95
  208.5 10.2 %fusion.78 = (bf16[112,64,256]{2,0,1:T(8,128)(2,1)}, f32[112,64]{0,1:T(8,128)S(1)}) fusion(f32[112,64]{0,1:T(8,128)} %get-tuple-element.713, f32[112,256]{1,0:T(8,128)S(1)} %constant_dynamic-slice_fusion.5, bf16[112,64,128]{2,0,1:T(8,128)(2,1)S(1)} %get-tuple-element.712, bf16[1024,128]{1,0:T(8,128)(2,1)S(1)} %get-tuple-element.711, s32[]{:T(128)S(6)} %select_n.121), kind=kOutput, calls=%fused_computation.37.clone.1 | convolution fusion | flops 499115008 | bytes 5742596 | tf_op jit(solution)/shard_map/while/body/eval_jaxpr/tjd,kd->tjk/dot_general | solution.py:67
  218.7 6.7 %select_add_fusion.5 = f32[112,64,128]{2,1,0:T(8,128)} fusion(f32[112,64,128]{2,1,0:T(8,128)} %get-tuple-element.696, bf16[112,64,256]{2,0,1:T(8,128)(2,1)} %get-tuple-element.621, pred[]{:T(512)S(6)} %compare.9, bf16[1024,128]{1,0:T(8,128)(2,1)S(1)} %get-tuple-element.711, s32[]{:T(128)S(6)} %select_n.121), kind=kOutput, calls=%fused_computation.40.clone.1 | convolution fusion | flops 471597056 | bytes 11075589 | tf_op jit(solution)/shard_map/while/body/eval_jaxpr/tjk,kd->tjd/dot_general | solution.py:95
  227.3 10.2 %fusion.78 = (bf16[112,64,256]{2,0,1:T(8,128)(2,1)}, f32[112,64]{0,1:T(8,128)S(1)}) fusion(f32[112,64]{0,1:T(8,128)} %get-tuple-element.713, f32[112,256]{1,0:T(8,128)S(1)} %constant_dynamic-slice_fusion.5, bf16[112,64,128]{2,0,1:T(8,128)(2,1)S(1)} %get-tuple-element.712, bf16[1024,128]{1,0:T(8,128)(2,1)S(1)} %get-tuple-element.711, s32[]{:T(128)S(6)} %select_n.121), kind=kOutput, calls=%fused_computation.37.clone.1 | convolution fusion | flops 499115008 | bytes 5742596 | tf_op jit(solution)/shard_map/while/body/eval_jaxpr/tjd,kd->tjk/dot_general | solution.py:67
  237.5 6.7 %select_add_fusion.5 = f32[112,64,128]{2,1,0:T(8,128)} fusion(f32[112,64,128]{2,1,0:T(8,128)} %get-tuple-element.696, bf16[112,64,256]{2,0,1:T(8,128)(2,1)} %get-tuple-element.621, pred[]{:T(512)S(6)} %compare.9, bf16[1024,128]{1,0:T(8,128)(2,1)S(1)} %get-tuple-element.711, s32[]{:T(128)S(6)} %select_n.121), kind=kOutput, calls=%fused_computation.40.clone.1 | convolution fusion | flops 471597056 | bytes 11075589 | tf_op jit(solution)/shard_map/while/body/eval_jaxpr/tjk,kd->tjd/dot_general | solution.py:95
  247.0 33.8 %reduce-scatter.6.cloned.1.call-done = f32[128,128]{1,0:T(8,128)} async-done(((f32[1024,128]{1,0:T(8,128)}), f32[128,128]{1,0:T(8,128)}) %reduce-scatter.6.cloned.1.call-update) | async-done | bytes 65552 | tf_op jit(solution)/shard_map/reduce_scatter | solution.py:110
  280.8 21.8 %reduce-scatter.8.cloned.1.call-done = f32[32,128]{1,0:T(8,128)} async-done(((f32[128,128]{1,0:T(8,128)}), f32[32,128]{1,0:T(8,128)}) %reduce-scatter.8.cloned.1.call-update) | async-done | bytes 16400 | tf_op jit(solution)/shard_map/reduce_scatter | solution.py:111
  (106 shorter events, 33.6 us)
Async XLA Ops:
  7.2 80.6 %all-gather.2.cloned.1.call-start = ((), (), s32[]{:S(2)}) async-start(), calls=%async_computation.3 | async-start | bytes 14155776 | tf_op jit(solution)/shard_map/all_gather | solution.py:53
  9.8 9.0 %copy-start.8 = (s32[8]{0:T(128)S(1)}, s32[8]{0:T(128)}, u32[]{:S(2)}) copy-start(s32[8]{0:T(128)} %param.23) | copy-start | bytes 100
  9.8 159.6 %reduce-scatter.4.cloned.1.call-start = ((), (), s32[]{:S(2)}) async-start(), calls=%async_computation.4 | async-start | bytes 2293760 | tf_op jit(solution)/shard_map/reduce_scatter | solution.py:56
  10.5 77.4 %copy-start.9 = (f32[448,32]{0,1:T(8,128)S(1)}, f32[448,32]{0,1:T(8,128)}, u32[]{:S(2)}) copy-start(f32[448,32]{0,1:T(8,128)} %param.17) | copy-start | bytes 172036
  87.9 44.7 %copy-start.6 = (bf16[128,128]{1,0:T(8,128)(2,1)S(1)}, bf16[128,128]{1,0:T(8,128)(2,1)}, u32[]{:S(2)}) copy-start(bf16[128,128]{1,0:T(8,128)(2,1)} %param.20) | copy-start | bytes 98308
  88.0 54.2 %copy-start.10 = (f32[112,64]{0,1:T(8,128)S(1)}, f32[112,64]{0,1:T(8,128)}, u32[]{:S(2)}) copy-start(f32[112,64]{0,1:T(8,128)} %param.19) | copy-start | bytes 86020
  88.0 3.8 %copy-start.2 = (bf16[448,32,192]{0,2,1:T(8,128)(2,1)S(1)}, bf16[448,32,192]{0,2,1:T(8,128)(2,1)}, u32[]{:S(2)}) copy-start(bf16[448,32,192]{0,2,1:T(8,128)(2,1)} %get-tuple-element.648) | copy-start | bytes 16515076 | tf_op jit(solution)/shard_map/while
  98.1 3.8 %copy-start.2 = (bf16[448,32,192]{0,2,1:T(8,128)(2,1)S(1)}, bf16[448,32,192]{0,2,1:T(8,128)(2,1)}, u32[]{:S(2)}) copy-start(bf16[448,32,192]{0,2,1:T(8,128)(2,1)} %get-tuple-element.648) | copy-start | bytes 16515076 | tf_op jit(solution)/shard_map/while
  108.3 3.8 %copy-start.2 = (bf16[448,32,192]{0,2,1:T(8,128)(2,1)S(1)}, bf16[448,32,192]{0,2,1:T(8,128)(2,1)}, u32[]{:S(2)}) copy-start(bf16[448,32,192]{0,2,1:T(8,128)(2,1)} %get-tuple-element.648) | copy-start | bytes 16515076 | tf_op jit(solution)/shard_map/while
  118.4 3.8 %copy-start.2 = (bf16[448,32,192]{0,2,1:T(8,128)(2,1)S(1)}, bf16[448,32,192]{0,2,1:T(8,128)(2,1)}, u32[]{:S(2)}) copy-start(bf16[448,32,192]{0,2,1:T(8,128)(2,1)} %get-tuple-element.648) | copy-start | bytes 16515076 | tf_op jit(solution)/shard_map/while
  128.6 1.3 copy-start.1
  129.9 150.9 %reduce-scatter.6.cloned.1.call-start = ((), (), s32[]{:S(2)}) async-start(), calls=%async_computation.5 | async-start | bytes 589824 | tf_op jit(solution)/shard_map/reduce_scatter | solution.py:110
  142.2 28.4 %copy-start.7 = (f32[112]{0:T(128)S(1)}, f32[112]{0:T(128)}, u32[]{:S(2)}) copy-start(f32[112]{0:T(128)} %param.21) | copy-start | bytes 1348
  182.2 5.7 %copy-start = (bf16[112,64,256]{2,0,1:T(8,128)(2,1)S(1)}, bf16[112,64,256]{2,0,1:T(8,128)(2,1)}, u32[]{:S(2)}) copy-start(bf16[112,64,256]{2,0,1:T(8,128)(2,1)} %get-tuple-element.621) | copy-start | bytes 11010052 | tf_op jit(solution)/shard_map/while
  182.2 6.8 %copy-start.4 = (f32[112,64]{0,1:T(8,128)S(1)}, f32[112,64]{0,1:T(8,128)}, u32[]{:S(2)}) copy-start(f32[112,64]{0,1:T(8,128)} %get-tuple-element.695) | copy-start | bytes 86020 | tf_op jit(solution)/shard_map/while
  199.9 6.8 %copy-start = (bf16[112,64,256]{2,0,1:T(8,128)(2,1)S(1)}, bf16[112,64,256]{2,0,1:T(8,128)(2,1)}, u32[]{:S(2)}) copy-start(bf16[112,64,256]{2,0,1:T(8,128)(2,1)} %get-tuple-element.621) | copy-start | bytes 11010052 | tf_op jit(solution)/shard_map/while
  199.9 7.9 %copy-start.4 = (f32[112,64]{0,1:T(8,128)S(1)}, f32[112,64]{0,1:T(8,128)}, u32[]{:S(2)}) copy-start(f32[112,64]{0,1:T(8,128)} %get-tuple-element.695) | copy-start | bytes 86020 | tf_op jit(solution)/shard_map/while
  207.8 0.6 copy-start.5
  218.7 6.8 %copy-start = (bf16[112,64,256]{2,0,1:T(8,128)(2,1)S(1)}, bf16[112,64,256]{2,0,1:T(8,128)(2,1)}, u32[]{:S(2)}) copy-start(bf16[112,64,256]{2,0,1:T(8,128)(2,1)} %get-tuple-element.621) | copy-start | bytes 11010052 | tf_op jit(solution)/shard_map/while
  218.7 7.9 %copy-start.4 = (f32[112,64]{0,1:T(8,128)S(1)}, f32[112,64]{0,1:T(8,128)}, u32[]{:S(2)}) copy-start(f32[112,64]{0,1:T(8,128)} %get-tuple-element.695) | copy-start | bytes 86020 | tf_op jit(solution)/shard_map/while
  237.5 6.8 %copy-start = (bf16[112,64,256]{2,0,1:T(8,128)(2,1)S(1)}, bf16[112,64,256]{2,0,1:T(8,128)(2,1)}, u32[]{:S(2)}) copy-start(bf16[112,64,256]{2,0,1:T(8,128)(2,1)} %get-tuple-element.621) | copy-start | bytes 11010052 | tf_op jit(solution)/shard_map/while
  237.5 7.9 %copy-start.4 = (f32[112,64]{0,1:T(8,128)S(1)}, f32[112,64]{0,1:T(8,128)}, u32[]{:S(2)}) copy-start(f32[112,64]{0,1:T(8,128)} %get-tuple-element.695) | copy-start | bytes 86020 | tf_op jit(solution)/shard_map/while
  246.1 0.8 copy-start.3
  246.9 55.7 %reduce-scatter.8.cloned.1.call-start = ((), (), s32[]{:S(2)}) async-start(), calls=%async_computation.6 | async-start | bytes 81920 | tf_op jit(solution)/shard_map/reduce_scatter | solution.py:111
  (3 other events, 1.9 us)
Sparse Core Ops, SparseCore 0:
  10.4 77.2 all-gather.1
  130.0 39.4 reduce-scatter.3
  247.0 33.7 reduce-scatter.5
  283.5 19.0 reduce-scatter.7
where the time goes:
time: 310 us; the launch traced here: 309 us
  waiting for transfers between devices  125 us (40%)
  matrix products  123 us (40%)
  local copies, waits for them, and re-layouts  29.9 us (10%)
  between operations  14.6 us (5%)
  blocking collectives  9.45 us (3%)
  other arithmetic  6.68 us (2%)
    all_gather x1, waiting for transfers between devices, per_device(): lax.all_gather(main_k, 'ctx', axis=0, tiled=True)  68.8 us
    dot_general x8, matrix products, raw_scores(): jnp.einsum('tjd,kd->tjk', index_q, key_block, preferred_element_type=jnp....  67.1 us
    reduce_scatter x1, waiting for transfers between devices, per_device(): lax.psum_scatter(key_terms, 'ctx', scatter_dimension=0, tiled=True)  33.8 us
    dot_general x4, matrix products, second_pass(): jnp.einsum('tjk,kd->tjd', score_grad, key_block, preferred_element_type=j...  25.9 us
    dot_general x4, matrix products, add_block(): jnp.einsum('qhd,khd->qhk', queries_wide, key_block, preferred_element_typ...  25.2 us
    reduce_scatter x1, waiting for transfers between devices, per_device(): grad_k = lax.psum_scatter(ctx_sums, 'tp', scatter_dimension=0, tiled=True)  21.8 us
    unnamed x16, local copies, waits for them, and re-layouts  12.9 us
    all_gather x1, blocking collectives, per_device(): index_keys = lax.all_gather(index_k, 'ctx', axis=0, tiled=True)  9.45 us
  transfers between devices with their start and end apart: 4, of which 4 were waited for; matrix products, arithmetic and copies ran while one was open for 12% of the time, Pallas kernels for 0%

commit v1 on v0

v1 whole, which is shorter than its diff:
```python
import functools
import math

import jax
import jax.numpy as jnp
from jax import lax
from jax.experimental import pallas as pl
from jax.experimental.pallas import tpu as pltpu
from jax.sharding import PartitionSpec as P

LOG2E = math.log2(math.e)
LN2 = math.log(2.0)
VMEM_BYTES = 56 * 1024 * 1024
BF = jnp.bfloat16
F32 = jnp.float32


def prep_kernel(width, heads_step, root, q_ref, ln_ref, out_ref):
    step = pl.program_id(0)
    heads = ln_ref.shape[1]
    pad = 2 * 128
    cols = heads_step * pad
    scaled = -root * ln_ref[...]
    high = scaled.astype(BF)
    rest = scaled - high.astype(F32)
    mid = rest.astype(BF)
    low = (rest - mid.astype(F32)).astype(BF)
    column = lax.broadcasted_iota(jnp.int32, (heads, cols), 1)
    head = lax.broadcasted_iota(jnp.int32, (heads, cols), 0) - step * heads_step
    spare = jnp.where(head % 2 == 0, width, 0)
    offset = column - head * pad - spare
    extra = jnp.zeros((q_ref.shape[0], cols), F32)
    for number, piece in enumerate((high, mid, low)):
        place = jnp.where(offset == number, 1.0, 0.0).astype(BF)
        extra = extra + jnp.dot(piece, place, preferred_element_type=F32)
    lane = lax.broadcasted_iota(jnp.int32, (q_ref.shape[0], pad), 1)
    for h in range(heads_step):
        first = (h // 2) * 2 * width + (h % 2) * (2 * width - pad)
        kept = lane < width if h % 2 == 0 else lane >= pad - width
        own = q_ref[:, first : first + pad].astype(F32)
        out_ref[:, h * pad : (h + 1) * pad] = jnp.where(
            kept, own, extra[:, h * pad : (h + 1) * pad]
        ).astype(BF)


def prep(main_q, log_norms, width):
    rows, total = main_q.shape
    heads = log_norms.shape[1]
    step_heads = 8
    return pl.pallas_call(
        functools.partial(prep_kernel, width, step_heads, math.sqrt(width)),
        grid=(heads // step_heads,),
        in_specs=[
            pl.BlockSpec((rows, step_heads * width), lambda i: (0, i)),
            pl.BlockSpec((rows, heads), lambda i: (0, 0)),
        ],
        out_specs=pl.BlockSpec((rows, step_heads * 256), lambda i: (0, i)),
        out_shape=jax.ShapeDtypeStruct((rows, heads * 256), BF),
        compiler_params=pltpu.CompilerParams(vmem_limit_bytes=VMEM_BYTES),
        name="prep",
    )(main_q, log_norms)


def mass_kernel(width, heads_step, n_keys, ranks, pos_ref, qa_ref, kpos_ref, *refs):
    key_refs, out_refs, total_ref = refs[:n_keys], refs[n_keys : n_keys + ranks], refs[n_keys + ranks]
    step = pl.program_id(0)
    pad = 256
    factor = LOG2E / math.sqrt(width)
    total = sum(r.shape[0] for r in key_refs)
    lane = lax.broadcasted_iota(jnp.int32, (total, pad), 1)
    ones_even = jnp.where((lane >= width) & (lane < width + 3), 1.0, 0.0).astype(BF)
    ones_odd = jnp.where(lane < 3, 1.0, 0.0).astype(BF)
    keep_even = jnp.where(lane < width, 1.0, 0.0).astype(BF)
    keep_odd = jnp.where(lane >= pad - width, 1.0, 0.0).astype(BF)

    @pl.when(step == 0)
    def _():
        total_ref[...] = jnp.zeros_like(total_ref)

    def one(h):
        first = (h // 2) * 2 * width + (h % 2) * (2 * width - pad)
        parts = [r[:, first : first + pad] for r in key_refs]
        keys = parts[0] if len(parts) == 1 else jnp.concatenate(parts, axis=0)
        if h % 2 == 0:
            keys = keys * keep_even + ones_even
        else:
            keys = keys * keep_odd + ones_odd
        scores = lax.dot_general(
            qa_ref[:, h * pad : (h + 1) * pad], keys, (((1,), (1,)), ((), ())),
            preferred_element_type=F32,
        )
        return jnp.exp2(scores * factor)

    for h in range(0, heads_step, 2):
        total_ref[...] += one(h) + one(h + 1)

    @pl.when(step == pl.num_programs(0) - 1)
    def _():
        own = total_ref.shape[0] // ranks
        for k in range(ranks):
            first = lax.rem(pos_ref[1] + k, ranks) * own
            row = pos_ref[0] + first + lax.broadcasted_iota(jnp.int32, out_refs[k].shape, 0)
            rows = total_ref[pl.ds(pl.multiple_of(first, 8), own), :]
            out_refs[k][...] = jnp.where(kpos_ref[...] <= row, rows, 0.0)


def mass(places, qa, kpos, key_list, width, ranks, step_heads=8):
    rows = qa.shape[0]
    heads = qa.shape[1] // 256
    total = sum(k.shape[0] for k in key_list)
    own = rows // ranks
    return pl.pallas_call(
        functools.partial(mass_kernel, width, step_heads, len(key_list), ranks),
        grid=(heads // step_heads,),
        in_specs=[
            pl.BlockSpec(memory_space=pltpu.SMEM),
            pl.BlockSpec((rows, step_heads * 256), lambda i: (0, i)),
            pl.BlockSpec((1, total), lambda i: (0, 0)),
        ]
        + [pl.BlockSpec((k.shape[0], step_heads * width), lambda i: (0, i)) for k in key_list],
        out_specs=[pl.BlockSpec((own, total), lambda i: (0, 0))] * ranks,
        out_shape=[jax.ShapeDtypeStruct((own, total), F32)] * ranks,
        scratch_shapes=[pltpu.VMEM((rows, total), F32)],
        compiler_params=pltpu.CompilerParams(vmem_limit_bytes=VMEM_BYTES),
        name="mass",
    )(places, qa, kpos, *key_list)


def first_kernel(heads, rows, scale, pos_ref, q_ref, key_ref, w_ref, kpos_ref,
                 sig_ref, dev_ref, prob_ref, raw, soft):
    keys = key_ref.shape[0]
    raw[...] = lax.dot_general(
        q_ref[...], key_ref[...], (((1,), (1,)), ((), ())), preferred_element_type=F32
    )
    w_turned = jnp.transpose(w_ref[...])
    for t in range(rows):
        w = w_turned[:, t : t + 1]
        w_soft = w * LN2
        w_sig = w * scale
        for c in range(keys // 128):
            at = (slice(t * heads, (t + 1) * heads), slice(c * 128, (c + 1) * 128))
            u = raw[at] * (scale * LOG2E)
            low = jnp.minimum(u, 0.0)
            high = jnp.maximum(u, 0.0)
            e = jnp.exp2(low - high)
            log_term = jnp.where(e < 2.0**-11, e * LOG2E, jnp.log2(1.0 + e))
            sp = high + log_term
            soft[at] = sp
            sig_ref[at] = jnp.exp2(low - log_term) * w_sig
            prob_ref[t : t + 1, c * 128 : (c + 1) * 128] = jnp.sum(w_soft * sp, axis=0, keepdims=True)

    row = pos_ref[0] + pl.program_id(0) * rows + lax.broadcasted_iota(jnp.int32, prob_ref.shape, 0)
    masked = jnp.where(kpos_ref[...] <= row, prob_ref[...], -jnp.inf)
    top = jnp.max(masked, axis=1, keepdims=True)
    terms = jnp.exp2((masked - top) * LOG2E)
    prob_ref[...] = terms / jnp.sum(terms, axis=1, keepdims=True)

    for t in range(rows):
        total = jnp.zeros((heads, 128), F32)
        for c in range(keys // 128):
            at = (slice(t * heads, (t + 1) * heads), slice(c * 128, (c + 1) * 128))
            total = total + soft[at] * prob_ref[t : t + 1, c * 128 : (c + 1) * 128]
        mean = LN2 * jnp.sum(total, axis=1, keepdims=True)
        for c in range(keys // 128):
            at = (slice(t * heads, (t + 1) * heads), slice(c * 128, (c + 1) * 128))
            dev_ref[at] = (mean - LN2 * soft[at]).astype(BF)


def first_pass(own_pos, q_flat, keys, weights, kpos, rows=8):
    total, width = q_flat.shape
    key_total = keys.shape[0]
    own, heads = weights.shape
    tile = rows * heads
    return pl.pallas_call(
        functools.partial(first_kernel, heads, rows, 1.0 / math.sqrt(width)),
        grid=(own // rows,),
        in_specs=[
            pl.BlockSpec(memory_space=pltpu.SMEM),
            pl.BlockSpec((tile, width), lambda i: (i, 0)),
            pl.BlockSpec((key_total, width), lambda i: (0, 0)),
            pl.BlockSpec((rows, heads), lambda i: (i, 0)),
            pl.BlockSpec((1, key_total), lambda i: (0, 0)),
        ],
        out_specs=[
            pl.BlockSpec((tile, key_total), lambda i: (i, 0)),
            pl.BlockSpec((tile, key_total), lambda i: (i, 0)),
            pl.BlockSpec((rows, key_total), lambda i: (i, 0)),
        ],
        out_shape=[
            jax.ShapeDtypeStruct((total, key_total), F32),
            jax.ShapeDtypeStruct((total, key_total), BF),
            jax.ShapeDtypeStruct((own, key_total), F32),
        ],
        scratch_shapes=[pltpu.VMEM((tile, key_total), F32), pltpu.VMEM((tile, key_total), F32)],
        compiler_params=pltpu.CompilerParams(vmem_limit_bytes=VMEM_BYTES),
        name="first_pass",
    )(own_pos, q_flat, keys, weights, kpos)


def second_kernel(heads, rows, group, splits, sig_ref, dev_ref, prob_ref, rw_ref, key_ref, qt_ref, *refs):
    count = sum(splits)
    parts, (gq_ref, gw_ref, gk_ref, grad, sums) = refs[:count], refs[count:]
    keys = key_ref.shape[0]
    groups = []
    for size in splits:
        groups.append(sum(r[...] for r in parts[:size]))
        parts = parts[size:]
    mass_rows = jnp.concatenate(groups, axis=1)
    target = rw_ref[...] * mass_rows / jnp.sum(mass_rows, axis=1, keepdims=True)
    coef = rw_ref[...] * prob_ref[...] - target

    @pl.when(pl.program_id(0) == 0)
    def _():
        gk_ref[...] = jnp.zeros_like(gk_ref)

    span = group * heads
    for g in range(rows // group):
        for u in range(group):
            t = g * group + u
            total = jnp.zeros((heads, 128), F32)
            for c in range(keys // 128):
                at = (slice(t * heads, (t + 1) * heads), slice(c * 128, (c + 1) * 128))
                cols = slice(c * 128, (c + 1) * 128)
                grad[at] = (sig_ref[at] * coef[t : t + 1, cols]).astype(BF)
                total = total + dev_ref[at].astype(F32) * target[t : t + 1, cols]
            sums[t * heads : (t + 1) * heads, :] = total
        block = grad[g * span : (g + 1) * span, :]
        gq_ref[g * span : (g + 1) * span, :] = jnp.dot(block, key_ref[...], preferred_element_type=F32)
        gk_ref[...] += jnp.dot(qt_ref[:, g * span : (g + 1) * span], block, preferred_element_type=F32)
    ones = jnp.ones((8, 128), F32)
    added = lax.dot_general(
        ones, sums[...], (((1,), (1,)), ((), ())), preferred_element_type=F32, precision=lax.Precision.HIGHEST
    )
    gw_ref[...] = added.reshape(gw_ref.shape)


def second_pass(sig, dev, prob, mass_parts, row_weight, keys, q_turned, heads, rows=8, group=4):
    total, key_total = sig.shape
    own = total // heads
    tile = rows * heads
    width = keys.shape[1]
    flat = [piece for pieces in mass_parts for piece in pieces]
    gq, gw, gk = pl.pallas_call(
        functools.partial(second_kernel, heads, rows, group, tuple(len(p) for p in mass_parts)),
        grid=(own // rows,),
        in_specs=[
            pl.BlockSpec((tile, key_total), lambda i: (i, 0)),
            pl.BlockSpec((tile, key_total), lambda i: (i, 0)),
            pl.BlockSpec((rows, key_total), lambda i: (i, 0)),
            pl.BlockSpec((rows, 1), lambda i: (i, 0)),
            pl.BlockSpec((key_total, width), lambda i: (0, 0)),
            pl.BlockSpec((width, tile), lambda i: (0, i)),
        ]
        + [pl.BlockSpec((rows, p.shape[1]), lambda i: (i, 0)) for p in flat],
        out_specs=[
            pl.BlockSpec((tile, width), lambda i: (i, 0)),
            pl.BlockSpec((1, 8, tile), lambda i: (i, 0, 0)),
            pl.BlockSpec((width, key_total), lambda i: (0, 0)),
        ],
        out_shape=[
            jax.ShapeDtypeStruct((total, width), F32),
            jax.ShapeDtypeStruct((own // rows, 8, tile), F32),
            jax.ShapeDtypeStruct((width, key_total), F32),
        ],
        scratch_shapes=[pltpu.VMEM((tile, key_total), BF), pltpu.VMEM((tile, 128), F32)],
        compiler_params=pltpu.CompilerParams(vmem_limit_bytes=VMEM_BYTES),
        name="second_pass",
    )(sig, dev, prob, row_weight, keys, q_turned, *flat)
    return gq, gw[:, 0, :].reshape(own, heads), gk


def swap(x, bit):
    size = lax.axis_size("ctx")
    return lax.ppermute(x, "ctx", [(i, i ^ bit) for i in range(size)])


def turn(x, steps):
    size = lax.axis_size("tp")
    return lax.ppermute(x, "tp", [(i, (i + steps) % size) for i in range(size)])


def after(x, *others):
    return lax.optimization_barrier((x, *others))[0]


def per_device(main_q, main_k, log_norms, index_q, index_w, index_k, row_weight, offsets, key_map):
    key_rows = main_k.shape[0]
    own_rows, heads, index_width = index_q.shape
    main_heads = log_norms.shape[1]
    width = main_k.shape[1] // main_heads
    places_ctx = lax.axis_size("ctx")
    ranks = lax.axis_size("tp")
    here = lax.axis_index("ctx")
    rank = lax.axis_index("tp")
    half = key_rows // 2
    far_bits = [b for b in (2**i for i in range(1, places_ctx.bit_length() - 1))]
    far = [sum(b for i, b in enumerate(far_bits) if n >> i & 1) for n in range(1, 2 ** len(far_bits))]
    near_far = [d for d in far if d & (d - 1) == 0]
    rest_far = [d for d in far if d & (d - 1) != 0]

    top, low = main_k[:half], main_k[half:]
    pieces = {(0, 0): top, (0, 1): low}
    index_keys = swap(index_k, 1)
    index_keys = jnp.concatenate([index_k, index_keys], axis=0)
    for n, b in enumerate(near_far):
        for part in (1 - n % 2, n % 2):
            pieces[b, part] = swap(pieces[0, part], b)
    sibling = swap(main_k, 1)
    for b in far_bits:
        index_keys = jnp.concatenate([index_keys, swap(index_keys, b)], axis=0)

    order = [0, 1] + [d + s for d in near_far for s in (0, 1)] + [d + s for d in rest_far for s in (0, 1)]
    blocks = jnp.stack([here ^ d for d in order])
    key_pos = (key_map[blocks][:, None] * key_rows + jnp.arange(key_rows, dtype=jnp.int32)[None, :]).reshape(1, -1)
    if order != sorted(order):
        index_keys = jnp.concatenate([index_keys[d * key_rows : (d + 1) * key_rows] for d in order], axis=0)
    places = jnp.stack([offsets[0], rank]).astype(jnp.int32)
    own_pos = (offsets[0] + rank * own_rows).reshape(1).astype(jnp.int32)

    def head_sums(first, key_list):
        size = sum(k.shape[0] for k in key_list)
        first = first * key_rows
        sums = mass(places, queries, key_pos[:, first : first + size], key_list, width, ranks)
        return [sums[0]] + [turn(sums[k], k) for k in range(1, ranks)]

    queries = prep(main_q, log_norms, width)
    sums_0 = head_sums(0, [main_k, sibling])

    for d in rest_far:
        for part in (0, 1):
            last = (d & -d) if part == 0 else 1 << (d.bit_length() - 1)
            pieces[d, part] = swap(pieces[d ^ last, part], last)

    def group_of(numbers):
        chosen = []
        for d in numbers:
            own = [pieces[d, 0], pieces[d, 1]]
            chosen += own + [swap(p, 1) for p in own]
        return chosen

    q_flat = index_q.reshape(own_rows * heads, index_width)
    sig, dev, prob = first_pass(own_pos, q_flat, index_keys, index_w, key_pos)
    sums_1 = head_sums(2, group_of(near_far))
    sums_2 = head_sums(2 + 2 * len(near_far), group_of(rest_far))
    grad_q, grad_w, key_terms = second_pass(
        sig, dev, prob, [sums_0, sums_1, sums_2], row_weight[:, None], index_keys, q_flat.T, heads
    )

    blocks_of = {d: key_terms[:, i * key_rows : (i + 1) * key_rows] for i, d in enumerate(order)}
    for bit in [1] + far_bits:
        kept = [d for d in sorted(blocks_of) if not d & bit]
        sent = swap(jnp.stack([blocks_of[d ^ bit] for d in kept]), bit)
        blocks_of = {d: blocks_of[d] + sent[i] for i, d in enumerate(kept)}
    terms = blocks_of[0].T.reshape(ranks, key_rows // ranks, index_width)
    grad_k = lax.dynamic_index_in_dim(terms, rank, 0, keepdims=False)
    for k in range(1, ranks):
        grad_k = grad_k + turn(lax.dynamic_index_in_dim(terms, (rank + k) % ranks, 0, keepdims=False), k)
    return (grad_q.reshape(index_q.shape), grad_w, grad_k)


def solution(mesh):
    placed = (
        P("ctx", "tp"),
        P("ctx", "tp"),
        P("ctx", "tp"),
        P(("ctx", "tp"), None, None),
        P(("ctx", "tp"), None),
        P("ctx", None),
        P(("ctx", "tp")),
        P("ctx"),
        P(),
    )
    return jax.shard_map(
        per_device,
        mesh=mesh,
        in_specs=placed,
        out_specs=(P(("ctx", "tp"), None, None), P(("ctx", "tp"), None), P(("ctx", "tp"), None)),
        check_vma=False,
    )
```

time: 310 us -> 206 us (0.66)
  matrix products: 123 us -> 0 us
  Pallas kernels: 0 us -> 86.1 us
  waiting for transfers between devices: 125 us -> 61.8 us
  starting transfers between devices: 0.16 us -> 36.1 us
  local copies, waits for them, and re-layouts: 29.9 us -> 14 us
  between operations: 14.6 us -> 1.56 us
  blocking collectives: 9.45 us -> 0 us
    dot_general x20 -> x0, matrix products: 123 us -> none  [the longest x8 67.1 us: raw_scores(): jnp.einsum('tjd,kd->tjk', index_q, key_block, preferred_element_type=jnp....]
    pallas_call x0 -> x6, Pallas kernels: none -> 86.1 us  [the longest x1 29.5 us: first_pass(): pl.pallas_call(functools.partial(first_kernel, heads, rows, 1.0 / math.sq...]
    all_gather x1 -> x0, waiting for transfers between devices: 68.8 us -> none  [per_device(): lax.all_gather(main_k, 'ctx', axis=0, tiled=True)]
    ppermute x0 -> x31, waiting for transfers between devices: none -> 61.8 us  [the longest x19 57.9 us: swap(): return lax.ppermute(x, 'ctx', [(i, i ^ bit) for i in range(size)])]
    reduce_scatter x3 -> x0, waiting for transfers between devices: 56.1 us -> none  [the longest x1 33.8 us: per_device(): lax.psum_scatter(key_terms, 'ctx', scatter_dimension=0, tiled=True)]
    ppermute x0 -> x31, starting transfers between devices: none -> 36.1 us  [the longest x12 23 us: turn(): return lax.ppermute(x, 'tp', [(i, (i + steps) % size) for i in range(size)])]
    dynamic_slice x12 -> x0, local copies, waits for them, and re-layouts: 9.67 us -> none  [the longest x4 9.31 us: add_block(): lax.dynamic_slice_in_dim(keys, first_key, block_keys, 0)]
    all_gather x1 -> x0, blocking collectives: 9.45 us -> none  [per_device(): index_keys = lax.all_gather(index_k, 'ctx', axis=0, tiled=True)]
  transfers between devices with their start and end apart: 4 -> 31, of which waited for: 4 -> 12; matrix products, arithmetic and copies ran while one was open for 12% -> 6% of each run, Pallas kernels for 0% -> 30%
where the time goes in v1:
time: 206 us; the launch traced here: 205 us
  Pallas kernels  86.1 us (42%)
  waiting for transfers between devices  61.8 us (30%)
  starting transfers between devices  36.1 us (18%)
  local copies, waits for them, and re-layouts  14 us (7%)
  other arithmetic  5.55 us (3%)
    ppermute x19, waiting for transfers between devices, swap(): return lax.ppermute(x, 'ctx', [(i, i ^ bit) for i in range(size)])  57.9 us
    pallas_call x1, Pallas kernels, first_pass(): pl.pallas_call(functools.partial(first_kernel, heads, rows, 1.0 / math.sq...  29.5 us
    pallas_call x1, Pallas kernels, second_pass(): pl.pallas_call(functools.partial(second_kernel, heads, rows, group, tuple...  24.3 us
    ppermute x12, starting transfers between devices, turn(): return lax.ppermute(x, 'tp', [(i, (i + steps) % size) for i in range(size)])  23 us
    pallas_call x3, Pallas kernels, mass(): pl.pallas_call(functools.partial(mass_kernel, width, step_heads, len(key_...  22.7 us
    ppermute x19, starting transfers between devices, swap(): return lax.ppermute(x, 'ctx', [(i, i ^ bit) for i in range(size)])  13 us
    pallas_call x1, Pallas kernels, prep(): pl.pallas_call(functools.partial(prep_kernel, width, step_heads, math.sqr...  9.53 us
  transfers between devices with their start and end apart: 31, of which 12 were waited for; matrix products, arithmetic and copies ran while one was open for 6% of the time, Pallas kernels for 30%

profile of v1, /device:TPU:0, one launch (start us, length us, event | category | flops | bytes accessed | tf_op | source)
XLA Modules:
  0.0 205.1 jit_solution(5830198748357218391)
XLA Ops:
  2.2 3.0 %collective-permute-start.12 = (bf16[64,6144]{1,0:T(8,128)(2,1)S(1)}, bf16[64,6144]{1,0:T(8,128)(2,1)S(1)}, u32[]{:S(2)}, u32[]{:S(2)}) collective-permute-start(bf16[64,6144]{1,0:T(8,128)(2,1)S(1)} %get-tuple-element.45), channel_id=1, source_target_pairs={{0,16},{4,20},{8,24},{12,28},{16,0},{20,4},{24,8},{28,12},{1,17},{... | collective-permute-start | bytes 2359304 | tf_op jit(solution)/shard_map/ppermute | solution.py:274
  9.5 1.9 collective-permute-start.1
  11.4 12.2 %collective-permute-done.12.refs_5_ = bf16[64,6144]{1,0:T(8,128)(2,1)S(1)} collective-permute-done((bf16[64,6144]{1,0:T(8,128)(2,1)S(1)}, bf16[64,6144]{1,0:T(8,128)(2,1)S(1)}, u32[]{:S(2)}, u32[]{:S(2)}) %collective-permute-start.12) | collective-permute-done | bytes 786464 | tf_op jit(solution)/shard_map/ppermute | solution.py:274
  23.6 2.1 %collective-permute-done.8.refs_1_ = bf16[64,6144]{1,0:T(8,128)(2,1)S(1)} collective-permute-done((bf16[64,6144]{1,0:T(8,128)(2,1)S(1)}, bf16[64,6144]{1,0:T(8,128)(2,1)S(1)}, u32[]{:S(2)}, u32[]{:S(2)}) %collective-permute-start.8) | collective-permute-done | bytes 786464 | tf_op jit(solution)/shard_map/ppermute | solution.py:274
  25.7 16.7 %collective-permute-done.1 = bf16[256,128]{1,0:T(8,128)(2,1)S(1)} collective-permute-done((bf16[256,128]{1,0:T(8,128)(2,1)S(1)}, bf16[256,128]{1,0:T(8,128)(2,1)S(1)}, u32[]{:S(2)}, u32[]{:S(2)}) %collective-permute-start.1) | collective-permute-done | bytes 65568 | tf_op jit(solution)/shard_map/ppermute | solution.py:274
  45.3 11.2 %collective-permute-done.19.refs_1_ = bf16[64,6144]{1,0:T(8,128)(2,1)} collective-permute-done((bf16[64,6144]{1,0:T(8,128)(2,1)S(1)}, bf16[64,6144]{1,0:T(8,128)(2,1)}, u32[]{:S(2)}, u32[]{:S(2)}) %collective-permute-start.19) | collective-permute-done | bytes 786464 | tf_op jit(solution)/shard_map/ppermute | solution.py:274
  57.1 5.7 %collective-permute-done.18.refs_0_ = bf16[64,6144]{1,0:T(8,128)(2,1)} collective-permute-done((bf16[64,6144]{1,0:T(8,128)(2,1)}, bf16[64,6144]{1,0:T(8,128)(2,1)}, u32[]{:S(2)}, u32[]{:S(2)}) %collective-permute-start.18) | collective-permute-done | bytes 786464 | tf_op jit(solution)/shard_map/ppermute | solution.py:274
  66.8 9.5 %prep.1.qa_ref = bf16[448,8192]{1,0:T(8,128)(2,1)} custom-call(bf16[448,6144]{1,0:T(8,128)(2,1)} %q_ref.1, f32[448,32]{1,0:T(8,128)} %copy.24.ln_ref), custom_call_target="tpu_custom_call" | custom-call | tf_op jit(solution)/shard_map/prep/pallas_call | solution.py:50
  76.3 6.7 %mass.3 = (f32[112,256]{1,0:T(8,128)}, f32[112,256]{1,0:T(8,128)}, f32[112,256]{1,0:T(8,128)}, f32[112,256]{1,0:T(8,128)}) custom-call(s32[2]{0:T(128)} %pad_add_fusion.pos_ref, bf16[448,8192]{1,0:T(8,128)(2,1)} %prep.1.qa_ref, s32[1,256]{1,0:T(1,128)} %get-tuple-element.57.kpos_ref, bf16[128,6144]{1,0:T(8,128)(2,1)} %refs_0_.1, bf16[128,6144]{1,0:T(8,128)(2,1)} %copy-done.3), custom_call_target="tpu_custom_call" | custom-call | tf_op jit(solution)/shard_map/mass/pallas_call | solution.py:112
  83.0 1.6 collective-permute-start.4
  85.2 9.3 %mass.4 = (f32[112,512]{1,0:T(8,128)}, f32[112,512]{1,0:T(8,128)}, f32[112,512]{1,0:T(8,128)}, f32[112,512]{1,0:T(8,128)}) custom-call(s32[2]{0:T(128)} %pad_add_fusion.pos_ref, bf16[448,8192]{1,0:T(8,128)(2,1)} %prep.1.qa_ref, s32[1,512]{1,0:T(1,128)} %slice.83.kpos_ref, bf16[64,6144]{1,0:T(8,128)(2,1)} %collective-permute-done.7.refs_0_, ...), custom_call_target="tpu_custom_call" | custom-call | tf_op jit(solution)/shard_map/mass/pallas_call | solution.py:112
  94.5 1.6 collective-permute-start.15
  97.6 2.9 %copy.23 = bf16[7168,128]{0,1:T(8,128)(2,1)} copy(bf16[7168,128]{1,0:T(8,128)(2,1)S(1)} %bitcast.89) | data formatting | bytes 3670016 | tf_op jit(solution)/shard_map/reshape | solution.py:341
  101.7 2.8 %collective-permute-start.6 = (f32[112,256]{1,0:T(8,128)}, f32[112,256]{1,0:T(8,128)S(1)}, u32[]{:S(2)}, u32[]{:S(2)}) collective-permute-start(f32[112,256]{1,0:T(8,128)} %get-tuple-element.27), channel_id=1, source_target_pairs={{0,3},{1,0},{2,1},{3,2},{4,7},{5,4},{6,5},{7,6},{8,11},{9,8},{10,9... | collective-permute-start | bytes 344072 | tf_op jit(solution)/shard_map/ppermute | solution.py:279
  106.2 6.8 %mass.5 = (f32[112,256]{1,0:T(8,128)}, f32[112,256]{1,0:T(8,128)}, f32[112,256]{1,0:T(8,128)}, f32[112,256]{1,0:T(8,128)}) custom-call(s32[2]{0:T(128)} %pad_add_fusion.pos_ref, bf16[448,8192]{1,0:T(8,128)(2,1)} %prep.1.qa_ref, s32[1,256]{1,0:T(1,128)} %get-tuple-element.56.kpos_ref, bf16[64,6144]{1,0:T(8,128)(2,1)} %collective-permute-done.18.refs_0_, ...), custom_call_target="tpu_custom_call" | custom-call | tf_op jit(solution)/shard_map/mass/pallas_call | solution.py:112
  114.0 6.9 %collective-permute-start.22 = (f32[112,256]{1,0:T(8,128)}, f32[112,256]{1,0:T(8,128)S(1)}, u32[]{:S(2)}, u32[]{:S(2)}) collective-permute-start(f32[112,256]{1,0:T(8,128)} %get-tuple-element.33), channel_id=1, source_target_pairs={{0,1},{1,2},{2,3},{3,0},{4,5},{5,6},{6,7},{7,4},{8,9},{9,10},{10,1... | collective-permute-start | bytes 344072 | tf_op jit(solution)/shard_map/ppermute | solution.py:279
  120.9 3.3 %collective-permute-start.23 = (f32[112,256]{1,0:T(8,128)}, f32[112,256]{1,0:T(8,128)S(1)}, u32[]{:S(2)}, u32[]{:S(2)}) collective-permute-start(f32[112,256]{1,0:T(8,128)} %get-tuple-element.34), channel_id=1, source_target_pairs={{0,2},{1,3},{2,0},{3,1},{4,6},{5,7},{6,4},{7,5},{8,10},{9,11},{10,... | collective-permute-start | bytes 344072 | tf_op jit(solution)/shard_map/ppermute | solution.py:279
  125.9 29.5 %first_pass.1 = (f32[7168,1024]{1,0:T(8,128)}, bf16[7168,1024]{1,0:T(8,128)(2,1)}, f32[112,1024]{1,0:T(8,128)}) custom-call(s32[1]{0:T(128)} %bitcast.1.pos_ref, bf16[7168,128]{1,0:T(8,128)(2,1)} %bitcast.88, bf16[1024,128]{1,0:T(8,128)(2,1)} %copy-done.4, f32[112,64]{1,0:T(8,128)} %copy.22.w_ref, s32[1,1024]{1,0:T(1,128)} %bitcast.95), custom_call_target="tpu_custom_call" | custom-call | tf_op jit(solution)/shard_map/first_pass/pallas_call | solution.py:174
  156.4 24.3 %second_pass.1 = (f32[7168,128]{1,0:T(8,128)}, f32[14,8,512]{2,1,0:T(8,128)}, f32[128,1024]{1,0:T(8,128)}) custom-call(f32[7168,1024]{1,0:T(8,128)} %get-tuple-element.21.sig_ref, bf16[7168,1024]{1,0:T(8,128)(2,1)} %get-tuple-element.22.dev_ref, f32[112,1024]{1,0:T(8,128)} %get-tuple-element.23.prob_ref, f32[112,1]{1,0:T(8,128)} %copy.25.rw_ref, ...), custom_call_target="tpu_custom_call" | custom-call | tf_op jit(solution)/shard_map/second_pass/pallas_call | solution.py:243
  185.8 4.0 %collective-permute-done.26 = f32[2,128,128]{2,1,0:T(8,128)S(1)} collective-permute-done((f32[2,128,128]{2,1,0:T(8,128)S(1)}, f32[2,128,128]{2,1,0:T(8,128)S(1)}, u32[]{:S(2)}, u32[]{:S(2)}) %collective-permute-start.26) | collective-permute-done | bytes 131104 | tf_op jit(solution)/shard_map/ppermute | solution.py:274
  192.0 3.0 %collective-permute-done.27 = f32[1,128,128]{2,1,0:T(8,128)S(1)} collective-permute-done((f32[1,128,128]{2,1,0:T(8,128)S(1)}, f32[1,128,128]{2,1,0:T(8,128)S(1)}, u32[]{:S(2)}, u32[]{:S(2)}) %collective-permute-start.27) | collective-permute-done | bytes 65568 | tf_op jit(solution)/shard_map/ppermute | solution.py:274
  196.0 2.0 collective-permute-start.28
  198.0 1.9 collective-permute-start.30
  201.7 2.7 %collective-permute-done.29 = f32[32,128]{1,0:T(8,128)S(1)} collective-permute-done((f32[32,128]{1,0:T(8,128)S(1)}, f32[32,128]{1,0:T(8,128)S(1)}, u32[]{:S(2)}, u32[]{:S(2)}) %collective-permute-start.29) | collective-permute-done | bytes 16416 | tf_op jit(solution)/shard_map/ppermute | solution.py:279
  (120 shorter events, 31.7 us)
Async XLA Ops:
  2.2 21.4 %collective-permute-start.12 = (bf16[64,6144]{1,0:T(8,128)(2,1)S(1)}, bf16[64,6144]{1,0:T(8,128)(2,1)S(1)}, u32[]{:S(2)}, u32[]{:S(2)}) collective-permute-start(bf16[64,6144]{1,0:T(8,128)(2,1)S(1)} %get-tuple-element.45), channel_id=1, source_target_pairs={{0,16},{4,20},{8,24},{12,28},{16,0},{20,4},{24,8},{28,12},{1,17},{... | collective-permute-start | bytes 2359304 | tf_op jit(solution)/shard_map/ppermute | solution.py:274
  5.2 20.5 %collective-permute-start.8 = (bf16[64,6144]{1,0:T(8,128)(2,1)S(1)}, bf16[64,6144]{1,0:T(8,128)(2,1)S(1)}, u32[]{:S(2)}, u32[]{:S(2)}) collective-permute-start(bf16[64,6144]{1,0:T(8,128)(2,1)S(1)} %get-tuple-element.45), channel_id=1, source_target_pairs={{0,8},{4,12},{8,0},{12,4},{16,24},{20,28},{24,16},{28,20},{1,9},{5... | collective-permute-start | bytes 2359304 | tf_op jit(solution)/shard_map/ppermute | solution.py:274
  6.7 35.8 %collective-permute-start.11 = (bf16[64,6144]{1,0:T(8,128)(2,1)S(1)}, bf16[64,6144]{1,0:T(8,128)(2,1)}, u32[]{:S(2)}, u32[]{:S(2)}) collective-permute-start(bf16[64,6144]{1,0:T(8,128)(2,1)S(1)} %get-tuple-element.46), channel_id=1, source_target_pairs={{0,16},{4,20},{8,24},{12,28},{16,0},{20,4},{24,8},{28,12},{1,17},{... | collective-permute-start | bytes 2359304 | tf_op jit(solution)/shard_map/ppermute | solution.py:274
  7.2 35.8 %collective-permute-start.7 = (bf16[64,6144]{1,0:T(8,128)(2,1)S(1)}, bf16[64,6144]{1,0:T(8,128)(2,1)}, u32[]{:S(2)}, u32[]{:S(2)}) collective-permute-start(bf16[64,6144]{1,0:T(8,128)(2,1)S(1)} %get-tuple-element.46), channel_id=1, source_target_pairs={{0,8},{4,12},{8,0},{12,4},{16,24},{20,28},{24,16},{28,20},{1,9},{5... | collective-permute-start | bytes 2359304 | tf_op jit(solution)/shard_map/ppermute | solution.py:274
  9.5 33.0 %collective-permute-start.1 = (bf16[256,128]{1,0:T(8,128)(2,1)S(1)}, bf16[256,128]{1,0:T(8,128)(2,1)S(1)}, u32[]{:S(2)}, u32[]{:S(2)}) collective-permute-start(bf16[256,128]{1,0:T(8,128)(2,1)S(1)} %pad_maximum_fusion.3), channel_id=1, source_target_pairs={{0,8},{4,12},{8,0},{12,4},{16,24},{20,28},{24,16},{28,20},{1,9},{5... | collective-permute-start | bytes 196616 | tf_op jit(solution)/shard_map/ppermute | solution.py:274
  23.6 21.7 %collective-permute-start.14 = (bf16[64,6144]{1,0:T(8,128)(2,1)S(1)}, bf16[64,6144]{1,0:T(8,128)(2,1)}, u32[]{:S(2)}, u32[]{:S(2)}) collective-permute-start(bf16[64,6144]{1,0:T(8,128)(2,1)S(1)} %collective-permute-done.12.refs_5_), channel_id=1, source_target_pairs={{0,4},{4,0},{8,12},{12,8},{16,20},{20,16},{24,28},{28,24},{1,5},{5... | collective-permute-start | bytes 2359304 | tf_op jit(solution)/shard_map/ppermute | solution.py:274
  25.7 30.9 %collective-permute-start.19 = (bf16[64,6144]{1,0:T(8,128)(2,1)S(1)}, bf16[64,6144]{1,0:T(8,128)(2,1)}, u32[]{:S(2)}, u32[]{:S(2)}) collective-permute-start(bf16[64,6144]{1,0:T(8,128)(2,1)S(1)} %collective-permute-done.8.refs_1_), channel_id=1, source_target_pairs={{0,16},{4,20},{8,24},{12,28},{16,0},{20,4},{24,8},{28,12},{1,17},{... | collective-permute-start | bytes 2359304 | tf_op jit(solution)/shard_map/ppermute | solution.py:274
  42.5 22.4 %collective-permute-start.3 = (bf16[128,6144]{1,0:T(8,128)(2,1)}, bf16[128,6144]{1,0:T(8,128)(2,1)S(1)}, u32[]{:S(2)}, u32[]{:S(2)}) collective-permute-start(bf16[128,6144]{1,0:T(8,128)(2,1)} %refs_0_.1), channel_id=1, source_target_pairs={{0,4},{4,0},{8,12},{12,8},{16,20},{20,16},{24,28},{28,24},{1,5},{5... | collective-permute-start | bytes 4718600 | tf_op jit(solution)/shard_map/ppermute | solution.py:274
  42.5 14.1 %collective-permute-start.10 = (bf16[64,6144]{1,0:T(8,128)(2,1)S(1)}, bf16[64,6144]{1,0:T(8,128)(2,1)}, u32[]{:S(2)}, u32[]{:S(2)}) collective-permute-start(bf16[64,6144]{1,0:T(8,128)(2,1)S(1)} %collective-permute-done.8.refs_1_), channel_id=1, source_target_pairs={{0,4},{4,0},{8,12},{12,8},{16,20},{20,16},{24,28},{28,24},{1,5},{5... | collective-permute-start | bytes 2359304 | tf_op jit(solution)/shard_map/ppermute | solution.py:274
  43.0 19.8 %collective-permute-start.18 = (bf16[64,6144]{1,0:T(8,128)(2,1)}, bf16[64,6144]{1,0:T(8,128)(2,1)}, u32[]{:S(2)}, u32[]{:S(2)}) collective-permute-start(bf16[64,6144]{1,0:T(8,128)(2,1)} %collective-permute-done.11.refs_4_), channel_id=1, source_target_pairs={{0,8},{4,12},{8,0},{12,4},{16,24},{20,28},{24,16},{28,20},{1,9},{5... | collective-permute-start | bytes 2359304 | tf_op jit(solution)/shard_map/ppermute | solution.py:274
  45.3 37.7 %collective-permute-start.13 = (bf16[64,6144]{1,0:T(8,128)(2,1)}, bf16[64,6144]{1,0:T(8,128)(2,1)}, u32[]{:S(2)}, u32[]{:S(2)}) collective-permute-start(bf16[64,6144]{1,0:T(8,128)(2,1)} %collective-permute-done.11.refs_4_), channel_id=1, source_target_pairs={{0,4},{4,0},{8,12},{12,8},{16,20},{20,16},{24,28},{28,24},{1,5},{5... | collective-permute-start | bytes 2359304 | tf_op jit(solution)/shard_map/ppermute | solution.py:274
  56.6 28.7 %collective-permute-start.9 = (bf16[64,6144]{1,0:T(8,128)(2,1)}, bf16[64,6144]{1,0:T(8,128)(2,1)}, u32[]{:S(2)}, u32[]{:S(2)}) collective-permute-start(bf16[64,6144]{1,0:T(8,128)(2,1)} %collective-permute-done.7.refs_0_), channel_id=1, source_target_pairs={{0,4},{4,0},{8,12},{12,8},{16,20},{20,16},{24,28},{28,24},{1,5},{5... | collective-permute-start | bytes 2359304 | tf_op jit(solution)/shard_map/ppermute | solution.py:274
  56.6 47.9 %collective-permute-start.21 = (bf16[64,6144]{1,0:T(8,128)(2,1)}, bf16[64,6144]{1,0:T(8,128)(2,1)}, u32[]{:S(2)}, u32[]{:S(2)}) collective-permute-start(bf16[64,6144]{1,0:T(8,128)(2,1)} %collective-permute-done.19.refs_1_), channel_id=1, source_target_pairs={{0,4},{4,0},{8,12},{12,8},{16,20},{20,16},{24,28},{28,24},{1,5},{5... | collective-permute-start | bytes 2359304 | tf_op jit(solution)/shard_map/ppermute | solution.py:274
  62.8 42.1 %collective-permute-start.20 = (bf16[64,6144]{1,0:T(8,128)(2,1)}, bf16[64,6144]{1,0:T(8,128)(2,1)}, u32[]{:S(2)}, u32[]{:S(2)}) collective-permute-start(bf16[64,6144]{1,0:T(8,128)(2,1)} %collective-permute-done.18.refs_0_), channel_id=1, source_target_pairs={{0,4},{4,0},{8,12},{12,8},{16,20},{20,16},{24,28},{28,24},{1,5},{5... | collective-permute-start | bytes 2359304 | tf_op jit(solution)/shard_map/ppermute | solution.py:274
  64.9 35.7 %collective-permute-start.2 = (bf16[512,128]{1,0:T(8,128)(2,1)}, bf16[512,128]{1,0:T(8,128)(2,1)}, u32[]{:S(2)}, u32[]{:S(2)}) collective-permute-start(bf16[512,128]{1,0:T(8,128)(2,1)} %pad_maximum_fusion.1), channel_id=1, source_target_pairs={{0,16},{4,20},{8,24},{12,28},{16,0},{20,4},{24,8},{28,12},{1,17},{... | collective-permute-start | bytes 393224 | tf_op jit(solution)/shard_map/ppermute | solution.py:274
  83.0 18.7 %collective-permute-start.4 = (f32[112,256]{1,0:T(8,128)}, f32[112,256]{1,0:T(8,128)S(1)}, u32[]{:S(2)}, u32[]{:S(2)}) collective-permute-start(f32[112,256]{1,0:T(8,128)} %get-tuple-element.25), channel_id=1, source_target_pairs={{0,1},{1,2},{2,3},{3,0},{4,5},{5,6},{6,7},{7,4},{8,9},{9,10},{10,1... | collective-permute-start | bytes 344072 | tf_op jit(solution)/shard_map/ppermute | solution.py:279
  94.5 29.7 %collective-permute-start.15 = (f32[112,512]{1,0:T(8,128)}, f32[112,512]{1,0:T(8,128)S(1)}, u32[]{:S(2)}, u32[]{:S(2)}) collective-permute-start(f32[112,512]{1,0:T(8,128)} %get-tuple-element.29), channel_id=1, source_target_pairs={{0,1},{1,2},{2,3},{3,0},{4,5},{5,6},{6,7},{7,4},{8,9},{9,10},{10,1... | collective-permute-start | bytes 688136 | tf_op jit(solution)/shard_map/ppermute | solution.py:279
  100.5 13.5 %collective-permute-start.5 = (f32[112,256]{1,0:T(8,128)}, f32[112,256]{1,0:T(8,128)S(1)}, u32[]{:S(2)}, u32[]{:S(2)}) collective-permute-start(f32[112,256]{1,0:T(8,128)} %get-tuple-element.26), channel_id=1, source_target_pairs={{0,2},{1,3},{2,0},{3,1},{4,6},{5,7},{6,4},{7,5},{8,10},{9,11},{10,... | collective-permute-start | bytes 344072 | tf_op jit(solution)/shard_map/ppermute | solution.py:279
  101.7 19.2 %collective-permute-start.6 = (f32[112,256]{1,0:T(8,128)}, f32[112,256]{1,0:T(8,128)S(1)}, u32[]{:S(2)}, u32[]{:S(2)}) collective-permute-start(f32[112,256]{1,0:T(8,128)} %get-tuple-element.27), channel_id=1, source_target_pairs={{0,3},{1,0},{2,1},{3,2},{4,7},{5,4},{6,5},{7,6},{8,11},{9,8},{10,9... | collective-permute-start | bytes 344072 | tf_op jit(solution)/shard_map/ppermute | solution.py:279
  104.5 50.9 %collective-permute-start.16 = (f32[112,512]{1,0:T(8,128)}, f32[112,512]{1,0:T(8,128)S(1)}, u32[]{:S(2)}, u32[]{:S(2)}) collective-permute-start(f32[112,512]{1,0:T(8,128)} %get-tuple-element.30), channel_id=1, source_target_pairs={{0,2},{1,3},{2,0},{3,1},{4,6},{5,7},{6,4},{7,5},{8,10},{9,11},{10,... | collective-permute-start | bytes 688136 | tf_op jit(solution)/shard_map/ppermute | solution.py:279
  104.9 50.6 %collective-permute-start.17 = (f32[112,512]{1,0:T(8,128)S(1)}, f32[112,512]{1,0:T(8,128)S(1)}, u32[]{:S(2)}, u32[]{:S(2)}) collective-permute-start(f32[112,512]{1,0:T(8,128)S(1)} %copy-done.21), channel_id=1, source_target_pairs={{0,3},{1,0},{2,1},{3,2},{4,7},{5,4},{6,5},{7,6},{8,11},{9,8},{10,9... | collective-permute-start | bytes 688136 | tf_op jit(solution)/shard_map/ppermute | solution.py:279
  114.0 41.5 %collective-permute-start.22 = (f32[112,256]{1,0:T(8,128)}, f32[112,256]{1,0:T(8,128)S(1)}, u32[]{:S(2)}, u32[]{:S(2)}) collective-permute-start(f32[112,256]{1,0:T(8,128)} %get-tuple-element.33), channel_id=1, source_target_pairs={{0,1},{1,2},{2,3},{3,0},{4,5},{5,6},{6,7},{7,4},{8,9},{9,10},{10,1... | collective-permute-start | bytes 344072 | tf_op jit(solution)/shard_map/ppermute | solution.py:279
  120.9 34.6 %collective-permute-start.23 = (f32[112,256]{1,0:T(8,128)}, f32[112,256]{1,0:T(8,128)S(1)}, u32[]{:S(2)}, u32[]{:S(2)}) collective-permute-start(f32[112,256]{1,0:T(8,128)} %get-tuple-element.34), channel_id=1, source_target_pairs={{0,2},{1,3},{2,0},{3,1},{4,6},{5,7},{6,4},{7,5},{8,10},{9,11},{10,... | collective-permute-start | bytes 344072 | tf_op jit(solution)/shard_map/ppermute | solution.py:279
  124.2 31.3 %collective-permute-start.24 = (f32[112,256]{1,0:T(8,128)}, f32[112,256]{1,0:T(8,128)S(1)}, u32[]{:S(2)}, u32[]{:S(2)}) collective-permute-start(f32[112,256]{1,0:T(8,128)} %get-tuple-element.35), channel_id=1, source_target_pairs={{0,3},{1,0},{2,1},{3,2},{4,7},{5,4},{6,5},{7,6},{8,11},{9,8},{10,9... | collective-permute-start | bytes 344072 | tf_op jit(solution)/shard_map/ppermute | solution.py:279
  (29 other events, 553.9 us)

commit v2 on v0

v2 whole, which is shorter than its diff:
```python
import functools
import math

import jax
import jax.numpy as jnp
from jax import lax
from jax.experimental import pallas as pl
from jax.experimental.pallas import tpu as pltpu
from jax.sharding import PartitionSpec as P

LOG2E = math.log2(math.e)
LN2 = math.log(2.0)
TOP = 120.0
VMEM_BYTES = 56 * 1024 * 1024
BF = jnp.bfloat16
F32 = jnp.float32


SHORT = pl.CostEstimate(flops=0, transcendentals=0, bytes_accessed=1024)


def prep_kernel(width, step_heads, root, q_ref, ln_ref, out_ref):
    heads, rows = ln_ref.shape
    pad, lanes = 256, 128
    cols = step_heads * lanes
    scaled = -root * ln_ref[...]
    high = scaled.astype(BF).astype(F32)
    mid = (scaled - high).astype(BF).astype(F32)
    low = (scaled - high - mid).astype(BF).astype(F32)
    terms = jnp.concatenate([high, mid, low], axis=0).astype(BF)
    column = lax.broadcasted_iota(jnp.int32, (3 * heads, cols), 1)
    source = lax.broadcasted_iota(jnp.int32, (3 * heads, cols), 0)
    head = source % heads - pl.program_id(0) * step_heads
    spare = jnp.where(head % 2 == 0, width - lanes, 0) + source // heads
    place = jnp.where(column == head * lanes + spare, 1.0, 0.0).astype(BF)
    extra = lax.dot_general(
        terms, place, (((0,), (0,)), ((), ())), preferred_element_type=F32
    ).astype(BF)
    lane = lax.broadcasted_iota(jnp.int32, (rows, lanes), 1)
    for h in range(step_heads):
        odd = h % 2
        first = (h // 2) * 2 * width + odd * (2 * width - pad)
        at = h * pad
        kept = lane >= pad - width if odd else lane < width - lanes
        mixed, plain = (0, lanes) if odd else (lanes, 0)
        out_ref[:, at + plain : at + plain + lanes] = q_ref[:, first + plain : first + plain + lanes]
        out_ref[:, at + mixed : at + mixed + lanes] = jnp.where(
            kept, q_ref[:, first + mixed : first + mixed + lanes], extra[:, h * lanes : (h + 1) * lanes]
        )


def prep(main_q, norms_turned, width, step_heads=8):
    rows = main_q.shape[0]
    heads = norms_turned.shape[0]
    return pl.pallas_call(
        functools.partial(prep_kernel, width, step_heads, math.sqrt(width)),
        grid=(heads // step_heads,),
        in_specs=[
            pl.BlockSpec((rows, step_heads * width), lambda i: (0, i)),
            pl.BlockSpec((heads, rows), lambda i: (0, 0)),
        ],
        out_specs=pl.BlockSpec((rows, step_heads * 256), lambda i: (0, i)),
        out_shape=jax.ShapeDtypeStruct((rows, heads * 256), BF),
        compiler_params=pltpu.CompilerParams(vmem_limit_bytes=VMEM_BYTES),
        cost_estimate=SHORT,
        name="prep",
    )(main_q, norms_turned)


def mass_kernel(width, step_heads, n_keys, ranks, pos_ref, kpos_ref, qa_hbm, *refs):
    key_hbm, out_refs = refs[:n_keys], refs[n_keys : n_keys + ranks]
    qa_ref, keys_ref, total_ref, q_sems, k_sems = refs[n_keys + ranks :]
    pad = 256
    factor = LOG2E / math.sqrt(width)
    rows, total = total_ref.shape
    steps = qa_ref.shape[1] // (step_heads * pad)
    copies = []
    for i in range(steps):
        cols = pl.ds(i * step_heads * pad, step_heads * pad)
        group = [pltpu.make_async_copy(qa_hbm.at[:, cols], qa_ref.at[:, cols], q_sems.at[i])]
        cols = pl.ds(i * step_heads * width, step_heads * width)
        first = 0
        for n, k in enumerate(key_hbm):
            at = pl.ds(first, k.shape[0])
            group.append(pltpu.make_async_copy(k.at[:, cols], keys_ref.at[at, cols], k_sems.at[i, n]))
            first += k.shape[0]
        for copy in group:
            copy.start()
        copies.append(group)
    lane = lax.broadcasted_iota(jnp.int32, (total, pad), 1)
    ones_even = jnp.where((lane >= width) & (lane < width + 3), 1.0, 0.0).astype(BF)
    ones_odd = jnp.where(lane < 3, 1.0, 0.0).astype(BF)
    keep_even = jnp.where(lane < width, 1.0, 0.0).astype(BF)
    keep_odd = jnp.where(lane >= pad - width, 1.0, 0.0).astype(BF)

    def one(h):
        first = (h // 2) * 2 * width + (h % 2) * (2 * width - pad)
        keys = keys_ref[:, first : first + pad]
        keys = keys * keep_odd + ones_odd if h % 2 else keys * keep_even + ones_even
        scores = lax.dot_general(
            qa_ref[:, h * pad : (h + 1) * pad], keys, (((1,), (1,)), ((), ())), preferred_element_type=F32
        )
        return jnp.exp2(scores * factor)

    for i in range(steps):
        for copy in copies[i]:
            copy.wait()
        for h in range(i * step_heads, (i + 1) * step_heads, 2):
            both = one(h) + one(h + 1)
            total_ref[...] = both if h == 0 else total_ref[...] + both

    own = rows // ranks
    for k in range(ranks):
        first = lax.rem(pos_ref[1] + k, ranks) * own
        row = pos_ref[0] + first + lax.broadcasted_iota(jnp.int32, out_refs[k].shape, 0)
        mine = total_ref[pl.ds(pl.multiple_of(first, 8), own), :]
        out_refs[k][...] = jnp.where(kpos_ref[...] <= row, mine, 0.0)


def mass(places, qa, kpos, key_list, width, ranks, step_heads=8):
    rows = qa.shape[0]
    heads = qa.shape[1] // 256
    total = sum(k.shape[0] for k in key_list)
    own = rows // ranks
    steps = heads // step_heads
    vmem = pl.BlockSpec(memory_space=pltpu.VMEM)
    return pl.pallas_call(
        functools.partial(mass_kernel, width, step_heads, len(key_list), ranks),
        in_specs=[pl.BlockSpec(memory_space=pltpu.SMEM), vmem]
        + [pl.BlockSpec(memory_space=pl.ANY)] * (1 + len(key_list)),
        out_specs=[vmem] * ranks,
        out_shape=[jax.ShapeDtypeStruct((own, total), F32)] * ranks,
        scratch_shapes=[
            pltpu.VMEM(qa.shape, BF),
            pltpu.VMEM((total, heads * width), BF),
            pltpu.VMEM((rows, total), F32),
            pltpu.SemaphoreType.DMA((steps,)),
            pltpu.SemaphoreType.DMA((steps, len(key_list))),
        ],
        compiler_params=pltpu.CompilerParams(vmem_limit_bytes=VMEM_BYTES),
        cost_estimate=SHORT,
        name="mass",
    )(places, kpos, qa, *key_list)


def in_pairs(steps, load, work, finish):
    pairs = (steps - 1) // 2
    load(0, 0)

    def two(p, _):
        first = 2 * p
        finish(first, 2)
        load(first + 1, 1)
        work(first, 0)
        load(first + 2, 0)
        work(first + 1, 1)
        return 0

    lax.fori_loop(0, pairs, two, 0)
    last = 2 * pairs
    if steps % 2 == 0:
        finish(last, 2)
        load(last + 1, 1)
        work(last, 0)
        work(last + 1, 1)
    else:
        finish(last, 1)
        work(last, 0)


def tile_of(i, size):
    return pl.ds(i * size if isinstance(i, int) else pl.multiple_of(i * size, size), size)


def first_kernel(rows, scale, pos_ref, q_ref, key_ref, w_ref, kpos_ref, power_hbm, prob_ref, raw_0, raw_1, ring, sems):
    keys = key_ref.shape[0]
    own, heads = w_ref.shape
    span = rows * heads
    steps = own // rows
    raws = (raw_0, raw_1)
    slots = ring.shape[0]

    def copy_out(i):
        slot = i % slots if isinstance(i, int) else lax.rem(i, slots)
        return pltpu.make_async_copy(ring.at[slot], power_hbm.at[tile_of(i, span), :], sems.at[slot])

    def multiply(i, slot):
        raws[slot][...] = lax.dot_general(
            q_ref[tile_of(i, span), :], key_ref[...], (((1,), (1,)), ((), ())), preferred_element_type=F32
        )

    def finish(i, count):
        for n in range(count):
            if isinstance(i, int):
                if i + n >= slots:
                    copy_out(i + n - slots).wait()
            else:

                @pl.when(i + n >= slots)
                def _():
                    copy_out(i + n - slots).wait()

    def elements(i, slot):
        raw = raws[slot]
        where = i % slots if isinstance(i, int) else lax.rem(i, slots)
        w_turned = jnp.transpose(w_ref[tile_of(i, rows), :]) * LN2
        logits = []
        for t in range(rows):
            w = w_turned[:, t : t + 1]
            parts = []
            for c in range(keys // 128):
                at = (slice(t * heads, (t + 1) * heads), slice(c * 128, (c + 1) * 128))
                u = raw[at] * (scale * LOG2E)
                power = jnp.exp2(jnp.minimum(u, TOP))
                ring[(where, *at)] = power
                soft = jnp.maximum(u, jnp.log2(1.0 + power))
                parts.append(jnp.sum(w * soft, axis=0, keepdims=True))
            logits.append(jnp.concatenate(parts, axis=1))
        prob_ref[tile_of(i, rows), :] = jnp.concatenate(logits, axis=0)
        copy_out(i).start()

    in_pairs(steps, multiply, elements, finish)
    row = pos_ref[0] + lax.broadcasted_iota(jnp.int32, prob_ref.shape, 0)
    masked = jnp.where(kpos_ref[...] <= row, prob_ref[...], -jnp.inf)
    top = jnp.max(masked, axis=1, keepdims=True)
    terms = jnp.exp2((masked - top) * LOG2E)
    prob_ref[...] = terms / jnp.sum(terms, axis=1, keepdims=True)
    for i in range(max(steps - slots, 0), steps):
        copy_out(i).wait()


def first_pass(own_pos, q_flat, keys, weights, kpos, rows=8, slots=4):
    total, width = q_flat.shape
    key_total = keys.shape[0]
    own, heads = weights.shape
    tile = rows * heads
    vmem = pl.BlockSpec(memory_space=pltpu.VMEM)
    return pl.pallas_call(
        functools.partial(first_kernel, rows, 1.0 / math.sqrt(width)),
        in_specs=[pl.BlockSpec(memory_space=pltpu.SMEM), vmem, vmem, vmem, vmem],
        out_specs=[pl.BlockSpec(memory_space=pl.ANY), vmem],
        out_shape=[
            jax.ShapeDtypeStruct((total, key_total), F32),
            jax.ShapeDtypeStruct((own, key_total), F32),
        ],
        scratch_shapes=[
            pltpu.VMEM((tile, key_total), F32),
            pltpu.VMEM((tile, key_total), F32),
            pltpu.VMEM((slots, tile, key_total), F32),
            pltpu.SemaphoreType.DMA((slots,)),
        ],
        compiler_params=pltpu.CompilerParams(vmem_limit_bytes=VMEM_BYTES),
        cost_estimate=SHORT,
        name="first_pass",
    )(own_pos, q_flat, keys, weights, kpos)


def second_kernel(rows, splits, cuts, columns, scale, big_ref, rw_ref, w_ref, key_ref, qt_ref, *refs):
    powers, probs, refs = refs[:cuts], refs[cuts : 2 * cuts], refs[2 * cuts :]
    count = sum(splits)
    parts, refs = refs[:count], refs[count:]
    gq_hbm, gw_ref, mine_ref, theirs_ref, power_ref, out_ref, coef_ref, grad_0, grad_1, sems, out_sems = refs
    grads = (grad_0, grad_1)
    keys = key_ref.shape[0]
    own, heads = w_ref.shape
    tile = rows * heads
    steps = own // rows
    lane = lax.broadcasted_iota(jnp.int32, (heads, 128), 1)

    def copy_in(i, source=powers[0], first=0):
        return pltpu.make_async_copy(source.at[tile_of(first, tile), :], power_ref.at[tile_of(i, tile), :], sems.at[i])

    def copy_out(i):
        at = tile_of(i, tile)
        return pltpu.make_async_copy(out_ref.at[at, :], gq_hbm.at[at, :], out_sems.at[i])

    done = 0
    for source in powers:
        count = source.shape[0] // tile
        for i in range(count):
            copy_in(done + i, source, i).start()
        done += count
    groups = []
    for size in splits:
        groups.append(sum(r[...] for r in parts[:size]))
        parts = parts[size:]
    span = keys // len(columns)
    mass_rows = jnp.concatenate([groups[g][:, n * span : (n + 1) * span] for g, n in columns], axis=1)
    target = mass_rows / jnp.sum(mass_rows, axis=1, keepdims=True)
    coef_ref[...] = rw_ref[...] * (jnp.concatenate([r[...] for r in probs], axis=0) - target)
    mine_ref[...] = jnp.zeros_like(mine_ref)
    theirs_ref[...] = jnp.zeros_like(theirs_ref)
    side = keys // 2

    def lanes_of(columns):
        block = jnp.zeros((heads, 128), F32)
        for t, column in enumerate(columns):
            block = jnp.where(lane == t, column, block)
        return jnp.transpose(block)[:rows, :]

    def elements(i, slot):
        coef = coef_ref[tile_of(i, rows), :]
        w_turned = jnp.transpose(w_ref[tile_of(i, rows), :]) * scale
        columns = []
        for t in range(rows):
            w = w_turned[:, t : t + 1]
            total = jnp.zeros((heads, 128), F32)
            from_row = tile_of(i * rows + t, heads)
            for c in range(keys // 128):
                cols = slice(c * 128, (c + 1) * 128)
                row = coef[t : t + 1, cols]
                power = power_ref[from_row, cols]
                up = 1.0 + power
                grads[slot][t * heads : (t + 1) * heads, cols] = (
                    power * pl.reciprocal(up, approx=False) * (row * w)
                ).astype(BF)
                total = total + jnp.log2(up) * row
            columns.append(jnp.sum(total, axis=1, keepdims=True))
        gw_ref[tile_of(i, rows), :] = lanes_of(columns) * LN2

    def multiply(i, slot):
        block = grads[slot][...]
        at = tile_of(i, tile)
        out_ref[at, :] = jnp.dot(block, key_ref[...], preferred_element_type=F32)
        mine_ref[...] += jnp.dot(qt_ref[:, at], block[:, :side], preferred_element_type=F32)
        theirs_ref[...] += jnp.dot(qt_ref[:, at], block[:, side:], preferred_element_type=F32)

    def finish(i, number):
        for n in range(1, number + 1):
            if isinstance(i, int):
                if i + n < steps:
                    copy_in(i + n).wait()
            else:
                copy_in(i + n).wait()

    copy_in(0).wait()
    in_pairs(steps, elements, multiply, finish)
    for i in range(steps):
        copy_out(i).start()

    @pl.when(big_ref[0] > 0)
    def _():
        def past_top(i, _):
            raw = lax.dot_general(
                qt_ref[:, tile_of(i, tile)], key_ref[...], (((0,), (1,)), ((), ())), preferred_element_type=F32
            )
            over = jnp.maximum(raw * (scale * LOG2E) - TOP, 0.0)
            coef = coef_ref[tile_of(i, rows), :]
            columns = [
                jnp.sum(over[t * heads : (t + 1) * heads, :] * coef[t : t + 1, :], axis=1, keepdims=True)
                for t in range(rows)
            ]
            gw_ref[tile_of(i, rows), :] += lanes_of(columns) * LN2
            return 0

        lax.fori_loop(0, steps, past_top, 0)

    for i in range(steps):
        copy_out(i).wait()


def may_pass_top(q_flat, keys):
    q_most = jnp.max(jnp.sum(jnp.square(q_flat.astype(F32)), axis=1))
    k_most = jnp.max(jnp.sum(jnp.square(keys.astype(F32)), axis=1))
    bound = q_most * k_most * (LOG2E * LOG2E / q_flat.shape[1])
    return (bound > (TOP - 1.0) ** 2).astype(jnp.int32).reshape(1)


def second_pass(big, powers, probs, mass_parts, columns, row_weight, weights, keys, q_turned, rows=8):
    key_total = keys.shape[0]
    total = q_turned.shape[1]
    own, heads = weights.shape
    tile = rows * heads
    steps = own // rows
    width = keys.shape[1]
    flat = [piece for pieces in mass_parts for piece in pieces]
    vmem = pl.BlockSpec(memory_space=pltpu.VMEM)
    hbm = pl.BlockSpec(memory_space=pl.ANY)
    return pl.pallas_call(
        functools.partial(
            second_kernel,
            rows,
            tuple(len(p) for p in mass_parts),
            len(powers),
            columns,
            1.0 / math.sqrt(width),
        ),
        in_specs=[pl.BlockSpec(memory_space=pltpu.SMEM)]
        + [vmem] * 4
        + [hbm] * len(powers)
        + [vmem] * (len(probs) + len(flat)),
        out_specs=[hbm, vmem, vmem, vmem],
        out_shape=[
            jax.ShapeDtypeStruct((total, width), F32),
            jax.ShapeDtypeStruct((own, heads), F32),
            jax.ShapeDtypeStruct((width, key_total // 2), F32),
            jax.ShapeDtypeStruct((width, key_total // 2), F32),
        ],
        scratch_shapes=[
            pltpu.VMEM((total, key_total), F32),
            pltpu.VMEM((total, width), F32),
            pltpu.VMEM((own, key_total), F32),
            pltpu.VMEM((tile, key_total), BF),
            pltpu.VMEM((tile, key_total), BF),
            pltpu.SemaphoreType.DMA((steps,)),
            pltpu.SemaphoreType.DMA((steps,)),
        ],
        compiler_params=pltpu.CompilerParams(vmem_limit_bytes=VMEM_BYTES),
        cost_estimate=SHORT,
        name="second_pass",
    )(big, row_weight, weights, keys, q_turned, *powers, *probs, *flat)


def swap(x, bit):
    size = lax.axis_size("ctx")
    return lax.ppermute(x, "ctx", [(i, i ^ bit) for i in range(size)])


def turn(x, steps):
    size = lax.axis_size("tp")
    return lax.ppermute(x, "tp", [(i, (i + steps) % size) for i in range(size)])


def together(*values):
    return lax.optimization_barrier(values)


def after(x, *others):
    return lax.optimization_barrier((x, *others))[0]


def per_device(main_q, main_k, log_norms, index_q, index_w, index_k, row_weight, offsets, key_map):
    key_rows = main_k.shape[0]
    own_rows, heads, index_width = index_q.shape
    main_heads = log_norms.shape[1]
    width = main_k.shape[1] // main_heads
    places_ctx = lax.axis_size("ctx")
    ranks = lax.axis_size("tp")
    here = lax.axis_index("ctx")
    rank = lax.axis_index("tp")
    far_bits = [b for b in (2**i for i in range(1, places_ctx.bit_length() - 1))]
    sums_of_bits = [sum(b for i, b in enumerate(far_bits) if n >> i & 1) for n in range(1, 2 ** len(far_bits))]
    near_far = [d for d in sums_of_bits if d & (d - 1) == 0]
    rest_far = sorted((d for d in sums_of_bits if d & (d - 1) != 0), key=int.bit_count)

    queries = prep(main_q, log_norms.T, width)
    index_far = [swap(index_k, d) for d in near_far + rest_far]
    main_k, index_k, *index_far = together(main_k, index_k, *index_far)
    keys_at = {0: main_k}
    for d in near_far:
        keys_at[d] = swap(main_k, d)
    keys_at[1] = swap(main_k, 1)
    index_w, row_weight, offsets, key_map, index_q, index_k, queries = together(
        index_w, row_weight, offsets, key_map, index_q, index_k, queries
    )
    index_mine = [index_k] + index_far
    index_theirs = swap(jnp.stack(index_mine), 1)
    far = [0] + near_far + rest_far
    order = far + [d + 1 for d in far]
    blocks = jnp.stack([here ^ d for d in order])
    key_pos = key_map[blocks][:, None] * key_rows + jnp.arange(key_rows, dtype=jnp.int32)[None, :]
    index_keys = jnp.concatenate([*index_mine, index_theirs.reshape(-1, index_width)], axis=0)
    own_pos = (offsets[0] + rank * own_rows).reshape(1).astype(jnp.int32)

    def head_sums(members, parts):
        places = jnp.stack([offsets[0], rank if parts > 1 else 0 * rank]).astype(jnp.int32)
        group_pos = jnp.concatenate([key_pos[order.index(d)] for d in members]).reshape(1, -1)
        return mass(places, queries, group_pos, [keys_at[d] for d in members], width, parts)

    def to_owners(sums):
        return [sums[0]] + [turn(sums[k], k) for k in range(1, ranks)]

    q_flat = index_q.reshape(own_rows * heads, index_width)
    q_turned = q_flat.T
    big = may_pass_top(q_flat, index_keys)
    row_weight = row_weight[:, None]
    tiles = own_rows // 8
    ends = [0, tiles * 5 // 7, tiles]
    powers, probs = [], []

    def index_part(n, *others):
        first, last = ends[n] * 8, ends[n + 1] * 8
        rows = after(q_flat[first * heads : last * heads], *others)
        power, prob = first_pass(own_pos + first, rows, index_keys, index_w[first:last], key_pos.reshape(1, -1))
        powers.append(power)
        probs.append(prob)
        return prob

    group_own = [0, 1]
    group_near = [d + side for d in near_far for side in (0, 1)]
    group_rest = [d + side for d in rest_far for side in (0, 1)]
    groups = [group_own, group_near, group_rest]
    columns = tuple((n, group.index(d)) for d in order for n, group in enumerate(groups) if d in group)

    sums_own = head_sums(group_own, 1)[0]
    part_0 = index_part(0, sums_own)
    sums_own = lax.psum_scatter(sums_own, "tp", scatter_dimension=0, tiled=True)
    part_0, sums_own, *got = together(part_0, sums_own, *[keys_at[d] for d in near_far])
    keys_at.update(zip(near_far, got))
    for d in rest_far:
        lowest, highest = d & -d, 1 << (d.bit_length() - 1)
        source = jnp.where(here % 2 == 0, keys_at[d ^ lowest], keys_at[d ^ highest])
        keys_at[d] = lax.ppermute(
            source, "ctx", [(i, i ^ (highest if i % 2 else lowest)) for i in range(places_ctx)]
        )
    for d in near_far:
        keys_at[d + 1] = swap(keys_at[d], 1)
    sums_near = head_sums(group_near, ranks)
    got = together(sums_near[0], *[keys_at[d] for d in rest_far])
    keys_at.update(zip(rest_far, got[1:]))
    for d in rest_far:
        keys_at[d + 1] = swap(keys_at[d], 1)
    sums_near = to_owners(sums_near)
    sums_rest = head_sums(group_rest, ranks)
    index_part(1, sums_rest[0])
    sums_rest = to_owners(sums_rest)
    grad_q, grad_w, mine, theirs = second_pass(
        big, powers, probs, [[sums_own], sums_near, sums_rest], columns, row_weight, index_w, index_keys, q_turned
    )

    mine = mine + swap(theirs, 1)
    terms = mine[:, :key_rows]
    for n, d in enumerate(far[1:], 1):
        terms = terms + swap(mine[:, n * key_rows : (n + 1) * key_rows], d)
    terms = terms.T.reshape(ranks, key_rows // ranks, index_width)
    grad_k = lax.dynamic_index_in_dim(terms, rank, 0, keepdims=False)
    for k in range(1, ranks):
        grad_k = grad_k + turn(lax.dynamic_index_in_dim(terms, (rank + k) % ranks, 0, keepdims=False), k)
    return (grad_q.reshape(index_q.shape), grad_w, grad_k)


def solution(mesh):
    placed = (
        P("ctx", "tp"),
        P("ctx", "tp"),
        P("ctx", "tp"),
        P(("ctx", "tp"), None, None),
        P(("ctx", "tp"), None),
        P("ctx", None),
        P(("ctx", "tp")),
        P("ctx"),
        P(),
    )
    return jax.shard_map(
        per_device,
        mesh=mesh,
        in_specs=placed,
        out_specs=(P(("ctx", "tp"), None, None), P(("ctx", "tp"), None), P(("ctx", "tp"), None)),
        check_vma=False,
    )
```

time: 310 us -> 177 us (0.57)
  matrix products: 123 us -> 0 us
  waiting for transfers between devices: 125 us -> 29.3 us
  Pallas kernels: 0 us -> 71.3 us
  starting transfers between devices: 0.16 us -> 31.7 us
  local copies, waits for them, and re-layouts: 29.9 us -> 17.3 us
  blocking collectives: 9.45 us -> 0 us
  other arithmetic: 6.68 us -> 10.4 us
    dot_general x20 -> x0, matrix products: 123 us -> none  [the longest x8 67.1 us: raw_scores(): jnp.einsum('tjd,kd->tjk', index_q, key_block, preferred_element_type=jnp....]
    pallas_call x0 -> x7, Pallas kernels: none -> 71.3 us  [the longest x3 23 us: mass(): pl.pallas_call(functools.partial(mass_kernel, width, step_heads, len(key_...]
    all_gather x1 -> x0, waiting for transfers between devices: 68.8 us -> none  [per_device(): lax.all_gather(main_k, 'ctx', axis=0, tiled=True)]
    reduce_scatter x3 -> x1, waiting for transfers between devices: 56.1 us -> 0.01 us  [per_device(): sums_own = lax.psum_scatter(sums_own, 'tp', scatter_dimension=0, tiled=True)]
    ppermute x0 -> x24, starting transfers between devices: none -> 31.6 us  [the longest x14 16.8 us: swap(): return lax.ppermute(x, 'ctx', [(i, i ^ bit) for i in range(size)])]
    ppermute x0 -> x24, waiting for transfers between devices: none -> 29.3 us  [the longest x14 18.5 us: swap(): return lax.ppermute(x, 'ctx', [(i, i ^ bit) for i in range(size)])]
    dynamic_slice x12 -> x0, local copies, waits for them, and re-layouts: 9.67 us -> none  [the longest x4 9.31 us: add_block(): lax.dynamic_slice_in_dim(keys, first_key, block_keys, 0)]
    all_gather x1 -> x0, blocking collectives: 9.45 us -> none  [per_device(): index_keys = lax.all_gather(index_k, 'ctx', axis=0, tiled=True)]
  transfers between devices with their start and end apart: 4 -> 25, of which waited for: 4 -> 13; matrix products, arithmetic and copies ran while one was open for 12% -> 12% of each run, Pallas kernels for 0% -> 28%
where the time goes in v2:
time: 177 us; the launch traced here: 176 us
  Pallas kernels  71.3 us (40%)
  starting transfers between devices  31.7 us (18%)
  waiting for transfers between devices  29.3 us (17%)
  local copies, waits for them, and re-layouts  17.3 us (10%)
  between operations  16.3 us (9%)
  other arithmetic  10.4 us (6%)
    pallas_call x3, Pallas kernels, mass(): pl.pallas_call(functools.partial(mass_kernel, width, step_heads, len(key_...  23 us
    pallas_call x1, Pallas kernels, second_pass(): pl.pallas_call(functools.partial(second_kernel, rows, tuple((len(p) for p...  21.7 us
    pallas_call x2, Pallas kernels, first_pass(): pl.pallas_call(functools.partial(first_kernel, rows, 1.0 / math.sqrt(widt...  19.8 us
    ppermute x14, waiting for transfers between devices, swap(): return lax.ppermute(x, 'ctx', [(i, i ^ bit) for i in range(size)])  18.5 us
    ppermute x14, starting transfers between devices, swap(): return lax.ppermute(x, 'ctx', [(i, i ^ bit) for i in range(size)])  16.8 us
    ppermute x9, starting transfers between devices, turn(): return lax.ppermute(x, 'tp', [(i, (i + steps) % size) for i in range(size)])  13.3 us
    unnamed x49, local copies, waits for them, and re-layouts  7.28 us
    pallas_call x1, Pallas kernels, prep(): pl.pallas_call(functools.partial(prep_kernel, width, step_heads, math.sqr...  6.85 us
  transfers between devices with their start and end apart: 25, of which 13 were waited for; matrix products, arithmetic and copies ran while one was open for 12% of the time, Pallas kernels for 28%

profile of v2, /device:TPU:0, one launch (start us, length us, event | category | flops | bytes accessed | tf_op | source)
XLA Modules:
  0.0 176.3 jit_solution(13356035910999039075)
XLA Ops:
  7.2 3.0 %collective-permute-start = (bf16[128,128]{1,0:T(8,128)(2,1)}, bf16[128,128]{1,0:T(8,128)(2,1)S(1)}, u32[]{:S(2)}, u32[]{:S(2)}) collective-permute-start(bf16[128,128]{1,0:T(8,128)(2,1)} %param.14), channel_id=1, source_target_pairs={{0,8},{4,12},{8,0},{12,4},{16,24},{20,28},{24,16},{28,20},{1,9},{5... | collective-permute-start | bytes 98312 | tf_op jit(solution)/shard_map/ppermute | solution.py:416
  12.3 2.0 %collective-permute-done.1 = bf16[128,128]{1,0:T(8,128)(2,1)S(1)} collective-permute-done((bf16[128,128]{1,0:T(8,128)(2,1)}, bf16[128,128]{1,0:T(8,128)(2,1)S(1)}, u32[]{:S(2)}, u32[]{:S(2)}) %collective-permute-start.1) | collective-permute-done | bytes 32800 | tf_op jit(solution)/shard_map/ppermute | solution.py:416
  14.4 2.4 %collective-permute-done.2 = bf16[128,128]{1,0:T(8,128)(2,1)S(1)} collective-permute-done((bf16[128,128]{1,0:T(8,128)(2,1)}, bf16[128,128]{1,0:T(8,128)(2,1)S(1)}, u32[]{:S(2)}, u32[]{:S(2)}) %collective-permute-start.2) | collective-permute-done | bytes 32800 | tf_op jit(solution)/shard_map/ppermute | solution.py:416
  17.4 6.8 %prep.1.qa_hbm = bf16[448,8192]{1,0:T(8,128)(2,1)} custom-call(bf16[448,6144]{1,0:T(8,128)(2,1)} %q_ref.1, f32[32,448]{1,0:T(8,128)} %bitcast.72), custom_call_target="tpu_custom_call" | custom-call | bytes 1024 | tf_op jit(solution)/shard_map/prep/pallas_call | solution.py:55
  28.7 6.6 %mass.3 = f32[448,256]{1,0:T(8,128)} custom-call(s32[2]{0:T(128)} %pad_add_fusion.3.pos_ref, s32[1,256]{1,0:T(1,128)} %bitcast.77, bf16[448,8192]{1,0:T(8,128)(2,1)} %prep.1.qa_hbm, bf16[128,6144]{1,0:T(8,128)(2,1)} %refs_0_, bf16[128,6144]{1,0:T(8,128)(2,1)} %copy-done.4), custom_call_target="tpu_custom_call" | custom-call | bytes 1024 | tf_op jit(solution)/shard_map/mass/pallas_call | solution.py:127
  40.6 1.6 constant_dynamic-update-slice_fusion.key_ref
  42.1 13.5 %first_pass.2 = (f32[5120,1024]{1,0:T(8,128)}, f32[80,1024]{1,0:T(8,128)}) custom-call(s32[1]{0:T(128)} %bitcast.11.pos_ref, bf16[5120,128]{1,0:T(8,128)(2,1)} %bitcast.64, bf16[1024,128]{1,0:T(8,128)(2,1)} %constant_dynamic-update-slice_fusion.key_ref, f32[80,64]{1,0:T(8,128)} %slice.74.w_ref, s32[1,1024]{1,0:T(1,128)} %bitcast.73), custom_call_target="tpu_custom_call" | custom-call | bytes 1024 | tf_op jit(solution)/shard_map/first_pass/pallas_call | solution.py:238
  55.6 6.5 %collective-permute-done.5.refs_0_ = bf16[128,6144]{1,0:T(8,128)(2,1)S(1)} collective-permute-done((bf16[128,6144]{1,0:T(8,128)(2,1)}, bf16[128,6144]{1,0:T(8,128)(2,1)S(1)}, u32[]{:S(2)}, u32[]{:S(2)}) %collective-permute-start.5) | collective-permute-done | bytes 1572896 | tf_op jit(solution)/shard_map/ppermute | solution.py:416
  63.0 1.6 broadcast_select_fusion
  64.6 1.6 collective-permute-start.9
  69.5 10.0 %mass.4 = (f32[112,512]{1,0:T(8,128)}, f32[112,512]{1,0:T(8,128)}, f32[112,512]{1,0:T(8,128)}, f32[112,512]{1,0:T(8,128)}) custom-call(s32[2]{0:T(128)} %pad_add_fusion.4.pos_ref, s32[1,512]{1,0:T(1,128)} %bitcast.75, bf16[448,8192]{1,0:T(8,128)(2,1)} %prep.1.qa_hbm, bf16[128,6144]{1,0:T(8,128)(2,1)} %copy-done.3, bf16[128,6144]{1,0:T(8,128)(2,1)} %copy-done.6, ...), custom_call_target="tpu_custom_call" | custom-call | bytes 1024 | tf_op jit(solution)/shard_map/mass/pallas_call | solution.py:127
  79.5 5.7 %collective-permute-done.9.refs_0_ = bf16[128,6144]{1,0:T(8,128)(2,1)} collective-permute-done((bf16[128,6144]{1,0:T(8,128)(2,1)S(1)}, bf16[128,6144]{1,0:T(8,128)(2,1)}, u32[]{:S(2)}, u32[]{:S(2)}) %collective-permute-start.9) | collective-permute-done | bytes 1572896 | tf_op jit(solution)/shard_map/ppermute | solution.py:503
  86.7 2.9 %copy.37 = bf16[7168,128]{0,1:T(8,128)(2,1)} copy(bf16[7168,128]{1,0:T(8,128)(2,1)S(1)} %bitcast.62) | data formatting | bytes 3670016 | tf_op jit(solution)/shard_map/reshape | solution.py:473
  90.4 1.6 collective-permute-start.11
  93.6 2.6 %collective-permute-start.12 = (f32[112,512]{1,0:T(8,128)}, f32[112,512]{1,0:T(8,128)S(1)}, u32[]{:S(2)}, u32[]{:S(2)}) collective-permute-start(f32[112,512]{1,0:T(8,128)} %get-tuple-element.62), channel_id=1, source_target_pairs={{0,2},{1,3},{2,0},{3,1},{4,6},{5,7},{6,4},{7,5},{8,10},{9,11},{10,... | collective-permute-start | bytes 688136 | tf_op jit(solution)/shard_map/ppermute | solution.py:421
  99.3 6.5 %mass.5 = (f32[112,256]{1,0:T(8,128)}, f32[112,256]{1,0:T(8,128)}, f32[112,256]{1,0:T(8,128)}, f32[112,256]{1,0:T(8,128)}) custom-call(s32[2]{0:T(128)} %pad_add_fusion.4.pos_ref, s32[1,256]{1,0:T(1,128)} %bitcast.76, bf16[448,8192]{1,0:T(8,128)(2,1)} %prep.1.qa_hbm, bf16[128,6144]{1,0:T(8,128)(2,1)} %collective-permute-done.9.refs_0_, ...), custom_call_target="tpu_custom_call" | custom-call | bytes 1024 | tf_op jit(solution)/shard_map/mass/pallas_call | solution.py:127
  106.9 2.8 %collective-permute-start.16 = (f32[112,256]{1,0:T(8,128)}, f32[112,256]{1,0:T(8,128)S(1)}, u32[]{:S(2)}, u32[]{:S(2)}) collective-permute-start(f32[112,256]{1,0:T(8,128)} %get-tuple-element.66), channel_id=1, source_target_pairs={{0,3},{1,0},{2,1},{3,2},{4,7},{5,4},{6,5},{7,6},{8,11},{9,8},{10,9... | collective-permute-start | bytes 344072 | tf_op jit(solution)/shard_map/ppermute | solution.py:421
  112.7 6.3 %first_pass.3 = (f32[2048,1024]{1,0:T(8,128)}, f32[32,1024]{1,0:T(8,128)}) custom-call(s32[1]{0:T(128)S(6)} %add.103.pos_ref, bf16[2048,128]{1,0:T(8,128)(2,1)} %bitcast.65, bf16[1024,128]{1,0:T(8,128)(2,1)} %constant_dynamic-update-slice_fusion.key_ref, f32[32,64]{1,0:T(8,128)} %slice.75.w_ref, s32[1,1024]{1,0:T(1,128)} %bitcast.74), custom_call_target="tpu_custom_call" | custom-call | bytes 1024 | tf_op jit(solution)/shard_map/first_pass/pallas_call | solution.py:238
  119.1 3.6 %collective-permute-done.15.refs_11_ = f32[112,256]{1,0:T(8,128)S(1)} collective-permute-done((f32[112,256]{1,0:T(8,128)}, f32[112,256]{1,0:T(8,128)S(1)}, u32[]{:S(2)}, u32[]{:S(2)}) %collective-permute-start.15) | collective-permute-done | bytes 114720 | tf_op jit(solution)/shard_map/ppermute | solution.py:421
  123.3 21.7 %second_pass.1 = (f32[7168,128]{1,0:T(8,128)}, f32[112,64]{1,0:T(8,128)}, f32[128,512]{1,0:T(8,128)}, f32[128,512]{1,0:T(8,128)}) custom-call(s32[1]{0:T(128)} %bitcast.6.big_ref, f32[112,1]{1,0:T(8,128)} %copy.40.rw_ref, f32[112,64]{1,0:T(8,128)} %copy-done.8, bf16[1024,128]{1,0:T(8,128)(2,1)} %constant_dynamic-update-slice_fusion.key_ref, ...), custom_call_target="tpu_custom_call" | custom-call | bytes 1024 | tf_op jit(solution)/shard_map/second_pass/pallas_call | solution.py:379
  145.1 1.7 collective-permute-done.17
  147.9 9.2 %collective-permute-start.18 = (f32[128,128]{1,0:T(8,128)S(1)}, f32[128,128]{1,0:T(8,128)S(1)}, u32[]{:S(2)}, u32[]{:S(2)}) collective-permute-start(f32[128,128]{1,0:T(8,128)S(1)} %get-tuple-element.83), channel_id=1, source_target_pairs={{0,8},{4,12},{8,0},{12,4},{16,24},{20,28},{24,16},{28,20},{1,9},{5... | collective-permute-start | bytes 196616 | tf_op jit(solution)/shard_map/ppermute | solution.py:416
  159.5 3.1 %collective-permute-done.19 = f32[128,128]{1,0:T(8,128)S(1)} collective-permute-done((f32[128,128]{1,0:T(8,128)S(1)}, f32[128,128]{1,0:T(8,128)S(1)}, u32[]{:S(2)}, u32[]{:S(2)}) %collective-permute-start.19) | collective-permute-done | bytes 65568 | tf_op jit(solution)/shard_map/ppermute | solution.py:416
  162.8 3.7 %collective-permute-start.23 = (f32[32,128]{1,0:T(8,128)S(1)}, f32[32,128]{1,0:T(8,128)S(1)}, u32[]{:S(2)}, u32[]{:S(2)}) collective-permute-start(f32[32,128]{1,0:T(8,128)S(1)} %get-tuple-element.87), channel_id=1, source_target_pairs={{0,3},{1,0},{2,1},{3,2},{4,7},{5,4},{6,5},{7,6},{8,11},{9,8},{10,9... | collective-permute-start | bytes 49160 | tf_op jit(solution)/shard_map/ppermute | solution.py:421
  (115 shorter events, 33.2 us)
Async XLA Ops:
  7.2 55.3 %reduce-scatter.2.cloned.1.call-start = ((), (), s32[]{:S(2)}) async-start(), calls=%async_computation.1 | async-start | bytes 573440 | tf_op jit(solution)/shard_map/reduce_scatter | solution.py:497
  7.2 5.1 %collective-permute-start = (bf16[128,128]{1,0:T(8,128)(2,1)}, bf16[128,128]{1,0:T(8,128)(2,1)S(1)}, u32[]{:S(2)}, u32[]{:S(2)}) collective-permute-start(bf16[128,128]{1,0:T(8,128)(2,1)} %param.14), channel_id=1, source_target_pairs={{0,8},{4,12},{8,0},{12,4},{16,24},{20,28},{24,16},{28,20},{1,9},{5... | collective-permute-start | bytes 98312 | tf_op jit(solution)/shard_map/ppermute | solution.py:416
  10.2 4.1 %collective-permute-start.1 = (bf16[128,128]{1,0:T(8,128)(2,1)}, bf16[128,128]{1,0:T(8,128)(2,1)S(1)}, u32[]{:S(2)}, u32[]{:S(2)}) collective-permute-start(bf16[128,128]{1,0:T(8,128)(2,1)} %param.14), channel_id=1, source_target_pairs={{0,16},{4,20},{8,24},{12,28},{16,0},{20,4},{24,8},{28,12},{1,17},{... | collective-permute-start | bytes 98312 | tf_op jit(solution)/shard_map/ppermute | solution.py:416
  11.8 5.0 %collective-permute-start.2 = (bf16[128,128]{1,0:T(8,128)(2,1)}, bf16[128,128]{1,0:T(8,128)(2,1)S(1)}, u32[]{:S(2)}, u32[]{:S(2)}) collective-permute-start(bf16[128,128]{1,0:T(8,128)(2,1)} %param.14), channel_id=1, source_target_pairs={{0,24},{4,28},{8,16},{12,20},{16,8},{20,12},{24,0},{28,4},{1,25},{... | collective-permute-start | bytes 98312 | tf_op jit(solution)/shard_map/ppermute | solution.py:416
  16.8 10.8 %collective-permute-start.4 = (bf16[128,6144]{1,0:T(8,128)(2,1)}, bf16[128,6144]{1,0:T(8,128)(2,1)S(1)}, u32[]{:S(2)}, u32[]{:S(2)}) collective-permute-start(bf16[128,6144]{1,0:T(8,128)(2,1)} %refs_0_), channel_id=1, source_target_pairs={{0,4},{4,0},{8,12},{12,8},{16,20},{20,16},{24,28},{28,24},{1,5},{5... | collective-permute-start | bytes 4718600 | tf_op jit(solution)/shard_map/ppermute | solution.py:416
  25.0 37.1 %collective-permute-start.5 = (bf16[128,6144]{1,0:T(8,128)(2,1)}, bf16[128,6144]{1,0:T(8,128)(2,1)S(1)}, u32[]{:S(2)}, u32[]{:S(2)}) collective-permute-start(bf16[128,6144]{1,0:T(8,128)(2,1)} %refs_0_), channel_id=1, source_target_pairs={{0,8},{4,12},{8,0},{12,4},{16,24},{20,28},{24,16},{28,20},{1,9},{5... | collective-permute-start | bytes 4718600 | tf_op jit(solution)/shard_map/ppermute | solution.py:416
  25.6 36.8 %collective-permute-start.6 = (bf16[128,6144]{1,0:T(8,128)(2,1)}, bf16[128,6144]{1,0:T(8,128)(2,1)}, u32[]{:S(2)}, u32[]{:S(2)}) collective-permute-start(bf16[128,6144]{1,0:T(8,128)(2,1)} %refs_0_), channel_id=1, source_target_pairs={{0,16},{4,20},{8,24},{12,28},{16,0},{20,4},{24,8},{28,12},{1,17},{... | collective-permute-start | bytes 4718600 | tf_op jit(solution)/shard_map/ppermute | solution.py:416
  36.0 4.5 %collective-permute-start.3 = (bf16[4,128,128]{2,1,0:T(8,128)(2,1)}, bf16[4,128,128]{2,1,0:T(8,128)(2,1)}, u32[]{:S(2)}, u32[]{:S(2)}) collective-permute-start(bf16[4,128,128]{2,1,0:T(8,128)(2,1)} %pad_maximum_fusion), channel_id=1, source_target_pairs={{0,4},{4,0},{8,12},{12,8},{16,20},{20,16},{24,28},{28,24},{1,5},{5... | collective-permute-start | bytes 393224 | tf_op jit(solution)/shard_map/ppermute | solution.py:416
  62.5 5.0 %collective-permute-start.7 = (bf16[128,6144]{1,0:T(8,128)(2,1)S(1)}, bf16[128,6144]{1,0:T(8,128)(2,1)S(1)}, u32[]{:S(2)}, u32[]{:S(2)}) collective-permute-start(bf16[128,6144]{1,0:T(8,128)(2,1)S(1)} %collective-permute-done.5.refs_0_), channel_id=1, source_target_pairs={{0,4},{4,0},{8,12},{12,8},{16,20},{20,16},{24,28},{28,24},{1,5},{5... | collective-permute-start | bytes 4718600 | tf_op jit(solution)/shard_map/ppermute | solution.py:416
  62.5 5.9 %collective-permute-start.8 = (bf16[128,6144]{1,0:T(8,128)(2,1)}, bf16[128,6144]{1,0:T(8,128)(2,1)S(1)}, u32[]{:S(2)}, u32[]{:S(2)}) collective-permute-start(bf16[128,6144]{1,0:T(8,128)(2,1)} %collective-permute-done.6.refs_2_), channel_id=1, source_target_pairs={{0,4},{4,0},{8,12},{12,8},{16,20},{20,16},{24,28},{28,24},{1,5},{5... | collective-permute-start | bytes 4718600 | tf_op jit(solution)/shard_map/ppermute | solution.py:416
  64.6 20.6 %collective-permute-start.9 = (bf16[128,6144]{1,0:T(8,128)(2,1)S(1)}, bf16[128,6144]{1,0:T(8,128)(2,1)}, u32[]{:S(2)}, u32[]{:S(2)}) collective-permute-start(bf16[128,6144]{1,0:T(8,128)(2,1)S(1)} %broadcast_select_fusion), channel_id=1, source_target_pairs={{0,8},{4,20},{8,0},{12,28},{16,24},{20,4},{24,16},{28,12},{1,9},{5... | collective-permute-start | bytes 4718600 | tf_op jit(solution)/shard_map/ppermute | solution.py:503
  85.2 12.9 %collective-permute-start.10 = (bf16[128,6144]{1,0:T(8,128)(2,1)}, bf16[128,6144]{1,0:T(8,128)(2,1)S(1)}, u32[]{:S(2)}, u32[]{:S(2)}) collective-permute-start(bf16[128,6144]{1,0:T(8,128)(2,1)} %collective-permute-done.9.refs_0_), channel_id=1, source_target_pairs={{0,4},{4,0},{8,12},{12,8},{16,20},{20,16},{24,28},{28,24},{1,5},{5... | collective-permute-start | bytes 4718600 | tf_op jit(solution)/shard_map/ppermute | solution.py:416
  90.4 16.5 %collective-permute-start.11 = (f32[112,512]{1,0:T(8,128)}, f32[112,512]{1,0:T(8,128)}, u32[]{:S(2)}, u32[]{:S(2)}) collective-permute-start(f32[112,512]{1,0:T(8,128)} %get-tuple-element.61), channel_id=1, source_target_pairs={{0,1},{1,2},{2,3},{3,0},{4,5},{5,6},{6,7},{7,4},{8,9},{9,10},{10,1... | collective-permute-start | bytes 688136 | tf_op jit(solution)/shard_map/ppermute | solution.py:421
  93.6 25.4 %collective-permute-start.12 = (f32[112,512]{1,0:T(8,128)}, f32[112,512]{1,0:T(8,128)S(1)}, u32[]{:S(2)}, u32[]{:S(2)}) collective-permute-start(f32[112,512]{1,0:T(8,128)} %get-tuple-element.62), channel_id=1, source_target_pairs={{0,2},{1,3},{2,0},{3,1},{4,6},{5,7},{6,4},{7,5},{8,10},{9,11},{10,... | collective-permute-start | bytes 688136 | tf_op jit(solution)/shard_map/ppermute | solution.py:421
  96.2 22.8 %collective-permute-start.13 = (f32[112,512]{1,0:T(8,128)}, f32[112,512]{1,0:T(8,128)S(1)}, u32[]{:S(2)}, u32[]{:S(2)}) collective-permute-start(f32[112,512]{1,0:T(8,128)} %get-tuple-element.63), channel_id=1, source_target_pairs={{0,3},{1,0},{2,1},{3,2},{4,7},{5,4},{6,5},{7,6},{8,11},{9,8},{10,9... | collective-permute-start | bytes 688136 | tf_op jit(solution)/shard_map/ppermute | solution.py:421
  105.8 13.3 %collective-permute-start.14 = (f32[112,256]{1,0:T(8,128)}, f32[112,256]{1,0:T(8,128)S(1)}, u32[]{:S(2)}, u32[]{:S(2)}) collective-permute-start(f32[112,256]{1,0:T(8,128)} %get-tuple-element.64), channel_id=1, source_target_pairs={{0,1},{1,2},{2,3},{3,0},{4,5},{5,6},{6,7},{7,4},{8,9},{9,10},{10,1... | collective-permute-start | bytes 344072 | tf_op jit(solution)/shard_map/ppermute | solution.py:421
  106.5 16.1 %collective-permute-start.15 = (f32[112,256]{1,0:T(8,128)}, f32[112,256]{1,0:T(8,128)S(1)}, u32[]{:S(2)}, u32[]{:S(2)}) collective-permute-start(f32[112,256]{1,0:T(8,128)} %get-tuple-element.65), channel_id=1, source_target_pairs={{0,2},{1,3},{2,0},{3,1},{4,6},{5,7},{6,4},{7,5},{8,10},{9,11},{10,... | collective-permute-start | bytes 344072 | tf_op jit(solution)/shard_map/ppermute | solution.py:421
  106.9 15.8 %collective-permute-start.16 = (f32[112,256]{1,0:T(8,128)}, f32[112,256]{1,0:T(8,128)S(1)}, u32[]{:S(2)}, u32[]{:S(2)}) collective-permute-start(f32[112,256]{1,0:T(8,128)} %get-tuple-element.66), channel_id=1, source_target_pairs={{0,3},{1,0},{2,1},{3,2},{4,7},{5,4},{6,5},{7,6},{8,11},{9,8},{10,9... | collective-permute-start | bytes 344072 | tf_op jit(solution)/shard_map/ppermute | solution.py:421
  147.9 11.6 %collective-permute-start.18 = (f32[128,128]{1,0:T(8,128)S(1)}, f32[128,128]{1,0:T(8,128)S(1)}, u32[]{:S(2)}, u32[]{:S(2)}) collective-permute-start(f32[128,128]{1,0:T(8,128)S(1)} %get-tuple-element.83), channel_id=1, source_target_pairs={{0,8},{4,12},{8,0},{12,4},{16,24},{20,28},{24,16},{28,20},{1,9},{5... | collective-permute-start | bytes 196616 | tf_op jit(solution)/shard_map/ppermute | solution.py:416
  157.1 5.5 %collective-permute-start.19 = (f32[128,128]{1,0:T(8,128)S(1)}, f32[128,128]{1,0:T(8,128)S(1)}, u32[]{:S(2)}, u32[]{:S(2)}) collective-permute-start(f32[128,128]{1,0:T(8,128)S(1)} %get-tuple-element.85), channel_id=1, source_target_pairs={{0,16},{4,20},{8,24},{12,28},{16,0},{20,4},{24,8},{28,12},{1,17},{... | collective-permute-start | bytes 196616 | tf_op jit(solution)/shard_map/ppermute | solution.py:416
  157.1 5.5 %collective-permute-start.20 = (f32[128,128]{1,0:T(8,128)S(1)}, f32[128,128]{1,0:T(8,128)S(1)}, u32[]{:S(2)}, u32[]{:S(2)}) collective-permute-start(f32[128,128]{1,0:T(8,128)S(1)} %get-tuple-element.84), channel_id=1, source_target_pairs={{0,24},{4,28},{8,16},{12,20},{16,8},{20,12},{24,0},{28,4},{1,25},{... | collective-permute-start | bytes 196616 | tf_op jit(solution)/shard_map/ppermute | solution.py:416
  162.7 5.6 %collective-permute-start.21 = (f32[32,128]{1,0:T(8,128)S(1)}, f32[32,128]{1,0:T(8,128)S(1)}, u32[]{:S(2)}, u32[]{:S(2)}) collective-permute-start(f32[32,128]{1,0:T(8,128)S(1)} %get-tuple-element.86), channel_id=1, source_target_pairs={{0,1},{1,2},{2,3},{3,0},{4,5},{5,6},{6,7},{7,4},{8,9},{9,10},{10,1... | collective-permute-start | bytes 49160 | tf_op jit(solution)/shard_map/ppermute | solution.py:421
  162.7 5.5 %collective-permute-start.22 = (f32[32,128]{1,0:T(8,128)S(1)}, f32[32,128]{1,0:T(8,128)S(1)}, u32[]{:S(2)}, u32[]{:S(2)}) collective-permute-start(f32[32,128]{1,0:T(8,128)S(1)} %get-tuple-element.88), channel_id=1, source_target_pairs={{0,2},{1,3},{2,0},{3,1},{4,6},{5,7},{6,4},{7,5},{8,10},{9,11},{10,... | collective-permute-start | bytes 49160 | tf_op jit(solution)/shard_map/ppermute | solution.py:421
  162.8 6.0 %collective-permute-start.23 = (f32[32,128]{1,0:T(8,128)S(1)}, f32[32,128]{1,0:T(8,128)S(1)}, u32[]{:S(2)}, u32[]{:S(2)}) collective-permute-start(f32[32,128]{1,0:T(8,128)S(1)} %get-tuple-element.87), channel_id=1, source_target_pairs={{0,3},{1,0},{2,1},{3,2},{4,7},{5,4},{6,5},{7,6},{8,11},{9,8},{10,9... | collective-permute-start | bytes 49160 | tf_op jit(solution)/shard_map/ppermute | solution.py:421
  (23 other events, 196.8 us)
Sparse Core Ops, SparseCore 0:
  35.4 22.7 reduce-scatter.1

commit v3 on v2

--- a/solution.py
+++ b/solution.py
@@ -67,7 +67,8 @@
     )(main_q, norms_turned)
 
 
-def mass_kernel(width, step_heads, n_keys, ranks, pos_ref, kpos_ref, qa_hbm, *refs):
+def mass_kernel(width, step_heads, members, ranks, whole, pos_ref, qa_hbm, *refs):
+    n_keys = len(members)
     key_hbm, out_refs = refs[:n_keys], refs[n_keys : n_keys + ranks]
     qa_ref, keys_ref, total_ref, q_sems, k_sems = refs[n_keys + ranks :]
     pad = 256
@@ -84,9 +85,10 @@
             at = pl.ds(first, k.shape[0])
             group.append(pltpu.make_async_copy(k.at[:, cols], keys_ref.at[at, cols], k_sems.at[i, n]))
             first += k.shape[0]
+        copies.append(group)
+    for group in copies[:2]:
         for copy in group:
             copy.start()
-        copies.append(group)
     lane = lax.broadcasted_iota(jnp.int32, (total, pad), 1)
     ones_even = jnp.where((lane >= width) & (lane < width + 3), 1.0, 0.0).astype(BF)
     ones_odd = jnp.where(lane < 3, 1.0, 0.0).astype(BF)
@@ -105,29 +107,38 @@
     for i in range(steps):
         for copy in copies[i]:
             copy.wait()
+        for copy in copies[i + 2] if i + 2 < steps else []:
+            copy.start()
         for h in range(i * step_heads, (i + 1) * step_heads, 2):
             both = one(h) + one(h + 1)
             total_ref[...] = both if h == 0 else total_ref[...] + both
 
     own = rows // ranks
     for k in range(ranks):
-        first = lax.rem(pos_ref[1] + k, ranks) * own
-        row = pos_ref[0] + first + lax.broadcasted_iota(jnp.int32, out_refs[k].shape, 0)
-        mine = total_ref[pl.ds(pl.multiple_of(first, 8), own), :]
-        out_refs[k][...] = jnp.where(kpos_ref[...] <= row, mine, 0.0)
-
-
-def mass(places, qa, kpos, key_list, width, ranks, step_heads=8):
+        first = 0 if whole else lax.rem(pos_ref[1] + k, ranks) * own
+        column = 0
+        for place, keys in zip(members, key_hbm):
+            size = keys.shape[0]
+            shape = (own, size)
+            row = pos_ref[0] + first + lax.broadcasted_iota(jnp.int32, shape, 0)
+            key = pos_ref[2 + place[0]] + place[1] + lax.broadcasted_iota(jnp.int32, shape, 1)
+            mine = total_ref[tile_of(first, 1, own), column : column + size]
+            out_refs[k][:, column : column + size] = jnp.where(key <= row, mine, 0.0)
+            column += size
+
+
+def mass(places, qa, members, key_list, width, ranks, step_heads=8):
     rows = qa.shape[0]
     heads = qa.shape[1] // 256
     total = sum(k.shape[0] for k in key_list)
+    whole = ranks == 1
+    hbm = pl.BlockSpec(memory_space=pltpu.HBM)
     own = rows // ranks
     steps = heads // step_heads
     vmem = pl.BlockSpec(memory_space=pltpu.VMEM)
     return pl.pallas_call(
-        functools.partial(mass_kernel, width, step_heads, len(key_list), ranks),
-        in_specs=[pl.BlockSpec(memory_space=pltpu.SMEM), vmem]
-        + [pl.BlockSpec(memory_space=pl.ANY)] * (1 + len(key_list)),
+        functools.partial(mass_kernel, width, step_heads, tuple(members), ranks, whole),
+        in_specs=[pl.BlockSpec(memory_space=pltpu.SMEM), hbm] + [hbm] * len(key_list),
         out_specs=[vmem] * ranks,
         out_shape=[jax.ShapeDtypeStruct((own, total), F32)] * ranks,
         scratch_shapes=[
@@ -140,7 +151,7 @@
         compiler_params=pltpu.CompilerParams(vmem_limit_bytes=VMEM_BYTES),
         cost_estimate=SHORT,
         name="mass",
-    )(places, kpos, qa, *key_list)
+    )(places, qa, *key_list)
 
 
 def in_pairs(steps, load, work, finish):
@@ -168,11 +179,12 @@
         work(last, 0)
 
 
-def tile_of(i, size):
-    return pl.ds(i * size if isinstance(i, int) else pl.multiple_of(i * size, size), size)
-
-
-def first_kernel(rows, scale, pos_ref, q_ref, key_ref, w_ref, kpos_ref, power_hbm, prob_ref, raw_0, raw_1, ring, sems):
+def tile_of(i, step, size=None):
+    size = step if size is None else size
+    return pl.ds(i * step if isinstance(i, int) else pl.multiple_of(i * step, max(step, 8)), size)
+
+
+def first_kernel(rows, scale, start, pos_ref, q_ref, key_ref, w_ref, power_hbm, prob_ref, most_ref, raw_0, raw_1, logits, ring, sems):
     keys = key_ref.shape[0]
     own, heads = w_ref.shape
     span = rows * heads
@@ -200,28 +212,50 @@
                 def _():
                     copy_out(i + n - slots).wait()
 
-    def elements(i, slot):
+    def elements(capped, i, slot):
         raw = raws[slot]
         where = i % slots if isinstance(i, int) else lax.rem(i, slots)
         w_turned = jnp.transpose(w_ref[tile_of(i, rows), :]) * LN2
-        logits = []
         for t in range(rows):
             w = w_turned[:, t : t + 1]
-            parts = []
             for c in range(keys // 128):
                 at = (slice(t * heads, (t + 1) * heads), slice(c * 128, (c + 1) * 128))
                 u = raw[at] * (scale * LOG2E)
-                power = jnp.exp2(jnp.minimum(u, TOP))
+                power = jnp.exp2(jnp.minimum(u, TOP) if capped else u)
                 ring[(where, *at)] = power
-                soft = jnp.maximum(u, jnp.log2(1.0 + power))
-                parts.append(jnp.sum(w * soft, axis=0, keepdims=True))
-            logits.append(jnp.concatenate(parts, axis=1))
-        prob_ref[tile_of(i, rows), :] = jnp.concatenate(logits, axis=0)
+                soft = jnp.log2(1.0 + power)
+                soft = jnp.maximum(u, soft) if capped else soft
+                logits[slot, t : t + 1, c * 128 : (c + 1) * 128] = jnp.sum(w * soft, axis=0, keepdims=True)
+        prob_ref[tile_of(i, rows), :] = logits[slot]
         copy_out(i).start()
 
-    in_pairs(steps, multiply, elements, finish)
-    row = pos_ref[0] + lax.broadcasted_iota(jnp.int32, prob_ref.shape, 0)
-    masked = jnp.where(kpos_ref[...] <= row, prob_ref[...], -jnp.inf)
+    q_most = jnp.zeros((8, 1), F32)
+    for i in range(steps):
+        part = jnp.sum(jnp.square(q_ref[tile_of(i, span), :].astype(F32)), axis=1, keepdims=True)
+        q_most = jnp.maximum(q_most, jnp.max(part.reshape(-1, 8, 1), axis=0))
+    k_most = jnp.max(jnp.sum(jnp.square(key_ref[...].astype(F32)), axis=1, keepdims=True))
+    most_ref[...] = jnp.broadcast_to(q_most * (k_most * (scale * LOG2E) ** 2), most_ref.shape)
+    past_top = jnp.max(most_ref[...]) > (TOP - 1.0) ** 2
+
+    @pl.when(jnp.logical_not(past_top))
+    def _():
+        in_pairs(steps, multiply, functools.partial(elements, False), finish)
+
+    @pl.when(past_top)
+    def _():
+        in_pairs(steps, multiply, functools.partial(elements, True), finish)
+
+    blocks = pos_ref.shape[0] - 2
+    size = keys // blocks
+    row = pos_ref[0] + pos_ref[1] * start[1] + start[0] + lax.broadcasted_iota(jnp.int32, (own, size), 0)
+    lane = lax.broadcasted_iota(jnp.int32, (own, size), 1)
+    masked = jnp.concatenate(
+        [
+            jnp.where(pos_ref[2 + n] + lane <= row, prob_ref[:, n * size : (n + 1) * size], -jnp.inf)
+            for n in range(blocks)
+        ],
+        axis=1,
+    )
     top = jnp.max(masked, axis=1, keepdims=True)
     terms = jnp.exp2((masked - top) * LOG2E)
     prob_ref[...] = terms / jnp.sum(terms, axis=1, keepdims=True)
@@ -229,34 +263,36 @@
         copy_out(i).wait()
 
 
-def first_pass(own_pos, q_flat, keys, weights, kpos, rows=8, slots=4):
+def first_pass(places, start, q_flat, keys, weights, rows=8, slots=4):
     total, width = q_flat.shape
     key_total = keys.shape[0]
     own, heads = weights.shape
     tile = rows * heads
     vmem = pl.BlockSpec(memory_space=pltpu.VMEM)
     return pl.pallas_call(
-        functools.partial(first_kernel, rows, 1.0 / math.sqrt(width)),
-        in_specs=[pl.BlockSpec(memory_space=pltpu.SMEM), vmem, vmem, vmem, vmem],
-        out_specs=[pl.BlockSpec(memory_space=pl.ANY), vmem],
+        functools.partial(first_kernel, rows, 1.0 / math.sqrt(width), start),
+        in_specs=[pl.BlockSpec(memory_space=pltpu.SMEM), vmem, vmem, vmem],
+        out_specs=[pl.BlockSpec(memory_space=pltpu.HBM), vmem, vmem],
         out_shape=[
             jax.ShapeDtypeStruct((total, key_total), F32),
             jax.ShapeDtypeStruct((own, key_total), F32),
+            jax.ShapeDtypeStruct((8, 128), F32),
         ],
         scratch_shapes=[
             pltpu.VMEM((tile, key_total), F32),
             pltpu.VMEM((tile, key_total), F32),
+            pltpu.VMEM((2, rows, key_total), F32),
             pltpu.VMEM((slots, tile, key_total), F32),
             pltpu.SemaphoreType.DMA((slots,)),
         ],
         compiler_params=pltpu.CompilerParams(vmem_limit_bytes=VMEM_BYTES),
         cost_estimate=SHORT,
         name="first_pass",
-    )(own_pos, q_flat, keys, weights, kpos)
-
-
-def second_kernel(rows, splits, cuts, columns, scale, big_ref, rw_ref, w_ref, key_ref, qt_ref, *refs):
-    powers, probs, refs = refs[:cuts], refs[cuts : 2 * cuts], refs[2 * cuts :]
+    )(places, q_flat, keys, weights)
+
+
+def second_kernel(rows, splits, cuts, columns, scale, rw_ref, w_ref, key_ref, q_ref, *refs):
+    powers, probs, mosts, refs = refs[:cuts], refs[cuts : 2 * cuts], refs[2 * cuts : 3 * cuts], refs[3 * cuts :]
     count = sum(splits)
     parts, refs = refs[:count], refs[count:]
     gq_hbm, gw_ref, mine_ref, theirs_ref, power_ref, out_ref, coef_ref, grad_0, grad_1, sems, out_sems = refs
@@ -274,12 +310,24 @@
         at = tile_of(i, tile)
         return pltpu.make_async_copy(out_ref.at[at, :], gq_hbm.at[at, :], out_sems.at[i])
 
-    done = 0
+    sources = [(source, i) for source in powers for i in range(source.shape[0] // tile)]
+    runs = [0]
     for source in powers:
-        count = source.shape[0] // tile
-        for i in range(count):
-            copy_in(done + i, source, i).start()
-        done += count
+        runs.append(runs[-1] + source.shape[0] // tile)
+
+    def start_in(i):
+        if isinstance(i, int):
+            if i < steps:
+                copy_in(i, *sources[i]).start()
+        else:
+            for source, low, high in zip(powers, runs, runs[1:]):
+
+                @pl.when((i >= low) & (i < high))
+                def _():
+                    copy_in(i, source, i - low).start()
+
+    for i in range(3):
+        start_in(i)
     groups = []
     for size in splits:
         groups.append(sum(r[...] for r in parts[:size]))
@@ -292,16 +340,16 @@
     theirs_ref[...] = jnp.zeros_like(theirs_ref)
     side = keys // 2
 
-    def lanes_of(columns):
-        block = jnp.zeros((heads, 128), F32)
-        for t, column in enumerate(columns):
-            block = jnp.where(lane == t, column, block)
-        return jnp.transpose(block)[:rows, :]
+    def add_column(block, t, values):
+        return jnp.where(lane == t, jnp.sum(values, axis=1, keepdims=True), block)
+
+    def as_rows(block):
+        return jnp.transpose(block)[:rows, :] * LN2
 
     def elements(i, slot):
         coef = coef_ref[tile_of(i, rows), :]
         w_turned = jnp.transpose(w_ref[tile_of(i, rows), :]) * scale
-        columns = []
+        block = jnp.zeros((heads, 128), F32)
         for t in range(rows):
             w = w_turned[:, t : t + 1]
             total = jnp.zeros((heads, 128), F32)
@@ -315,42 +363,41 @@
                     power * pl.reciprocal(up, approx=False) * (row * w)
                 ).astype(BF)
                 total = total + jnp.log2(up) * row
-            columns.append(jnp.sum(total, axis=1, keepdims=True))
-        gw_ref[tile_of(i, rows), :] = lanes_of(columns) * LN2
+            block = add_column(block, t, total)
+        gw_ref[tile_of(i, rows), :] = as_rows(block)
 
     def multiply(i, slot):
         block = grads[slot][...]
         at = tile_of(i, tile)
         out_ref[at, :] = jnp.dot(block, key_ref[...], preferred_element_type=F32)
-        mine_ref[...] += jnp.dot(qt_ref[:, at], block[:, :side], preferred_element_type=F32)
-        theirs_ref[...] += jnp.dot(qt_ref[:, at], block[:, side:], preferred_element_type=F32)
+        turned = jnp.transpose(q_ref[at, :])
+        mine_ref[...] += jnp.dot(turned, block[:, :side], preferred_element_type=F32)
+        theirs_ref[...] += jnp.dot(turned, block[:, side:], preferred_element_type=F32)
+        copy_out(i).start()
 
     def finish(i, number):
         for n in range(1, number + 1):
-            if isinstance(i, int):
-                if i + n < steps:
-                    copy_in(i + n).wait()
-            else:
+            if not isinstance(i, int) or i + n < steps:
                 copy_in(i + n).wait()
+        for n in range(1, number + 1):
+            start_in(i + number + n)
 
     copy_in(0).wait()
     in_pairs(steps, elements, multiply, finish)
-    for i in range(steps):
-        copy_out(i).start()
-
-    @pl.when(big_ref[0] > 0)
+    most = functools.reduce(jnp.maximum, [r[...] for r in mosts])
+
+    @pl.when(jnp.max(most) > (TOP - 1.0) ** 2)
     def _():
         def past_top(i, _):
             raw = lax.dot_general(
-                qt_ref[:, tile_of(i, tile)], key_ref[...], (((0,), (1,)), ((), ())), preferred_element_type=F32
+                q_ref[tile_of(i, tile), :], key_ref[...], (((1,), (1,)), ((), ())), preferred_element_type=F32
             )
             over = jnp.maximum(raw * (scale * LOG2E) - TOP, 0.0)
             coef = coef_ref[tile_of(i, rows), :]
-            columns = [
-                jnp.sum(over[t * heads : (t + 1) * heads, :] * coef[t : t + 1, :], axis=1, keepdims=True)
-                for t in range(rows)
-            ]
-            gw_ref[tile_of(i, rows), :] += lanes_of(columns) * LN2
+            block = jnp.zeros((heads, 128), F32)
+            for t in range(rows):
+                block = add_column(block, t, over[t * heads : (t + 1) * heads, :] * coef[t : t + 1, :])
+            gw_ref[tile_of(i, rows), :] += as_rows(block)
             return 0
 
         lax.fori_loop(0, steps, past_top, 0)
@@ -359,23 +406,17 @@
         copy_out(i).wait()
 
 
-def may_pass_top(q_flat, keys):
-    q_most = jnp.max(jnp.sum(jnp.square(q_flat.astype(F32)), axis=1))
-    k_most = jnp.max(jnp.sum(jnp.square(keys.astype(F32)), axis=1))
-    bound = q_most * k_most * (LOG2E * LOG2E / q_flat.shape[1])
-    return (bound > (TOP - 1.0) ** 2).astype(jnp.int32).reshape(1)
-
-
-def second_pass(big, powers, probs, mass_parts, columns, row_weight, weights, keys, q_turned, rows=8):
+def second_pass(firsts, mass_parts, columns, row_weight, weights, keys, q_flat, rows=8):
+    powers, probs, mosts = zip(*firsts)
     key_total = keys.shape[0]
-    total = q_turned.shape[1]
+    total = q_flat.shape[0]
     own, heads = weights.shape
     tile = rows * heads
     steps = own // rows
     width = keys.shape[1]
     flat = [piece for pieces in mass_parts for piece in pieces]
     vmem = pl.BlockSpec(memory_space=pltpu.VMEM)
-    hbm = pl.BlockSpec(memory_space=pl.ANY)
+    hbm = pl.BlockSpec(memory_space=pltpu.HBM)
     return pl.pallas_call(
         functools.partial(
             second_kernel,
@@ -385,10 +426,7 @@
             columns,
             1.0 / math.sqrt(width),
         ),
-        in_specs=[pl.BlockSpec(memory_space=pltpu.SMEM)]
-        + [vmem] * 4
-        + [hbm] * len(powers)
-        + [vmem] * (len(probs) + len(flat)),
+        in_specs=[vmem] * 4 + [hbm] * len(powers) + [vmem] * (2 * len(probs) + len(flat)),
         out_specs=[hbm, vmem, vmem, vmem],
         out_shape=[
             jax.ShapeDtypeStruct((total, width), F32),
@@ -408,7 +446,7 @@
         compiler_params=pltpu.CompilerParams(vmem_limit_bytes=VMEM_BYTES),
         cost_estimate=SHORT,
         name="second_pass",
-    )(big, row_weight, weights, keys, q_turned, *powers, *probs, *flat)
+    )(row_weight, weights, keys, q_flat, *powers, *probs, *mosts, *flat)
 
 
 def swap(x, bit):
@@ -444,47 +482,37 @@
     rest_far = sorted((d for d in sums_of_bits if d & (d - 1) != 0), key=int.bit_count)
 
     queries = prep(main_q, log_norms.T, width)
-    index_far = [swap(index_k, d) for d in near_far + rest_far]
-    main_k, index_k, *index_far = together(main_k, index_k, *index_far)
     keys_at = {0: main_k}
     for d in near_far:
         keys_at[d] = swap(main_k, d)
     keys_at[1] = swap(main_k, 1)
-    index_w, row_weight, offsets, key_map, index_q, index_k, queries = together(
-        index_w, row_weight, offsets, key_map, index_q, index_k, queries
+    index_w, row_weight, offsets, key_map, index_q, queries = together(
+        index_w, row_weight, offsets, key_map, index_q, queries
     )
-    index_mine = [index_k] + index_far
-    index_theirs = swap(jnp.stack(index_mine), 1)
     far = [0] + near_far + rest_far
     order = far + [d + 1 for d in far]
     blocks = jnp.stack([here ^ d for d in order])
-    key_pos = key_map[blocks][:, None] * key_rows + jnp.arange(key_rows, dtype=jnp.int32)[None, :]
-    index_keys = jnp.concatenate([*index_mine, index_theirs.reshape(-1, index_width)], axis=0)
-    own_pos = (offsets[0] + rank * own_rows).reshape(1).astype(jnp.int32)
+    places = jnp.concatenate([offsets[:1], rank.reshape(1), key_map[blocks] * key_rows]).astype(jnp.int32)
 
     def head_sums(members, parts):
-        places = jnp.stack([offsets[0], rank if parts > 1 else 0 * rank]).astype(jnp.int32)
-        group_pos = jnp.concatenate([key_pos[order.index(d)] for d in members]).reshape(1, -1)
-        return mass(places, queries, group_pos, [keys_at[d] for d in members], width, parts)
+        at = [(order.index(d), 0) for d in members]
+        return mass(places, queries, at, [keys_at[d] for d in members], width, parts)
 
     def to_owners(sums):
         return [sums[0]] + [turn(sums[k], k) for k in range(1, ranks)]
 
     q_flat = index_q.reshape(own_rows * heads, index_width)
-    q_turned = q_flat.T
-    big = may_pass_top(q_flat, index_keys)
     row_weight = row_weight[:, None]
     tiles = own_rows // 8
-    ends = [0, tiles * 5 // 7, tiles]
-    powers, probs = [], []
-
-    def index_part(n, *others):
-        first, last = ends[n] * 8, ends[n + 1] * 8
-        rows = after(q_flat[first * heads : last * heads], *others)
-        power, prob = first_pass(own_pos + first, rows, index_keys, index_w[first:last], key_pos.reshape(1, -1))
-        powers.append(power)
-        probs.append(prob)
-        return prob
+    ends = [0, tiles * 2 // 7 * 8, tiles * 8]
+    q_parts = [q_flat[a * heads : b * heads] for a, b in zip(ends, ends[1:])]
+    w_parts = [index_w[a:b] for a, b in zip(ends, ends[1:])]
+    firsts = []
+
+    def index_part(n, index_keys, *others):
+        rows = after(q_parts[n], *others)
+        firsts.append(first_pass(places, (ends[n], own_rows), rows, index_keys, w_parts[n]))
+        return firsts[-1][1]
 
     group_own = [0, 1]
     group_near = [d + side for d in near_far for side in (0, 1)]
@@ -493,10 +521,15 @@
     columns = tuple((n, group.index(d)) for d in order for n, group in enumerate(groups) if d in group)
 
     sums_own = head_sums(group_own, 1)[0]
-    part_0 = index_part(0, sums_own)
+    index_k = after(index_k, sums_own)
+    index_mine = [index_k] + [swap(index_k, d) for d in near_far + rest_far]
+    got = together(*index_mine, *[keys_at[d] for d in near_far], row_weight, *q_parts, *w_parts)
+    index_mine, got = got[: len(index_mine)], got[len(index_mine) :]
+    keys_at.update(zip(near_far, got))
+    row_weight, *got = got[len(near_far) :]
+    q_parts, w_parts = got[: len(q_parts)], got[len(q_parts) :]
+    index_theirs = swap(jnp.stack(index_mine), 1)
     sums_own = lax.psum_scatter(sums_own, "tp", scatter_dimension=0, tiled=True)
-    part_0, sums_own, *got = together(part_0, sums_own, *[keys_at[d] for d in near_far])
-    keys_at.update(zip(near_far, got))
     for d in rest_far:
         lowest, highest = d & -d, 1 << (d.bit_length() - 1)
         source = jnp.where(here % 2 == 0, keys_at[d ^ lowest], keys_at[d ^ highest])
@@ -505,17 +538,19 @@
         )
     for d in near_far:
         keys_at[d + 1] = swap(keys_at[d], 1)
+    index_keys = jnp.concatenate([*index_mine, index_theirs.reshape(-1, index_width)], axis=0)
     sums_near = head_sums(group_near, ranks)
-    got = together(sums_near[0], *[keys_at[d] for d in rest_far])
-    keys_at.update(zip(rest_far, got[1:]))
+    part_0 = index_part(0, index_keys, sums_near[0])
+    sums_near = to_owners(sums_near)
+    part_0, *got = together(part_0, *[keys_at[d] for d in rest_far])
+    keys_at.update(zip(rest_far, got))
     for d in rest_far:
         keys_at[d + 1] = swap(keys_at[d], 1)
-    sums_near = to_owners(sums_near)
     sums_rest = head_sums(group_rest, ranks)
-    index_part(1, sums_rest[0])
+    index_part(1, index_keys, sums_rest[0])
     sums_rest = to_owners(sums_rest)
     grad_q, grad_w, mine, theirs = second_pass(
-        big, powers, probs, [[sums_own], sums_near, sums_rest], columns, row_weight, index_w, index_keys, q_turned
+        firsts, [[sums_own], sums_near, sums_rest], columns, row_weight, index_w, index_keys, q_flat
     )
 
     mine = mine + swap(theirs, 1)

time: 177 us -> 167 us (0.944)
  local copies, waits for them, and re-layouts: 17.3 us -> 11.4 us
  other arithmetic: 10.4 us -> 4.77 us
  starting transfers between devices: 31.7 us -> 35.4 us
    ppermute x1, waiting for transfers between devices: 5.7 us -> 0.01 us  [per_device(): lax.ppermute(source, 'ctx', [(i, i ^ (highest if i % 2 else lowest)) for...]
    ppermute x9, waiting for transfers between devices: 5.16 us -> 9.11 us  [turn(): return lax.ppermute(x, 'tp', [(i, (i + steps) % size) for i in range(size)])]
    ppermute x14, starting transfers between devices: 16.8 us -> 20.7 us  [swap(): return lax.ppermute(x, 'ctx', [(i, i ^ bit) for i in range(size)])]
    reshape x1 -> x0, local copies, waits for them, and re-layouts: 2.93 us -> none  [per_device(): q_flat = index_q.reshape(own_rows * heads, index_width)]
    reduce_sum x2 -> x0, other arithmetic: 2.17 us -> none  [the longest x1 1.16 us: may_pass_top(): k_most = jnp.max(jnp.sum(jnp.square(keys.astype(F32)), axis=1))]
    unnamed x49 -> x43, local copies, waits for them, and re-layouts: 7.28 us -> 6.44 us
  transfers between devices with their start and end apart: 25 -> 25, of which waited for: 13 -> 9; matrix products, arithmetic and copies ran while one was open for 12% -> 6% of each run, Pallas kernels for 28% -> 30%
where the time goes in v3:
time: 167 us
  Pallas kernels  71.4 us (43%)
  starting transfers between devices  35.4 us (21%)
  waiting for transfers between devices  28.9 us (17%)
  between operations  15 us (9%)
  local copies, waits for them, and re-layouts  11.4 us (7%)
  other arithmetic  4.77 us (3%)
    pallas_call x3, Pallas kernels, mass(): pl.pallas_call(functools.partial(mass_kernel, width, step_heads, tuple(me...  22.8 us
    pallas_call x1, Pallas kernels, second_pass(): pl.pallas_call(functools.partial(second_kernel, rows, tuple((len(p) for p...  21.4 us
    ppermute x14, starting transfers between devices, swap(): return lax.ppermute(x, 'ctx', [(i, i ^ bit) for i in range(size)])  20.7 us
    pallas_call x2, Pallas kernels, first_pass(): pl.pallas_call(functools.partial(first_kernel, rows, 1.0 / math.sqrt(widt...  20.4 us
    ppermute x14, waiting for transfers between devices, swap(): return lax.ppermute(x, 'ctx', [(i, i ^ bit) for i in range(size)])  19.7 us
    ppermute x9, starting transfers between devices, turn(): return lax.ppermute(x, 'tp', [(i, (i + steps) % size) for i in range(size)])  13.4 us
    ppermute x9, waiting for transfers between devices, turn(): return lax.ppermute(x, 'tp', [(i, (i + steps) % size) for i in range(size)])  9.11 us
    pallas_call x1, Pallas kernels, prep(): pl.pallas_call(functools.partial(prep_kernel, width, step_heads, math.sqr...  6.83 us
  transfers between devices with their start and end apart: 25, of which 9 were waited for; matrix products, arithmetic and copies ran while one was open for 6% of the time, Pallas kernels for 30%

profile of v3, /device:TPU:0, one launch (start us, length us, event | category | flops | bytes accessed | tf_op | source)
XLA Modules:
  0.0 166.8 jit_solution(6340033033257322102)
XLA Ops:
  7.7 2.6 %collective-permute-start.4 = (bf16[128,6144]{1,0:T(8,128)(2,1)}, bf16[128,6144]{1,0:T(8,128)(2,1)S(1)}, u32[]{:S(2)}, u32[]{:S(2)}) collective-permute-start(bf16[128,6144]{1,0:T(8,128)(2,1)} %refs_0_.1), channel_id=1, source_target_pairs={{0,8},{4,12},{8,0},{12,4},{16,24},{20,28},{24,16},{28,20},{1,9},{5... | collective-permute-start | bytes 4718600 | tf_op jit(solution)/shard_map/ppermute | solution.py:454
  10.3 1.5 collective-permute-start.5
  12.5 6.8 %prep.1.qa_hbm = bf16[448,8192]{1,0:T(8,128)(2,1)} custom-call(bf16[448,6144]{1,0:T(8,128)(2,1)} %q_ref.1, f32[32,448]{1,0:T(8,128)} %bitcast.45), custom_call_target="tpu_custom_call" | custom-call | bytes 1024 | tf_op jit(solution)/shard_map/prep/pallas_call | solution.py:55
  20.8 6.8 %mass.3 = f32[448,256]{1,0:T(8,128)} custom-call(s32[10]{0:T(128)} %pad_add_fusion.pos_ref, bf16[448,8192]{1,0:T(8,128)(2,1)} %prep.1.qa_hbm, bf16[128,6144]{1,0:T(8,128)(2,1)} %refs_0_.1, bf16[128,6144]{1,0:T(8,128)(2,1)} %collective-permute-done.refs_1_), custom_call_target="tpu_custom_call" | custom-call | bytes 1024 | tf_op jit(solution)/shard_map/mass/pallas_call | solution.py:139
  28.3 2.9 %collective-permute-start.3 = (bf16[128,128]{1,0:T(8,128)(2,1)S(1)}, bf16[128,128]{1,0:T(8,128)(2,1)}, u32[]{:S(2)}, u32[]{:S(2)}) collective-permute-start(bf16[128,128]{1,0:T(8,128)(2,1)S(1)} %copy-done.12), channel_id=1, source_target_pairs={{0,24},{4,28},{8,16},{12,20},{16,8},{20,12},{24,0},{28,4},{1,25},{... | collective-permute-start | bytes 98312 | tf_op jit(solution)/shard_map/ppermute | solution.py:454
  34.5 11.2 %collective-permute-done.4.refs_0_ = bf16[128,6144]{1,0:T(8,128)(2,1)S(1)} collective-permute-done((bf16[128,6144]{1,0:T(8,128)(2,1)}, bf16[128,6144]{1,0:T(8,128)(2,1)S(1)}, u32[]{:S(2)}, u32[]{:S(2)}) %collective-permute-start.4) | collective-permute-done | bytes 1572896 | tf_op jit(solution)/shard_map/ppermute | solution.py:454
  45.8 2.0 %collective-permute-done.5.refs_2_ = bf16[128,6144]{1,0:T(8,128)(2,1)} collective-permute-done((bf16[128,6144]{1,0:T(8,128)(2,1)}, bf16[128,6144]{1,0:T(8,128)(2,1)}, u32[]{:S(2)}, u32[]{:S(2)}) %collective-permute-start.5) | collective-permute-done | bytes 1572896 | tf_op jit(solution)/shard_map/ppermute | solution.py:454
  49.0 1.7 broadcast_select_fusion
  50.7 1.3 collective-permute-start.9
  56.8 9.2 %mass.4 = (f32[112,512]{1,0:T(8,128)}, f32[112,512]{1,0:T(8,128)}, f32[112,512]{1,0:T(8,128)}, f32[112,512]{1,0:T(8,128)}) custom-call(s32[10]{0:T(128)} %pad_add_fusion.pos_ref, bf16[448,8192]{1,0:T(8,128)(2,1)} %prep.1.qa_hbm, bf16[128,6144]{1,0:T(8,128)(2,1)} %copy-done.3, bf16[128,6144]{1,0:T(8,128)(2,1)} %copy-done.5, ...), custom_call_target="tpu_custom_call" | custom-call | bytes 1024 | tf_op jit(solution)/shard_map/mass/pallas_call | solution.py:139
  66.1 6.8 %first_pass.2 = (f32[2048,1024]{1,0:T(8,128)}, f32[32,1024]{1,0:T(8,128)}, f32[8,128]{1,0:T(8,128)}) custom-call(s32[10]{0:T(128)} %pad_add_fusion.pos_ref, bf16[2048,128]{1,0:T(8,128)(2,1)} %bitcast.39, bf16[1024,128]{1,0:T(8,128)(2,1)} %copy-done.4, f32[32,64]{1,0:T(8,128)} %slice.42.w_ref), custom_call_target="tpu_custom_call" | custom-call | bytes 1024 | tf_op jit(solution)/shard_map/first_pass/pallas_call | solution.py:272
  73.5 1.6 collective-permute-start.11
  75.1 2.6 %collective-permute-start.12 = (f32[112,512]{1,0:T(8,128)}, f32[112,512]{1,0:T(8,128)S(1)}, u32[]{:S(2)}, u32[]{:S(2)}) collective-permute-start(f32[112,512]{1,0:T(8,128)} %get-tuple-element.72), channel_id=1, source_target_pairs={{0,2},{1,3},{2,0},{3,1},{4,6},{5,7},{6,4},{7,5},{8,10},{9,11},{10,... | collective-permute-start | bytes 688136 | tf_op jit(solution)/shard_map/ppermute | solution.py:459
  77.7 1.3 collective-permute-start.13
  80.2 6.7 %mass.5 = (f32[112,256]{1,0:T(8,128)}, f32[112,256]{1,0:T(8,128)}, f32[112,256]{1,0:T(8,128)}, f32[112,256]{1,0:T(8,128)}) custom-call(s32[10]{0:T(128)} %pad_add_fusion.pos_ref, bf16[448,8192]{1,0:T(8,128)(2,1)} %prep.1.qa_hbm, bf16[128,6144]{1,0:T(8,128)(2,1)} %collective-permute-done.9.refs_0_, bf16[128,6144]{1,0:T(8,128)(2,1)} %copy-done.7), custom_call_target="tpu_custom_call" | custom-call | bytes 1024 | tf_op jit(solution)/shard_map/mass/pallas_call | solution.py:139
  88.8 2.0 %collective-permute-start.16 = (f32[112,256]{1,0:T(8,128)}, f32[112,256]{1,0:T(8,128)S(1)}, u32[]{:S(2)}, u32[]{:S(2)}) collective-permute-start(f32[112,256]{1,0:T(8,128)} %get-tuple-element.76), channel_id=1, source_target_pairs={{0,3},{1,0},{2,1},{3,2},{4,7},{5,4},{6,5},{7,6},{8,11},{9,8},{10,9... | collective-permute-start | bytes 344072 | tf_op jit(solution)/shard_map/ppermute | solution.py:459
  91.6 13.6 %first_pass.3 = (f32[5120,1024]{1,0:T(8,128)}, f32[80,1024]{1,0:T(8,128)}, f32[8,128]{1,0:T(8,128)}) custom-call(s32[10]{0:T(128)} %pad_add_fusion.pos_ref, bf16[5120,128]{1,0:T(8,128)(2,1)} %bitcast.38, bf16[1024,128]{1,0:T(8,128)(2,1)} %copy-done.4, f32[80,64]{1,0:T(8,128)} %slice.43.w_ref), custom_call_target="tpu_custom_call" | custom-call | bytes 1024 | tf_op jit(solution)/shard_map/first_pass/pallas_call | solution.py:272
  105.3 7.5 %collective-permute-done.15.refs_13_ = f32[112,256]{1,0:T(8,128)S(1)} collective-permute-done((f32[112,256]{1,0:T(8,128)}, f32[112,256]{1,0:T(8,128)S(1)}, u32[]{:S(2)}, u32[]{:S(2)}) %collective-permute-start.15) | collective-permute-done | bytes 114720 | tf_op jit(solution)/shard_map/ppermute | solution.py:459
  113.5 21.4 %second_pass.1 = (f32[7168,128]{1,0:T(8,128)}, f32[112,64]{1,0:T(8,128)}, f32[128,512]{1,0:T(8,128)}, f32[128,512]{1,0:T(8,128)}) custom-call(f32[112,1]{1,0:T(8,128)} %copy.23.rw_ref, f32[112,64]{1,0:T(8,128)} %copy-done.8, bf16[1024,128]{1,0:T(8,128)(2,1)} %copy-done.4, bf16[7168,128]{1,0:T(8,128)(2,1)} %bitcast.37, ...), custom_call_target="tpu_custom_call" | custom-call | bytes 1024 | tf_op jit(solution)/shard_map/second_pass/pallas_call | solution.py:420
  134.9 1.7 %collective-permute-done.17 = f32[128,512]{1,0:T(8,128)S(1)} collective-permute-done((f32[128,512]{1,0:T(8,128)}, f32[128,512]{1,0:T(8,128)S(1)}, u32[]{:S(2)}, u32[]{:S(2)}) %collective-permute-start.17) | collective-permute-done | bytes 262176 | tf_op jit(solution)/shard_map/ppermute | solution.py:454
  137.7 9.8 %collective-permute-start.18 = (f32[128,128]{1,0:T(8,128)S(1)}, f32[128,128]{1,0:T(8,128)S(1)}, u32[]{:S(2)}, u32[]{:S(2)}) collective-permute-start(f32[128,128]{1,0:T(8,128)S(1)} %get-tuple-element.87), channel_id=1, source_target_pairs={{0,8},{4,12},{8,0},{12,4},{16,24},{20,28},{24,16},{28,20},{1,9},{5... | collective-permute-start | bytes 196616 | tf_op jit(solution)/shard_map/ppermute | solution.py:454
  147.5 1.5 collective-permute-start.20
  149.9 3.2 %collective-permute-done.19 = f32[128,128]{1,0:T(8,128)S(1)} collective-permute-done((f32[128,128]{1,0:T(8,128)S(1)}, f32[128,128]{1,0:T(8,128)S(1)}, u32[]{:S(2)}, u32[]{:S(2)}) %collective-permute-start.19) | collective-permute-done | bytes 65568 | tf_op jit(solution)/shard_map/ppermute | solution.py:454
  153.3 3.7 %collective-permute-start.23 = (f32[32,128]{1,0:T(8,128)S(1)}, f32[32,128]{1,0:T(8,128)S(1)}, u32[]{:S(2)}, u32[]{:S(2)}) collective-permute-start(f32[32,128]{1,0:T(8,128)S(1)} %get-tuple-element.91), channel_id=1, source_target_pairs={{0,3},{1,0},{2,1},{3,2},{4,7},{5,4},{6,5},{7,6},{8,11},{9,8},{10,9... | collective-permute-start | bytes 49160 | tf_op jit(solution)/shard_map/ppermute | solution.py:459
  (98 shorter events, 22.1 us)
Async XLA Ops:
  7.2 98.0 %reduce-scatter.2.cloned.1.call-start = ((), (), s32[]{:S(2)}) async-start(), calls=%async_computation.1 | async-start | bytes 573440 | tf_op jit(solution)/shard_map/reduce_scatter | solution.py:532
  7.2 13.5 %collective-permute-start = (bf16[128,6144]{1,0:T(8,128)(2,1)}, bf16[128,6144]{1,0:T(8,128)(2,1)}, u32[]{:S(2)}, u32[]{:S(2)}) collective-permute-start(bf16[128,6144]{1,0:T(8,128)(2,1)} %refs_0_.1), channel_id=1, source_target_pairs={{0,4},{4,0},{8,12},{12,8},{16,20},{20,16},{24,28},{28,24},{1,5},{5... | collective-permute-start | bytes 4718600 | tf_op jit(solution)/shard_map/ppermute | solution.py:454
  7.7 38.0 %collective-permute-start.4 = (bf16[128,6144]{1,0:T(8,128)(2,1)}, bf16[128,6144]{1,0:T(8,128)(2,1)S(1)}, u32[]{:S(2)}, u32[]{:S(2)}) collective-permute-start(bf16[128,6144]{1,0:T(8,128)(2,1)} %refs_0_.1), channel_id=1, source_target_pairs={{0,8},{4,12},{8,0},{12,4},{16,24},{20,28},{24,16},{28,20},{1,9},{5... | collective-permute-start | bytes 4718600 | tf_op jit(solution)/shard_map/ppermute | solution.py:454
  10.3 37.5 %collective-permute-start.5 = (bf16[128,6144]{1,0:T(8,128)(2,1)}, bf16[128,6144]{1,0:T(8,128)(2,1)}, u32[]{:S(2)}, u32[]{:S(2)}) collective-permute-start(bf16[128,6144]{1,0:T(8,128)(2,1)} %refs_0_.1), channel_id=1, source_target_pairs={{0,16},{4,20},{8,24},{12,28},{16,0},{20,4},{24,8},{28,12},{1,17},{... | collective-permute-start | bytes 4718600 | tf_op jit(solution)/shard_map/ppermute | solution.py:454
  27.6 20.2 %collective-permute-start.1 = (bf16[128,128]{1,0:T(8,128)(2,1)S(1)}, bf16[128,128]{1,0:T(8,128)(2,1)S(1)}, u32[]{:S(2)}, u32[]{:S(2)}) collective-permute-start(bf16[128,128]{1,0:T(8,128)(2,1)S(1)} %copy-done.12), channel_id=1, source_target_pairs={{0,8},{4,12},{8,0},{12,4},{16,24},{20,28},{24,16},{28,20},{1,9},{5... | collective-permute-start | bytes 98312 | tf_op jit(solution)/shard_map/ppermute | solution.py:454
  28.2 20.3 %collective-permute-start.2 = (bf16[128,128]{1,0:T(8,128)(2,1)S(1)}, bf16[128,128]{1,0:T(8,128)(2,1)}, u32[]{:S(2)}, u32[]{:S(2)}) collective-permute-start(bf16[128,128]{1,0:T(8,128)(2,1)S(1)} %copy-done.12), channel_id=1, source_target_pairs={{0,16},{4,20},{8,24},{12,28},{16,0},{20,4},{24,8},{28,12},{1,17},{... | collective-permute-start | bytes 98312 | tf_op jit(solution)/shard_map/ppermute | solution.py:454
  28.3 20.2 %collective-permute-start.3 = (bf16[128,128]{1,0:T(8,128)(2,1)S(1)}, bf16[128,128]{1,0:T(8,128)(2,1)}, u32[]{:S(2)}, u32[]{:S(2)}) collective-permute-start(bf16[128,128]{1,0:T(8,128)(2,1)S(1)} %copy-done.12), channel_id=1, source_target_pairs={{0,24},{4,28},{8,16},{12,20},{16,8},{20,12},{24,0},{28,4},{1,25},{... | collective-permute-start | bytes 98312 | tf_op jit(solution)/shard_map/ppermute | solution.py:454
  48.5 6.0 %collective-permute-start.7 = (bf16[128,6144]{1,0:T(8,128)(2,1)S(1)}, bf16[128,6144]{1,0:T(8,128)(2,1)S(1)}, u32[]{:S(2)}, u32[]{:S(2)}) collective-permute-start(bf16[128,6144]{1,0:T(8,128)(2,1)S(1)} %collective-permute-done.4.refs_0_), channel_id=1, source_target_pairs={{0,4},{4,0},{8,12},{12,8},{16,20},{20,16},{24,28},{28,24},{1,5},{5... | collective-permute-start | bytes 4718600 | tf_op jit(solution)/shard_map/ppermute | solution.py:454
  48.5 6.0 %collective-permute-start.8 = (bf16[128,6144]{1,0:T(8,128)(2,1)}, bf16[128,6144]{1,0:T(8,128)(2,1)S(1)}, u32[]{:S(2)}, u32[]{:S(2)}) collective-permute-start(bf16[128,6144]{1,0:T(8,128)(2,1)} %collective-permute-done.5.refs_2_), channel_id=1, source_target_pairs={{0,4},{4,0},{8,12},{12,8},{16,20},{20,16},{24,28},{28,24},{1,5},{5... | collective-permute-start | bytes 4718600 | tf_op jit(solution)/shard_map/ppermute | solution.py:454
  50.7 22.2 %collective-permute-start.9 = (bf16[128,6144]{1,0:T(8,128)(2,1)S(1)}, bf16[128,6144]{1,0:T(8,128)(2,1)}, u32[]{:S(2)}, u32[]{:S(2)}) collective-permute-start(bf16[128,6144]{1,0:T(8,128)(2,1)S(1)} %broadcast_select_fusion), channel_id=1, source_target_pairs={{0,8},{4,20},{8,0},{12,28},{16,24},{20,4},{24,16},{28,12},{1,9},{5... | collective-permute-start | bytes 4718600 | tf_op jit(solution)/shard_map/ppermute | solution.py:536
  72.9 6.1 %collective-permute-start.10 = (bf16[128,6144]{1,0:T(8,128)(2,1)}, bf16[128,6144]{1,0:T(8,128)(2,1)S(1)}, u32[]{:S(2)}, u32[]{:S(2)}) collective-permute-start(bf16[128,6144]{1,0:T(8,128)(2,1)} %collective-permute-done.9.refs_0_), channel_id=1, source_target_pairs={{0,4},{4,0},{8,12},{12,8},{16,20},{20,16},{24,28},{28,24},{1,5},{5... | collective-permute-start | bytes 4718600 | tf_op jit(solution)/shard_map/ppermute | solution.py:454
  73.5 15.4 %collective-permute-start.11 = (f32[112,512]{1,0:T(8,128)}, f32[112,512]{1,0:T(8,128)S(1)}, u32[]{:S(2)}, u32[]{:S(2)}) collective-permute-start(f32[112,512]{1,0:T(8,128)} %get-tuple-element.71), channel_id=1, source_target_pairs={{0,1},{1,2},{2,3},{3,0},{4,5},{5,6},{6,7},{7,4},{8,9},{9,10},{10,1... | collective-permute-start | bytes 688136 | tf_op jit(solution)/shard_map/ppermute | solution.py:459
  75.1 30.1 %collective-permute-start.12 = (f32[112,512]{1,0:T(8,128)}, f32[112,512]{1,0:T(8,128)S(1)}, u32[]{:S(2)}, u32[]{:S(2)}) collective-permute-start(f32[112,512]{1,0:T(8,128)} %get-tuple-element.72), channel_id=1, source_target_pairs={{0,2},{1,3},{2,0},{3,1},{4,6},{5,7},{6,4},{7,5},{8,10},{9,11},{10,... | collective-permute-start | bytes 688136 | tf_op jit(solution)/shard_map/ppermute | solution.py:459
  77.7 27.5 %collective-permute-start.13 = (f32[112,512]{1,0:T(8,128)}, f32[112,512]{1,0:T(8,128)S(1)}, u32[]{:S(2)}, u32[]{:S(2)}) collective-permute-start(f32[112,512]{1,0:T(8,128)} %get-tuple-element.73), channel_id=1, source_target_pairs={{0,3},{1,0},{2,1},{3,2},{4,7},{5,4},{6,5},{7,6},{8,11},{9,8},{10,9... | collective-permute-start | bytes 688136 | tf_op jit(solution)/shard_map/ppermute | solution.py:459
  86.9 18.3 %collective-permute-start.14 = (f32[112,256]{1,0:T(8,128)}, f32[112,256]{1,0:T(8,128)S(1)}, u32[]{:S(2)}, u32[]{:S(2)}) collective-permute-start(f32[112,256]{1,0:T(8,128)} %get-tuple-element.74), channel_id=1, source_target_pairs={{0,1},{1,2},{2,3},{3,0},{4,5},{5,6},{6,7},{7,4},{8,9},{9,10},{10,1... | collective-permute-start | bytes 344072 | tf_op jit(solution)/shard_map/ppermute | solution.py:459
  87.7 25.1 %collective-permute-start.15 = (f32[112,256]{1,0:T(8,128)}, f32[112,256]{1,0:T(8,128)S(1)}, u32[]{:S(2)}, u32[]{:S(2)}) collective-permute-start(f32[112,256]{1,0:T(8,128)} %get-tuple-element.75), channel_id=1, source_target_pairs={{0,2},{1,3},{2,0},{3,1},{4,6},{5,7},{6,4},{7,5},{8,10},{9,11},{10,... | collective-permute-start | bytes 344072 | tf_op jit(solution)/shard_map/ppermute | solution.py:459
  88.8 23.9 %collective-permute-start.16 = (f32[112,256]{1,0:T(8,128)}, f32[112,256]{1,0:T(8,128)S(1)}, u32[]{:S(2)}, u32[]{:S(2)}) collective-permute-start(f32[112,256]{1,0:T(8,128)} %get-tuple-element.76), channel_id=1, source_target_pairs={{0,3},{1,0},{2,1},{3,2},{4,7},{5,4},{6,5},{7,6},{8,11},{9,8},{10,9... | collective-permute-start | bytes 344072 | tf_op jit(solution)/shard_map/ppermute | solution.py:459
  134.9 1.8 %collective-permute-start.17 = (f32[128,512]{1,0:T(8,128)}, f32[128,512]{1,0:T(8,128)S(1)}, u32[]{:S(2)}, u32[]{:S(2)}) collective-permute-start(f32[128,512]{1,0:T(8,128)} %get-tuple-element.80), channel_id=1, source_target_pairs={{0,4},{4,0},{8,12},{12,8},{16,20},{20,16},{24,28},{28,24},{1,5},{5... | collective-permute-start | bytes 786440 | tf_op jit(solution)/shard_map/ppermute | solution.py:454
  137.7 12.2 %collective-permute-start.18 = (f32[128,128]{1,0:T(8,128)S(1)}, f32[128,128]{1,0:T(8,128)S(1)}, u32[]{:S(2)}, u32[]{:S(2)}) collective-permute-start(f32[128,128]{1,0:T(8,128)S(1)} %get-tuple-element.87), channel_id=1, source_target_pairs={{0,8},{4,12},{8,0},{12,4},{16,24},{20,28},{24,16},{28,20},{1,9},{5... | collective-permute-start | bytes 196616 | tf_op jit(solution)/shard_map/ppermute | solution.py:454
  147.5 5.6 %collective-permute-start.19 = (f32[128,128]{1,0:T(8,128)S(1)}, f32[128,128]{1,0:T(8,128)S(1)}, u32[]{:S(2)}, u32[]{:S(2)}) collective-permute-start(f32[128,128]{1,0:T(8,128)S(1)} %get-tuple-element.89), channel_id=1, source_target_pairs={{0,16},{4,20},{8,24},{12,28},{16,0},{20,4},{24,8},{28,12},{1,17},{... | collective-permute-start | bytes 196616 | tf_op jit(solution)/shard_map/ppermute | solution.py:454
  147.5 5.6 %collective-permute-start.20 = (f32[128,128]{1,0:T(8,128)S(1)}, f32[128,128]{1,0:T(8,128)S(1)}, u32[]{:S(2)}, u32[]{:S(2)}) collective-permute-start(f32[128,128]{1,0:T(8,128)S(1)} %get-tuple-element.88), channel_id=1, source_target_pairs={{0,24},{4,28},{8,16},{12,20},{16,8},{20,12},{24,0},{28,4},{1,25},{... | collective-permute-start | bytes 196616 | tf_op jit(solution)/shard_map/ppermute | solution.py:454
  153.2 5.6 %collective-permute-start.21 = (f32[32,128]{1,0:T(8,128)S(1)}, f32[32,128]{1,0:T(8,128)S(1)}, u32[]{:S(2)}, u32[]{:S(2)}) collective-permute-start(f32[32,128]{1,0:T(8,128)S(1)} %get-tuple-element.90), channel_id=1, source_target_pairs={{0,1},{1,2},{2,3},{3,0},{4,5},{5,6},{6,7},{7,4},{8,9},{9,10},{10,1... | collective-permute-start | bytes 49160 | tf_op jit(solution)/shard_map/ppermute | solution.py:459
  153.2 5.5 %collective-permute-start.22 = (f32[32,128]{1,0:T(8,128)S(1)}, f32[32,128]{1,0:T(8,128)S(1)}, u32[]{:S(2)}, u32[]{:S(2)}) collective-permute-start(f32[32,128]{1,0:T(8,128)S(1)} %get-tuple-element.92), channel_id=1, source_target_pairs={{0,2},{1,3},{2,0},{3,1},{4,6},{5,7},{6,4},{7,5},{8,10},{9,11},{10,... | collective-permute-start | bytes 49160 | tf_op jit(solution)/shard_map/ppermute | solution.py:459
  153.3 6.0 %collective-permute-start.23 = (f32[32,128]{1,0:T(8,128)S(1)}, f32[32,128]{1,0:T(8,128)S(1)}, u32[]{:S(2)}, u32[]{:S(2)}) collective-permute-start(f32[32,128]{1,0:T(8,128)S(1)} %get-tuple-element.91), channel_id=1, source_target_pairs={{0,3},{1,0},{2,1},{3,2},{4,7},{5,4},{6,5},{7,6},{8,11},{9,8},{10,9... | collective-permute-start | bytes 49160 | tf_op jit(solution)/shard_map/ppermute | solution.py:459
  (20 other events, 204.1 us)
Sparse Core Ops, SparseCore 0:
  73.6 31.5 reduce-scatter.1

commit v4 on v3

--- a/solution.py
+++ b/solution.py
@@ -11,6 +11,7 @@
 LOG2E = math.log2(math.e)
 LN2 = math.log(2.0)
 TOP = 120.0
+AHEAD = 5
 VMEM_BYTES = 56 * 1024 * 1024
 BF = jnp.bfloat16
 F32 = jnp.float32
@@ -326,7 +327,7 @@
                 def _():
                     copy_in(i, source, i - low).start()
 
-    for i in range(3):
+    for i in range(AHEAD):
         start_in(i)
     groups = []
     for size in splits:
@@ -380,7 +381,7 @@
             if not isinstance(i, int) or i + n < steps:
                 copy_in(i + n).wait()
         for n in range(1, number + 1):
-            start_in(i + number + n)
+            start_in(i + AHEAD - 1 + n)
 
     copy_in(0).wait()
     in_pairs(steps, elements, multiply, finish)
@@ -523,13 +524,15 @@
     sums_own = head_sums(group_own, 1)[0]
     index_k = after(index_k, sums_own)
     index_mine = [index_k] + [swap(index_k, d) for d in near_far + rest_far]
-    got = together(*index_mine, *[keys_at[d] for d in near_far], row_weight, *q_parts, *w_parts)
+    sums_own = lax.psum_scatter(sums_own, "tp", scatter_dimension=0, tiled=True)
+    sums_own, *got = together(
+        sums_own, *index_mine, *[keys_at[d] for d in near_far], row_weight, *q_parts, *w_parts
+    )
     index_mine, got = got[: len(index_mine)], got[len(index_mine) :]
     keys_at.update(zip(near_far, got))
     row_weight, *got = got[len(near_far) :]
     q_parts, w_parts = got[: len(q_parts)], got[len(q_parts) :]
     index_theirs = swap(jnp.stack(index_mine), 1)
-    sums_own = lax.psum_scatter(sums_own, "tp", scatter_dimension=0, tiled=True)
     for d in rest_far:
         lowest, highest = d & -d, 1 << (d.bit_length() - 1)
         source = jnp.where(here % 2 == 0, keys_at[d ^ lowest], keys_at[d ^ highest])
@@ -539,9 +542,9 @@
     for d in near_far:
         keys_at[d + 1] = swap(keys_at[d], 1)
     index_keys = jnp.concatenate([*index_mine, index_theirs.reshape(-1, index_width)], axis=0)
-    sums_near = head_sums(group_near, ranks)
+    sums_near = head_sums(group_near, 1)
     part_0 = index_part(0, index_keys, sums_near[0])
-    sums_near = to_owners(sums_near)
+    sums_near = [lax.psum_scatter(sums_near[0], "tp", scatter_dimension=0, tiled=True)]
     part_0, *got = together(part_0, *[keys_at[d] for d in rest_far])
     keys_at.update(zip(rest_far, got))
     for d in rest_far:

time: 167 us -> 158 us (0.946)
  waiting for transfers between devices: 28.9 us -> 24 us
  starting transfers between devices: 35.4 us -> 30.9 us
  Pallas kernels: 71.4 us -> 69.3 us
    ppermute x9 -> x6, waiting for transfers between devices: 9.11 us -> 1.58 us  [turn(): return lax.ppermute(x, 'tp', [(i, (i + steps) % size) for i in range(size)])]
    ppermute x9 -> x6, starting transfers between devices: 13.4 us -> 9.44 us  [turn(): return lax.ppermute(x, 'tp', [(i, (i + steps) % size) for i in range(size)])]
    ppermute x14, waiting for transfers between devices: 19.7 us -> 22.4 us  [swap(): return lax.ppermute(x, 'ctx', [(i, i ^ bit) for i in range(size)])]
    pallas_call x1, Pallas kernels: 21.4 us -> 19 us  [second_pass(): pl.pallas_call(functools.partial(second_kernel, rows, tuple((len(p) for p...]
    unnamed x43 -> x41, local copies, waits for them, and re-layouts: 6.44 us -> 7.11 us
  transfers between devices with their start and end apart: 25 -> 23, of which waited for: 9 -> 9; matrix products, arithmetic and copies ran while one was open for 6% -> 7% of each run, Pallas kernels for 30% -> 32%
where the time goes in v4:
time: 158 us; the launch traced here: 157 us
  Pallas kernels  69.3 us (44%)
  starting transfers between devices  30.9 us (20%)
  waiting for transfers between devices  24 us (15%)
  between operations  15 us (9%)
  local copies, waits for them, and re-layouts  12.8 us (8%)
  other arithmetic  5.29 us (3%)
    pallas_call x3, Pallas kernels, mass(): pl.pallas_call(functools.partial(mass_kernel, width, step_heads, tuple(me...  23.2 us
    ppermute x14, waiting for transfers between devices, swap(): return lax.ppermute(x, 'ctx', [(i, i ^ bit) for i in range(size)])  22.4 us
    pallas_call x2, Pallas kernels, first_pass(): pl.pallas_call(functools.partial(first_kernel, rows, 1.0 / math.sqrt(widt...  20.4 us
    ppermute x14, starting transfers between devices, swap(): return lax.ppermute(x, 'ctx', [(i, i ^ bit) for i in range(size)])  20.2 us
    pallas_call x1, Pallas kernels, second_pass(): pl.pallas_call(functools.partial(second_kernel, rows, tuple((len(p) for p...  19 us
    ppermute x6, starting transfers between devices, turn(): return lax.ppermute(x, 'tp', [(i, (i + steps) % size) for i in range(size)])  9.44 us
    unnamed x41, local copies, waits for them, and re-layouts  7.11 us
    pallas_call x1, Pallas kernels, prep(): pl.pallas_call(functools.partial(prep_kernel, width, step_heads, math.sqr...  6.79 us
  transfers between devices with their start and end apart: 23, of which 9 were waited for; matrix products, arithmetic and copies ran while one was open for 7% of the time, Pallas kernels for 32%

profile of v4, /device:TPU:0, one launch (start us, length us, event | category | flops | bytes accessed | tf_op | source)
XLA Modules:
  0.0 157.3 jit_solution(775766249297536891)
XLA Ops:
  7.7 2.6 %collective-permute-start.4 = (bf16[128,6144]{1,0:T(8,128)(2,1)}, bf16[128,6144]{1,0:T(8,128)(2,1)S(1)}, u32[]{:S(2)}, u32[]{:S(2)}) collective-permute-start(bf16[128,6144]{1,0:T(8,128)(2,1)} %refs_0_.1), channel_id=1, source_target_pairs={{0,8},{4,12},{8,0},{12,4},{16,24},{20,28},{24,16},{28,20},{1,9},{5... | collective-permute-start | bytes 4718600 | tf_op jit(solution)/shard_map/ppermute | solution.py:455
  10.3 1.5 collective-permute-start.5
  12.5 6.8 %prep.1.qa_hbm = bf16[448,8192]{1,0:T(8,128)(2,1)} custom-call(bf16[448,6144]{1,0:T(8,128)(2,1)} %q_ref.1, f32[32,448]{1,0:T(8,128)} %bitcast.45), custom_call_target="tpu_custom_call" | custom-call | bytes 1024 | tf_op jit(solution)/shard_map/prep/pallas_call | solution.py:56
  20.6 6.8 %mass.3 = f32[448,256]{1,0:T(8,128)} custom-call(s32[10]{0:T(128)} %pad_add_fusion.pos_ref, bf16[448,8192]{1,0:T(8,128)(2,1)} %prep.1.qa_hbm, bf16[128,6144]{1,0:T(8,128)(2,1)} %refs_0_.1, bf16[128,6144]{1,0:T(8,128)(2,1)} %collective-permute-done.refs_1_), custom_call_target="tpu_custom_call" | custom-call | bytes 1024 | tf_op jit(solution)/shard_map/mass/pallas_call | solution.py:140
  28.2 2.9 %collective-permute-start.3 = (bf16[128,128]{1,0:T(8,128)(2,1)S(1)}, bf16[128,128]{1,0:T(8,128)(2,1)S(1)}, u32[]{:S(2)}, u32[]{:S(2)}) collective-permute-start(bf16[128,128]{1,0:T(8,128)(2,1)S(1)} %copy-done.9), channel_id=1, source_target_pairs={{0,24},{4,28},{8,16},{12,20},{16,8},{20,12},{24,0},{28,4},{1,25},{... | collective-permute-start | bytes 98312 | tf_op jit(solution)/shard_map/ppermute | solution.py:455
  35.2 10.6 %collective-permute-done.4.refs_0_ = bf16[128,6144]{1,0:T(8,128)(2,1)S(1)} collective-permute-done((bf16[128,6144]{1,0:T(8,128)(2,1)}, bf16[128,6144]{1,0:T(8,128)(2,1)S(1)}, u32[]{:S(2)}, u32[]{:S(2)}) %collective-permute-start.4) | collective-permute-done | bytes 1572896 | tf_op jit(solution)/shard_map/ppermute | solution.py:455
  45.8 2.0 %collective-permute-done.5.refs_2_ = bf16[128,6144]{1,0:T(8,128)(2,1)} collective-permute-done((bf16[128,6144]{1,0:T(8,128)(2,1)}, bf16[128,6144]{1,0:T(8,128)(2,1)}, u32[]{:S(2)}, u32[]{:S(2)}) %collective-permute-start.5) | collective-permute-done | bytes 1572896 | tf_op jit(solution)/shard_map/ppermute | solution.py:455
  49.1 1.6 %broadcast_select_fusion = bf16[128,6144]{1,0:T(8,128)(2,1)S(1)} fusion(bf16[128,6144]{1,0:T(8,128)(2,1)} %collective-permute-done.5.refs_2_, bf16[128,6144]{1,0:T(8,128)(2,1)S(1)} %collective-permute-done.4.refs_0_, pred[]{:T(512)S(6)} %eq.8), kind=kLoop, calls=%fused_computation.1 | loop fusion | flops 786432 | bytes 4718593 | tf_op jit(solution)/shard_map/jit(_where)/select_n | solution.py:538
  51.9 1.4 pad_maximum_fusion
  56.0 1.2 copy-done.6
  57.2 9.6 %mass.4 = f32[448,512]{1,0:T(8,128)} custom-call(s32[10]{0:T(128)} %pad_add_fusion.pos_ref, bf16[448,8192]{1,0:T(8,128)(2,1)} %prep.1.qa_hbm, bf16[128,6144]{1,0:T(8,128)(2,1)} %copy-done.3, bf16[128,6144]{1,0:T(8,128)(2,1)} %copy-done.5, bf16[128,6144]{1,0:T(8,128)(2,1)} %collective-permute-done.5.refs_2_, bf16[128,6144]{1,0:T(8,128)(2,1)} %copy-done.6), custom_call_target="tpu_custom_call" | custom-call | bytes 1024 | tf_op jit(solution)/shard_map/mass/pallas_call | solution.py:140
  67.6 6.8 %first_pass.2 = (f32[2048,1024]{1,0:T(8,128)}, f32[32,1024]{1,0:T(8,128)}, f32[8,128]{1,0:T(8,128)}) custom-call(s32[10]{0:T(128)} %pad_add_fusion.pos_ref, bf16[2048,128]{1,0:T(8,128)(2,1)} %bitcast.39, bf16[1024,128]{1,0:T(8,128)(2,1)} %copy-done.4, f32[32,64]{1,0:T(8,128)} %slice.42.w_ref), custom_call_target="tpu_custom_call" | custom-call | bytes 1024 | tf_op jit(solution)/shard_map/first_pass/pallas_call | solution.py:273
  75.0 3.2 %collective-permute-done.10.refs_1_ = bf16[128,6144]{1,0:T(8,128)(2,1)S(1)} collective-permute-done((bf16[128,6144]{1,0:T(8,128)(2,1)}, bf16[128,6144]{1,0:T(8,128)(2,1)S(1)}, u32[]{:S(2)}, u32[]{:S(2)}) %collective-permute-start.10) | collective-permute-done | bytes 1572896 | tf_op jit(solution)/shard_map/ppermute | solution.py:455
  79.4 6.8 %mass.5 = (f32[112,256]{1,0:T(8,128)}, f32[112,256]{1,0:T(8,128)}, f32[112,256]{1,0:T(8,128)}, f32[112,256]{1,0:T(8,128)}) custom-call(s32[10]{0:T(128)} %pad_add_fusion.pos_ref, bf16[448,8192]{1,0:T(8,128)(2,1)} %prep.1.qa_hbm, bf16[128,6144]{1,0:T(8,128)(2,1)} %collective-permute-done.9.refs_0_, bf16[128,6144]{1,0:T(8,128)(2,1)} %copy-done.7), custom_call_target="tpu_custom_call" | custom-call | bytes 1024 | tf_op jit(solution)/shard_map/mass/pallas_call | solution.py:140
  86.2 1.6 %collective-permute-start.11 = (f32[112,256]{1,0:T(8,128)}, f32[112,256]{1,0:T(8,128)S(1)}, u32[]{:S(2)}, u32[]{:S(2)}) collective-permute-start(f32[112,256]{1,0:T(8,128)} %get-tuple-element.68), channel_id=1, source_target_pairs={{0,1},{1,2},{2,3},{3,0},{4,5},{5,6},{6,7},{7,4},{8,9},{9,10},{10,1... | collective-permute-start | bytes 344072 | tf_op jit(solution)/shard_map/ppermute | solution.py:460
  87.8 2.6 %collective-permute-start.12 = (f32[112,256]{1,0:T(8,128)}, f32[112,256]{1,0:T(8,128)S(1)}, u32[]{:S(2)}, u32[]{:S(2)}) collective-permute-start(f32[112,256]{1,0:T(8,128)} %get-tuple-element.69), channel_id=1, source_target_pairs={{0,2},{1,3},{2,0},{3,1},{4,6},{5,7},{6,4},{7,5},{8,10},{9,11},{10,... | collective-permute-start | bytes 344072 | tf_op jit(solution)/shard_map/ppermute | solution.py:460
  90.5 1.3 collective-permute-start.13
  92.6 13.6 %first_pass.3 = (f32[5120,1024]{1,0:T(8,128)}, f32[80,1024]{1,0:T(8,128)}, f32[8,128]{1,0:T(8,128)}) custom-call(s32[10]{0:T(128)} %pad_add_fusion.pos_ref, bf16[5120,128]{1,0:T(8,128)(2,1)} %bitcast.38, bf16[1024,128]{1,0:T(8,128)(2,1)} %copy-done.4, f32[80,64]{1,0:T(8,128)} %slice.43.w_ref), custom_call_target="tpu_custom_call" | custom-call | bytes 1024 | tf_op jit(solution)/shard_map/first_pass/pallas_call | solution.py:273
  106.9 19.0 %second_pass.1 = (f32[7168,128]{1,0:T(8,128)}, f32[112,64]{1,0:T(8,128)}, f32[128,512]{1,0:T(8,128)}, f32[128,512]{1,0:T(8,128)}) custom-call(f32[112,1]{1,0:T(8,128)} %copy.23.rw_ref, f32[112,64]{1,0:T(8,128)} %copy-done.8, bf16[1024,128]{1,0:T(8,128)(2,1)} %copy-done.4, bf16[7168,128]{1,0:T(8,128)(2,1)} %bitcast.37, ...), custom_call_target="tpu_custom_call" | custom-call | bytes 1024 | tf_op jit(solution)/shard_map/second_pass/pallas_call | solution.py:421
  125.9 1.7 %collective-permute-done.14 = f32[128,512]{1,0:T(8,128)S(1)} collective-permute-done((f32[128,512]{1,0:T(8,128)}, f32[128,512]{1,0:T(8,128)S(1)}, u32[]{:S(2)}, u32[]{:S(2)}) %collective-permute-start.14) | collective-permute-done | bytes 262176 | tf_op jit(solution)/shard_map/ppermute | solution.py:455
  128.7 9.3 %collective-permute-start.15 = (f32[128,128]{1,0:T(8,128)S(1)}, f32[128,128]{1,0:T(8,128)S(1)}, u32[]{:S(2)}, u32[]{:S(2)}) collective-permute-start(f32[128,128]{1,0:T(8,128)S(1)} %get-tuple-element.81), channel_id=1, source_target_pairs={{0,8},{4,12},{8,0},{12,4},{16,24},{20,28},{24,16},{28,20},{1,9},{5... | collective-permute-start | bytes 196616 | tf_op jit(solution)/shard_map/ppermute | solution.py:455
  138.1 1.4 collective-permute-start.17
  140.4 3.2 %collective-permute-done.16 = f32[128,128]{1,0:T(8,128)S(1)} collective-permute-done((f32[128,128]{1,0:T(8,128)S(1)}, f32[128,128]{1,0:T(8,128)S(1)}, u32[]{:S(2)}, u32[]{:S(2)}) %collective-permute-start.16) | collective-permute-done | bytes 65568 | tf_op jit(solution)/shard_map/ppermute | solution.py:455
  143.9 3.7 %collective-permute-start.20 = (f32[32,128]{1,0:T(8,128)S(1)}, f32[32,128]{1,0:T(8,128)S(1)}, u32[]{:S(2)}, u32[]{:S(2)}) collective-permute-start(f32[32,128]{1,0:T(8,128)S(1)} %get-tuple-element.85), channel_id=1, source_target_pairs={{0,3},{1,0},{2,1},{3,2},{4,7},{5,4},{6,5},{7,6},{8,11},{9,8},{10,9... | collective-permute-start | bytes 49160 | tf_op jit(solution)/shard_map/ppermute | solution.py:460
  (93 shorter events, 20.9 us)
Async XLA Ops:
  7.2 41.3 %reduce-scatter.3.cloned.1.call-start = ((), (), s32[]{:S(2)}) async-start(), calls=%async_computation.2 | async-start | bytes 573440 | tf_op jit(solution)/shard_map/reduce_scatter | solution.py:527
  7.2 13.4 %collective-permute-start = (bf16[128,6144]{1,0:T(8,128)(2,1)}, bf16[128,6144]{1,0:T(8,128)(2,1)}, u32[]{:S(2)}, u32[]{:S(2)}) collective-permute-start(bf16[128,6144]{1,0:T(8,128)(2,1)} %refs_0_.1), channel_id=1, source_target_pairs={{0,4},{4,0},{8,12},{12,8},{16,20},{20,16},{24,28},{28,24},{1,5},{5... | collective-permute-start | bytes 4718600 | tf_op jit(solution)/shard_map/ppermute | solution.py:455
  7.7 38.0 %collective-permute-start.4 = (bf16[128,6144]{1,0:T(8,128)(2,1)}, bf16[128,6144]{1,0:T(8,128)(2,1)S(1)}, u32[]{:S(2)}, u32[]{:S(2)}) collective-permute-start(bf16[128,6144]{1,0:T(8,128)(2,1)} %refs_0_.1), channel_id=1, source_target_pairs={{0,8},{4,12},{8,0},{12,4},{16,24},{20,28},{24,16},{28,20},{1,9},{5... | collective-permute-start | bytes 4718600 | tf_op jit(solution)/shard_map/ppermute | solution.py:455
  10.3 37.5 %collective-permute-start.5 = (bf16[128,6144]{1,0:T(8,128)(2,1)}, bf16[128,6144]{1,0:T(8,128)(2,1)}, u32[]{:S(2)}, u32[]{:S(2)}) collective-permute-start(bf16[128,6144]{1,0:T(8,128)(2,1)} %refs_0_.1), channel_id=1, source_target_pairs={{0,16},{4,20},{8,24},{12,28},{16,0},{20,4},{24,8},{28,12},{1,17},{... | collective-permute-start | bytes 4718600 | tf_op jit(solution)/shard_map/ppermute | solution.py:455
  27.5 78.7 %reduce-scatter.5.cloned.1.call-start = ((), (), s32[]{:S(2)}) async-start(), calls=%async_computation.3 | async-start | bytes 1146880 | tf_op jit(solution)/shard_map/reduce_scatter | solution.py:547
  27.5 20.3 %collective-permute-start.1 = (bf16[128,128]{1,0:T(8,128)(2,1)S(1)}, bf16[128,128]{1,0:T(8,128)(2,1)}, u32[]{:S(2)}, u32[]{:S(2)}) collective-permute-start(bf16[128,128]{1,0:T(8,128)(2,1)S(1)} %copy-done.9), channel_id=1, source_target_pairs={{0,8},{4,12},{8,0},{12,4},{16,24},{20,28},{24,16},{28,20},{1,9},{5... | collective-permute-start | bytes 98312 | tf_op jit(solution)/shard_map/ppermute | solution.py:455
  28.1 20.4 %collective-permute-start.2 = (bf16[128,128]{1,0:T(8,128)(2,1)S(1)}, bf16[128,128]{1,0:T(8,128)(2,1)}, u32[]{:S(2)}, u32[]{:S(2)}) collective-permute-start(bf16[128,128]{1,0:T(8,128)(2,1)S(1)} %copy-done.9), channel_id=1, source_target_pairs={{0,16},{4,20},{8,24},{12,28},{16,0},{20,4},{24,8},{28,12},{1,17},{... | collective-permute-start | bytes 98312 | tf_op jit(solution)/shard_map/ppermute | solution.py:455
  28.2 20.3 %collective-permute-start.3 = (bf16[128,128]{1,0:T(8,128)(2,1)S(1)}, bf16[128,128]{1,0:T(8,128)(2,1)S(1)}, u32[]{:S(2)}, u32[]{:S(2)}) collective-permute-start(bf16[128,128]{1,0:T(8,128)(2,1)S(1)} %copy-done.9), channel_id=1, source_target_pairs={{0,24},{4,28},{8,16},{12,20},{16,8},{20,12},{24,0},{28,4},{1,25},{... | collective-permute-start | bytes 98312 | tf_op jit(solution)/shard_map/ppermute | solution.py:455
  48.5 6.3 %collective-permute-start.7 = (bf16[128,6144]{1,0:T(8,128)(2,1)S(1)}, bf16[128,6144]{1,0:T(8,128)(2,1)S(1)}, u32[]{:S(2)}, u32[]{:S(2)}) collective-permute-start(bf16[128,6144]{1,0:T(8,128)(2,1)S(1)} %collective-permute-done.4.refs_0_), channel_id=1, source_target_pairs={{0,4},{4,0},{8,12},{12,8},{16,20},{20,16},{24,28},{28,24},{1,5},{5... | collective-permute-start | bytes 4718600 | tf_op jit(solution)/shard_map/ppermute | solution.py:455
  48.6 6.3 %collective-permute-start.8 = (bf16[128,6144]{1,0:T(8,128)(2,1)}, bf16[128,6144]{1,0:T(8,128)(2,1)S(1)}, u32[]{:S(2)}, u32[]{:S(2)}) collective-permute-start(bf16[128,6144]{1,0:T(8,128)(2,1)} %collective-permute-done.5.refs_2_), channel_id=1, source_target_pairs={{0,4},{4,0},{8,12},{12,8},{16,20},{20,16},{24,28},{28,24},{1,5},{5... | collective-permute-start | bytes 4718600 | tf_op jit(solution)/shard_map/ppermute | solution.py:455
  50.7 23.7 %collective-permute-start.9 = (bf16[128,6144]{1,0:T(8,128)(2,1)S(1)}, bf16[128,6144]{1,0:T(8,128)(2,1)}, u32[]{:S(2)}, u32[]{:S(2)}) collective-permute-start(bf16[128,6144]{1,0:T(8,128)(2,1)S(1)} %broadcast_select_fusion), channel_id=1, source_target_pairs={{0,8},{4,20},{8,0},{12,28},{16,24},{20,4},{24,16},{28,12},{1,9},{5... | collective-permute-start | bytes 4718600 | tf_op jit(solution)/shard_map/ppermute | solution.py:539
  53.3 13.5 %collective-permute-start.6 = (bf16[4,128,128]{2,1,0:T(8,128)(2,1)}, bf16[4,128,128]{2,1,0:T(8,128)(2,1)S(1)}, u32[]{:S(2)}, u32[]{:S(2)}) collective-permute-start(bf16[4,128,128]{2,1,0:T(8,128)(2,1)} %pad_maximum_fusion), channel_id=1, source_target_pairs={{0,4},{4,0},{8,12},{12,8},{16,20},{20,16},{24,28},{28,24},{1,5},{5... | collective-permute-start | bytes 393224 | tf_op jit(solution)/shard_map/ppermute | solution.py:455
  74.4 3.9 %collective-permute-start.10 = (bf16[128,6144]{1,0:T(8,128)(2,1)}, bf16[128,6144]{1,0:T(8,128)(2,1)S(1)}, u32[]{:S(2)}, u32[]{:S(2)}) collective-permute-start(bf16[128,6144]{1,0:T(8,128)(2,1)} %collective-permute-done.9.refs_0_), channel_id=1, source_target_pairs={{0,4},{4,0},{8,12},{12,8},{16,20},{20,16},{24,28},{28,24},{1,5},{5... | collective-permute-start | bytes 4718600 | tf_op jit(solution)/shard_map/ppermute | solution.py:455
  86.2 19.9 %collective-permute-start.11 = (f32[112,256]{1,0:T(8,128)}, f32[112,256]{1,0:T(8,128)S(1)}, u32[]{:S(2)}, u32[]{:S(2)}) collective-permute-start(f32[112,256]{1,0:T(8,128)} %get-tuple-element.68), channel_id=1, source_target_pairs={{0,1},{1,2},{2,3},{3,0},{4,5},{5,6},{6,7},{7,4},{8,9},{9,10},{10,1... | collective-permute-start | bytes 344072 | tf_op jit(solution)/shard_map/ppermute | solution.py:460
  87.8 18.3 %collective-permute-start.12 = (f32[112,256]{1,0:T(8,128)}, f32[112,256]{1,0:T(8,128)S(1)}, u32[]{:S(2)}, u32[]{:S(2)}) collective-permute-start(f32[112,256]{1,0:T(8,128)} %get-tuple-element.69), channel_id=1, source_target_pairs={{0,2},{1,3},{2,0},{3,1},{4,6},{5,7},{6,4},{7,5},{8,10},{9,11},{10,... | collective-permute-start | bytes 344072 | tf_op jit(solution)/shard_map/ppermute | solution.py:460
  90.5 15.7 %collective-permute-start.13 = (f32[112,256]{1,0:T(8,128)}, f32[112,256]{1,0:T(8,128)S(1)}, u32[]{:S(2)}, u32[]{:S(2)}) collective-permute-start(f32[112,256]{1,0:T(8,128)} %get-tuple-element.70), channel_id=1, source_target_pairs={{0,3},{1,0},{2,1},{3,2},{4,7},{5,4},{6,5},{7,6},{8,11},{9,8},{10,9... | collective-permute-start | bytes 344072 | tf_op jit(solution)/shard_map/ppermute | solution.py:460
  106.9 43.6 %copy-start.1 = (s32[8]{0:T(128)S(1)}, s32[8]{0:T(128)}, u32[]{:S(2)}) copy-start(s32[8]{0:T(128)} %param.17) | copy-start | bytes 100
  125.9 1.8 %collective-permute-start.14 = (f32[128,512]{1,0:T(8,128)}, f32[128,512]{1,0:T(8,128)S(1)}, u32[]{:S(2)}, u32[]{:S(2)}) collective-permute-start(f32[128,512]{1,0:T(8,128)} %get-tuple-element.74), channel_id=1, source_target_pairs={{0,4},{4,0},{8,12},{12,8},{16,20},{20,16},{24,28},{28,24},{1,5},{5... | collective-permute-start | bytes 786440 | tf_op jit(solution)/shard_map/ppermute | solution.py:455
  128.7 11.7 %collective-permute-start.15 = (f32[128,128]{1,0:T(8,128)S(1)}, f32[128,128]{1,0:T(8,128)S(1)}, u32[]{:S(2)}, u32[]{:S(2)}) collective-permute-start(f32[128,128]{1,0:T(8,128)S(1)} %get-tuple-element.81), channel_id=1, source_target_pairs={{0,8},{4,12},{8,0},{12,4},{16,24},{20,28},{24,16},{28,20},{1,9},{5... | collective-permute-start | bytes 196616 | tf_op jit(solution)/shard_map/ppermute | solution.py:455
  138.0 5.6 %collective-permute-start.16 = (f32[128,128]{1,0:T(8,128)S(1)}, f32[128,128]{1,0:T(8,128)S(1)}, u32[]{:S(2)}, u32[]{:S(2)}) collective-permute-start(f32[128,128]{1,0:T(8,128)S(1)} %get-tuple-element.83), channel_id=1, source_target_pairs={{0,16},{4,20},{8,24},{12,28},{16,0},{20,4},{24,8},{28,12},{1,17},{... | collective-permute-start | bytes 196616 | tf_op jit(solution)/shard_map/ppermute | solution.py:455
  138.1 5.5 %collective-permute-start.17 = (f32[128,128]{1,0:T(8,128)S(1)}, f32[128,128]{1,0:T(8,128)S(1)}, u32[]{:S(2)}, u32[]{:S(2)}) collective-permute-start(f32[128,128]{1,0:T(8,128)S(1)} %get-tuple-element.82), channel_id=1, source_target_pairs={{0,24},{4,28},{8,16},{12,20},{16,8},{20,12},{24,0},{28,4},{1,25},{... | collective-permute-start | bytes 196616 | tf_op jit(solution)/shard_map/ppermute | solution.py:455
  143.7 5.6 %collective-permute-start.18 = (f32[32,128]{1,0:T(8,128)S(1)}, f32[32,128]{1,0:T(8,128)S(1)}, u32[]{:S(2)}, u32[]{:S(2)}) collective-permute-start(f32[32,128]{1,0:T(8,128)S(1)} %get-tuple-element.84), channel_id=1, source_target_pairs={{0,1},{1,2},{2,3},{3,0},{4,5},{5,6},{6,7},{7,4},{8,9},{9,10},{10,1... | collective-permute-start | bytes 49160 | tf_op jit(solution)/shard_map/ppermute | solution.py:460
  143.8 5.5 %collective-permute-start.19 = (f32[32,128]{1,0:T(8,128)S(1)}, f32[32,128]{1,0:T(8,128)S(1)}, u32[]{:S(2)}, u32[]{:S(2)}) collective-permute-start(f32[32,128]{1,0:T(8,128)S(1)} %get-tuple-element.86), channel_id=1, source_target_pairs={{0,2},{1,3},{2,0},{3,1},{4,6},{5,7},{6,4},{7,5},{8,10},{9,11},{10,... | collective-permute-start | bytes 49160 | tf_op jit(solution)/shard_map/ppermute | solution.py:460
  143.9 6.0 %collective-permute-start.20 = (f32[32,128]{1,0:T(8,128)S(1)}, f32[32,128]{1,0:T(8,128)S(1)}, u32[]{:S(2)}, u32[]{:S(2)}) collective-permute-start(f32[32,128]{1,0:T(8,128)S(1)} %get-tuple-element.85), channel_id=1, source_target_pairs={{0,3},{1,0},{2,1},{3,2},{4,7},{5,4},{6,5},{7,6},{8,11},{9,8},{10,9... | collective-permute-start | bytes 49160 | tf_op jit(solution)/shard_map/ppermute | solution.py:460
  (17 other events, 116.8 us)
Sparse Core Ops, SparseCore 0:
  27.6 20.4 reduce-scatter.2
  66.9 26.3 reduce-scatter.4
